TPU v7x, 32 devices: a whole 2x2x4 slice. The times are simulated.
32 devices in a mesh: clip: 4 (over y, x), chan: 8 (over z, core).
Axes of the slice: x: 2, y: 2, z: 4, core: 2. Of those that a mesh axis runs over, the one named last changes fastest.
Arguments:
- features: bfloat16 [128, 196, 1024], P(('clip', 'chan')), may hold values from -6 to 6
- cotangent: bfloat16 [128, 196, 1024], P(('clip', 'chan')), may hold values from -6 to 6
- frame_counts: int32 [4], replicated, may hold values from 8 to 32, as said below
- weight_first: float32 [3, 1024, 256], P(None, 'chan'), may hold values from -0.109375 to 0.109375
- weight_middle: float32 [9, 256, 256], P(None, 'chan'), may hold values from -0.125 to 0.125
- weight_last: float32 [256, 1024], P('chan'), may hold values from -0.375 to 0.375
- weight_embed: float32 [1024, 3, 512], P('chan'), may hold values from -0.1875 to 0.1875
- weight_back: float32 [512, 1024], P('chan'), may hold values from -0.25 to 0.25
- norm_params: float32 [5120], replicated, may hold values from 0.5 to 1.5
- moment_first: float32 [3, 1024, 256], P(None, 'chan'), may hold values from -0.0008544922 to 0.0008544922
- moment_middle: float32 [9, 256, 256], P(None, 'chan'), may hold values from -0.0008544922 to 0.0008544922
- moment_last: float32 [256, 1024], P('chan'), may hold values from -0.0008544922 to 0.0008544922
- moment_embed: float32 [1024, 3, 512], P('chan'), may hold values from -0.0008544922 to 0.0008544922
- moment_back: float32 [512, 1024], P('chan'), may hold values from -0.0008544922 to 0.0008544922
- moment_norm: float32 [5120], replicated, may hold values from -0.0024414062 to 0.0024414062
- second_first: float32 [3, 1024, 256], P(None, 'chan'), may hold values from 2.6733165e-09 to 1.0693266e-08
- second_middle: float32 [9, 256, 256], P(None, 'chan'), may hold values from 2.6733165e-09 to 1.0693266e-08
- second_last: float32 [256, 1024], P('chan'), may hold values from 2.6733165e-09 to 1.0693266e-08
- second_embed: float32 [1024, 3, 512], P('chan'), may hold values from 2.6733165e-09 to 1.0693266e-08
- second_back: float32 [512, 1024], P('chan'), may hold values from 2.6733165e-09 to 1.0693266e-08
- second_norm: float32 [5120], replicated, may hold values from 1.33665825e-08 to 5.346633e-08
Outputs:
- mixed: bfloat16 [128, 196, 1024], P(('clip', 'chan'))
- features_gradient: bfloat16 [128, 196, 1024], P(('clip', 'chan'))
- first_gradient: float32 [3, 1024, 256], replicated
- middle_gradient: float32 [9, 256, 256], replicated
- last_gradient: float32 [256, 1024], replicated
- embed_gradient: float32 [1024, 3, 512], replicated
- back_gradient: float32 [512, 1024], replicated
- norm_gradient: float32 [5120], replicated
- moment_first_new: float32 [3, 1024, 256], P(None, 'chan')
- moment_middle_new: float32 [9, 256, 256], P(None, 'chan')
- moment_last_new: float32 [256, 1024], P('chan')
- moment_embed_new: float32 [1024, 3, 512], P('chan')
- moment_back_new: float32 [512, 1024], P('chan')
- moment_norm_new: float32 [5120], replicated
- second_first_new: float32 [3, 1024, 256], P(None, 'chan')
- second_middle_new: float32 [9, 256, 256], P(None, 'chan')
- second_last_new: float32 [256, 1024], P('chan')
- second_embed_new: float32 [1024, 3, 512], P('chan')
- second_back_new: float32 [512, 1024], P('chan')
- second_norm_new: float32 [5120], replicated
- weight_first_new: float32 [3, 1024, 256], P(None, 'chan')
- weight_middle_new: float32 [9, 256, 256], P(None, 'chan')
- weight_last_new: float32 [256, 1024], P('chan')
- weight_embed_new: float32 [1024, 3, 512], P('chan')
- weight_back_new: float32 [512, 1024], P('chan')
- norm_params_new: float32 [5120], replicated
- gradient_norm: float32 [], replicated
Inputs may be any that keep to these rules, and one draw needn't show every extreme that they name: `frame_counts`: each clip has 8, 16 or 32 valid frames, and some clip has 32.
All inputs are finite; a program needn't handle non-finite values.
Results may differ from a plain program's by a relative error of at most 0.035.
Values may be sent and summed in bfloat16 or wider, within the bound.
No kernel may reach another device: no remote copies, remote signals or barrier semaphores. Data moves between devices by JAX's collectives and lax.ppermute only.
A program may use at most 256 MiB of HBM per device.

v0:
```python
import functools
import math

import jax
import jax.numpy as jnp
import numpy as np
from jax import lax
from jax.experimental import pallas as pl
from jax.experimental.layout import Layout, with_layout_constraint
from jax.experimental.pallas import tpu as pltpu
from jax.sharding import PartitionSpec as P

D = 1024
BOT = 256
INNER = 512
HH = 14
WW = 14
STEP = 10
DPC = 8


EPS_NORM = 1e-05
BETA_ONE = 0.9
BETA_TWO = 0.95
ADAM_EPS = 1e-08
WEIGHT_DECAY = 0.01
CLIP_AT = 1.0
GAIN_RATE = 0.5


def flipped(value, axis, mask):
    pairs = [(source, source ^ mask) for source in range(lax.axis_size(axis))]
    return lax.ppermute(value, axis, pairs)


def whole_of(shard):
    return lax.all_gather(shard.astype(jnp.bfloat16), "chan", axis=0, tiled=False)


def tap_of(weights, tap):
    return weights[:, tap].reshape(weights.shape[0] * weights.shape[2], weights.shape[3])


def beside(cells, spots):
    ends = lax.axis_size("chan") - 1
    upward = [(index, index + 1) for index in range(ends)]
    downward = [(index + 1, index) for index in range(ends)]
    return (
        lax.ppermute(cells[-1:], "chan", upward).reshape(spots, cells.shape[-1]),
        lax.ppermute(cells[:1], "chan", downward).reshape(spots, cells.shape[-1]),
    )


def total(value):
    for axis in ("chan", "clip"):
        bits = lax.axis_size(axis).bit_length() - 1
        levels = list(range(bits))
        groups = [levels[:1]] if axis == "chan" else []
        rest = levels[len(groups) :]
        groups += [rest[index : index + 2] for index in range(0, len(rest), 2)]
        for group in groups:
            base = 1 << group[0]
            parts = [flipped(value, axis, base * turn) for turn in range(1, 1 << len(group))]
            value = value + sum(parts[1:], parts[0])
    return value


def level_groups(axis):
    bits = lax.axis_size(axis).bit_length() - 1
    levels = list(range(bits))
    groups = [levels[:1]] if axis == "chan" else []
    rest = levels[len(groups) :]
    return groups + [rest[index : index + 2] for index in range(0, len(rest), 2)]


def level_steps():
    order = [("chan", group) for group in level_groups("chan")]
    order = order[:1] + [("clip", group) for group in level_groups("clip")] + order[1:]
    steps = []
    for axis, group in order:
        base, count = 1 << group[0], 1 << len(group)
        steps.append((axis, base, count, (lax.axis_index(axis) >> group[0]) & (count - 1)))
    return steps


def half_kernel(mine, arrived, out_ref):
    out_ref[...] = (mine[...].astype(F32) + arrived[...].astype(F32)).astype(LOW)


def core_step(mine, others):
    arrived = flipped(others, "chan", 1)
    return call(half_kernel, [(mine.shape, LOW)], (mine, arrived), scalars=0)[0]


def deal(place, halves, mine, others, sems):
    copies = [
        pltpu.make_async_copy(halves.at[place[0]], mine, sems.at[0]),
        pltpu.make_async_copy(halves.at[1 - place[0]], others, sems.at[1]),
    ]
    for copy in copies:
        copy.start()
    for copy in copies:
        copy.wait()


def put_rows(halves, at, values):
    size = halves.shape[1]
    cut = max(0, min(values.shape[0], size - at))
    if cut:
        halves[0, pl.ds(at, cut), :] = values[:cut]
    if cut < values.shape[0]:
        halves[1, pl.ds(at + cut - size, values.shape[0] - cut), :] = values[cut:]


def scatter_sum(value, steps):
    for axis, base, count, place in steps:
        size = value.shape[0] // count
        mine = lax.dynamic_slice_in_dim(value, place * size, size).astype(F32)
        arrived = [
            flipped(
                lax.dynamic_slice_in_dim(value, (place ^ turn) * size, size), axis, base * turn
            )
            for turn in range(1, count)
        ]
        for item in arrived:
            mine = mine + item.astype(F32)
        value = mine.astype(LOW)
    return value


def laid_out(rows, frames):
    grid = rows.reshape(frames, -1, rows.shape[1])
    return with_layout_constraint(grid, Layout(major_to_minor=(1, 0, 2)))


def tied(*values):
    return lax.optimization_barrier(values)


def gather_sum(value, steps):
    for axis, base, count, place in reversed(steps):
        size = value.shape[0]
        parts = [value] + [flipped(value, axis, base * turn) for turn in range(1, count)]
        whole = jnp.zeros((count,) + value.shape, LOW)
        for turn, part in enumerate(parts):
            whole = lax.dynamic_update_index_in_dim(whole, part, place ^ turn, 0)
        value = whole.reshape((count * size,) + value.shape[1:])
    return value


NEG = -1e30
MIB = 1 << 20
NN = (((1,), (0,)), ((), ()))
NT = (((1,), (1,)), ((), ()))
TN = (((0,), (0,)), ((), ()))
F32 = jnp.float32
LOW = jnp.bfloat16


def dot(left, right, dims=NN):
    return lax.dot_general(left, right, dims, preferred_element_type=F32)


def sig(values):
    return 0.5 * jnp.tanh(0.5 * values) + 0.5


def slope(values):
    gate = sig(values)
    return gate * (1.0 + values * (1.0 - gate))


def moments(sums, inverse):
    mean = sums[0:1] * inverse
    return mean, lax.rsqrt(sums[1:2] * inverse - mean * mean + EPS_NORM)


def column_sums(values):
    return jnp.sum(values, axis=0, keepdims=True)


def call(kernel, outs, args, scalars=1, scratch=(), vmem=16, far=(), far_out=(), micros=2):
    spaces = []
    for index in range(len(args)):
        if index < scalars:
            spaces.append(pl.BlockSpec(memory_space=pltpu.SMEM))
        elif index in far:
            spaces.append(pl.BlockSpec(memory_space=pltpu.HBM))
        else:
            spaces.append(pl.BlockSpec(memory_space=pltpu.VMEM))
    shapes = tuple(jax.ShapeDtypeStruct(shape, dtype) for shape, dtype in outs)
    out_specs = tuple(
        pl.BlockSpec(memory_space=pltpu.HBM if index in far_out else pltpu.VMEM)
        for index in range(len(outs))
    )
    return pl.pallas_call(
        kernel,
        out_shape=shapes,
        in_specs=spaces,
        out_specs=out_specs,
        scratch_shapes=list(scratch),
        compiler_params=pltpu.CompilerParams(vmem_limit_bytes=vmem * MIB),
        cost_estimate=pl.CostEstimate(
            flops=int(micros * 1e9), bytes_accessed=0, transcendentals=0
        ),
    )(*args)


def first_kernel(flags, cells, before, after, weights, pre_ref, sums_ref, early, late):
    rows = cells.shape[0]
    spots = before.shape[0]
    valid = flags[0]
    late[pl.ds(0, rows), :] = dot(cells[...], tap_of(weights, 2)) * valid
    late[pl.ds(rows, spots), :] = dot(after[...], tap_of(weights, 2)) * flags[2]
    early[pl.ds(0, spots), :] = dot(before[...], tap_of(weights, 0)) * flags[1]
    early[pl.ds(spots, rows), :] = dot(cells[...], tap_of(weights, 0)) * valid
    pre = (
        dot(cells[...], tap_of(weights, 1)) * valid
        + early[pl.ds(0, rows), :]
        + late[pl.ds(spots, rows), :]
    )
    pre_ref[...] = pre
    sums_ref[0:1, :] = column_sums(pre) * valid
    sums_ref[1:2, :] = column_sums(pre * pre) * valid


def first_conv(flags, cells, before, after, weights):
    rows, width = cells.shape
    narrow = weights.shape[3]
    spots = before.shape[0]
    return call(
        first_kernel,
        [((rows, narrow), F32), ((2, narrow), F32)],
        (flags, cells, before, after, weights),
        scratch=[pltpu.VMEM((rows + spots, narrow), F32)] * 2,
    )


def spread(values, edges, buffer, columns, rows):
    narrow = values.shape[1]
    margin = 16
    buffer[0, pl.ds(0, margin), :] = jnp.zeros((margin, narrow), F32)
    buffer[0, pl.ds(margin + rows, margin), :] = jnp.zeros((margin, narrow), F32)
    buffer[1, pl.ds(0, margin), :] = jnp.zeros((margin, narrow), F32)
    buffer[1, pl.ds(margin + rows, margin), :] = jnp.zeros((margin, narrow), F32)
    buffer[0, pl.ds(margin, rows), :] = values
    for across in range(3):
        moved = buffer[0, pl.ds(margin + across - 1, rows), :]
        if across == 0:
            moved = moved * edges[:, 0:1]
        if across == 2:
            moved = moved * edges[:, 1:2]
        buffer[1, pl.ds(margin, rows), :] = moved
        for down in range(3):
            part = buffer[1, pl.ds(margin + WW * (down - 1), rows), :]
            if down == 0:
                part = part * edges[:, 2:3]
            if down == 2:
                part = part * edges[:, 3:4]
            at = (3 * down + across) * narrow
            columns[:, at : at + narrow] = part.astype(LOW)


def spread_scratch(rows, narrow):
    return [pltpu.VMEM((2, rows + 32, narrow), F32), pltpu.VMEM((rows, 9 * narrow), LOW)]


def act_of(flags, pre, sums, scale_shift):
    mean, scale = moments(sums, flags[3])
    normal = (pre - mean) * scale
    return normal, normal * scale_shift[0:1] + scale_shift[1:2], scale


def middle_kernel(flags, pre, sums, gains, weights, edges, out_ref, sums_ref, buffer, columns):
    rows, narrow = pre.shape
    valid = flags[0]
    _, act, _ = act_of(flags, pre[...], sums[...], gains[...])
    spread(act * sig(act) * valid, edges[...], buffer, columns, rows)
    out = None
    for tap in range(9):
        part = dot(columns[:, tap * narrow : (tap + 1) * narrow], tap_of(weights, tap))
        out = part if out is None else out + part
    out_ref[...] = out
    sums_ref[0:1, :] = column_sums(out) * valid
    sums_ref[1:2, :] = column_sums(out * out) * valid


def middle_conv(flags, pre, sums, gains, weights, edges):
    rows, narrow = pre.shape
    return call(
        middle_kernel,
        [((rows, narrow), F32), ((2, narrow), F32)],
        (flags, pre, sums, gains, weights, edges),
        scratch=spread_scratch(rows, narrow),
    )


def last_kernel(flags, pre, sums, gains, weights, act_ref, sums_ref):
    valid = flags[0]
    _, act, _ = act_of(flags, pre[...], sums[...], gains[...])
    act_ref[...] = (act * sig(act) * valid).astype(LOW)
    for at in range(0, weights.shape[1], 256):
        out = dot(act_ref[...], weights[:, at : at + 256])
        sums_ref[0:1, at : at + 256] = column_sums(out) * valid
        sums_ref[1:2, at : at + 256] = column_sums(out * out) * valid


def last_conv(flags, pre, sums, gains, weights):
    rows, narrow = pre.shape
    width = weights.shape[1]
    return call(
        last_kernel,
        [((rows, narrow), LOW), ((2, width), F32)],
        (flags, pre, sums, gains, weights),
    )


def residual_tile(flags, act, cells, weights, sums, gains, at):
    mean, scale = moments(sums[:, at : at + 256], flags[3])
    normal = (dot(act[...], weights[:, at : at + 256]) - mean) * scale
    pre = cells[:, at : at + 256].astype(F32) + (
        normal * gains[0:1, at : at + 256] + gains[1:2, at : at + 256]
    )
    return normal, pre, scale


def embed_kernel(flags, act, cells, weights, sums, gains, embed, res_ref, query_ref, pair_ref):
    width = weights.shape[1]
    inner = query_ref.shape[1]
    for at in range(0, width, 256):
        _, pre, _ = residual_tile(flags, act, cells, weights, sums, gains, at)
        res_ref[:, at : at + 256] = (pre * sig(pre) * flags[0]).astype(LOW)
    for at in range(0, inner, 256):
        query_ref[:, at : at + 256] = dot(res_ref[...], embed[:, at : at + 256]).astype(LOW)
    for at in range(0, 2 * inner, 256):
        pair_ref[:, at : at + 256] = dot(
            res_ref[...], embed[:, inner + at : inner + at + 256]
        ).astype(LOW)


def embed_rows(flags, act, cells, weights, sums, gains, embed):
    rows, width = cells.shape
    inner = embed.shape[1] // 3
    return call(
        embed_kernel,
        [((rows, width), LOW), ((rows, inner), LOW), ((rows, 2 * inner), LOW)],
        (flags, act, cells, weights, sums, gains, embed),
        micros=7,
    )


def copies_of(refs, slots, sems):
    return [
        pltpu.make_async_copy(ref, slots.at[index], sems.at[index])
        for index, ref in enumerate(refs)
    ]


def attend_kernel(
    away, count, query, one, two, three, four, out_ref, log_ref, pairs, tails, scores, total, peak, sums, sems
):
    rows, inner = query.shape
    full = rows // 256 * 256
    rest = rows - full
    wide = 4 * rest
    turn = inner**-0.5 * math.log2(math.e)
    blocks = count[0]
    copies = copies_of((one, two, three, four), pairs, sems)
    for copy in copies:
        copy.start()

    @pl.when(blocks == 0)
    def _():
        out_ref[...] = jnp.zeros_like(out_ref)
        if away:
            log_ref[...] = jnp.zeros_like(log_ref)
            log_ref[0:1, :] = jnp.full((1, log_ref.shape[1]), NEG, F32)
        else:
            log_ref[...] = jnp.full_like(log_ref, NEG)

    peak[...] = jnp.full_like(peak, NEG)
    sums[...] = jnp.zeros_like(sums)

    def score(index, _):
        pltpu.make_async_copy(one, pairs.at[index], sems.at[index]).wait()

        @pl.when(index < blocks)
        def _():
            found = dot(query[...], pairs[index, pl.ds(0, full), :inner], NT)
            scores[index] = found
            top = peak[...]
            for at in range(0, full, 128):
                top = jnp.maximum(top, found[:, at : at + 128])
            peak[...] = top

        return 0

    lax.fori_loop(0, 4, score, 0)

    @pl.when(blocks > 0)
    def _():
        for index in range(4):
            tails[pl.ds(index * rest, rest), :] = pairs[index, pl.ds(full, rest), :]
        lane = lax.broadcasted_iota(jnp.int32, (rows, wide), 1)
        end = jnp.where(lane < blocks * rest, dot(query[...], tails[:, :inner], NT), NEG)
        top = jnp.maximum(
            jnp.max(peak[...], axis=1, keepdims=True), jnp.max(end, axis=1, keepdims=True)
        )
        top = top * turn
        lifted = jnp.exp2(end * turn - top)
        end_sum = jnp.sum(lifted, axis=1, keepdims=True)
        total[...] = dot(lifted.astype(LOW), tails[:, inner:])
        peak[...] = jnp.broadcast_to(top, peak.shape)

        def weigh(index, _):
            base = peak[...]
            running = sums[...]
            parts = []
            for at in range(0, full, 128):
                part = jnp.exp2(scores[index, :, at : at + 128] * turn - base)
                running = running + part
                parts.append(part.astype(LOW))
            sums[...] = running
            total[...] += dot(
                jnp.concatenate(parts, axis=1), pairs[index, pl.ds(0, full), inner:]
            )
            return 0

        lax.fori_loop(0, blocks, weigh, 0)
        found = jnp.sum(sums[...], axis=1, keepdims=True) + end_sum
        logs = jnp.broadcast_to(top + jnp.log2(found), peak.shape)
        if away:
            out = total[...] / found
            mean = column_sums(out) * (1.0 / rows)
            out_ref[...] = (out - mean).astype(out_ref.dtype)
            log_ref[...] = row_of(logs, log_ref.shape[1])
            log_ref[1:2, :inner] = mean
        else:
            out_ref[...] = (total[...] / found).astype(out_ref.dtype)
            log_ref[...] = logs


def attend(count, query, blocks, away):
    rows, inner = query.shape
    span = -(-rows // 128) * 128
    full = rows // 256 * 256
    rest = rows - full
    return call(
        functools.partial(attend_kernel, away),
        [((rows, inner), LOW), ((8, span) if away else (rows, 128), F32)],
        (count, query) + tuple(blocks),
        scratch=[
            pltpu.VMEM((4, rows, 2 * inner), LOW),
            pltpu.VMEM((4 * rest, 2 * inner), LOW),
            pltpu.VMEM((4, rows, full), F32),
            pltpu.VMEM((rows, inner), F32),
            pltpu.VMEM((rows, 128), F32),
            pltpu.VMEM((rows, 128), F32),
            pltpu.SemaphoreType.DMA((4,)),
        ],
        vmem=36,
        far=(2, 3, 4, 5),
        micros=10,
    )


def attend_back_kernel(away, held, split, count, query, grad, *refs):
    size = len(held)
    refs = list(refs)
    if away:
        packed = refs.pop(0)
    else:
        log_ref, term_ref = refs.pop(0), refs.pop(0)
    given_query = refs.pop(0) if away and held[0] == 0 else None
    blocks_in = [refs.pop(0) for _ in held]
    given = [refs.pop(0) for _ in held] if away else ()
    query_ref = refs.pop(0)
    outs = [[refs.pop(0) for _ in range(2 if place in split else 1)] for place in held]
    pairs, tails, stage, stage_tails, total, sems, out_sems = refs[:7]
    if away:
        log_ref, term_ref, in_sems = refs[7:]
    rows, inner = query.shape
    full = rows // 256 * 256
    rest = rows - full
    wide = size * rest
    scaling = inner**-0.5
    turn = scaling * math.log2(math.e)
    blocks = count[0]

    def main_of(ref):
        return ref.at[pl.ds(0, full)]

    def tail_of(ref):
        return ref.at[pl.ds(full, rest)]

    def tail_at(index):
        return pl.ds(index * rest, rest)

    begin = [
        pltpu.make_async_copy(tail_of(ref), tails.at[tail_at(index)], sems.at[1, index])
        for index, ref in enumerate(blocks_in)
    ] + [
        pltpu.make_async_copy(tail_of(ref), stage_tails.at[tail_at(index)], in_sems.at[1, index])
        for index, ref in enumerate(given)
    ]
    for copy in begin:
        copy.start()
    for index in range(size):
        pltpu.make_async_copy(main_of(blocks_in[index]), pairs.at[index], sems.at[0, index]).start()
        if away:
            pltpu.make_async_copy(main_of(given[index]), stage.at[index], in_sems.at[0, index]).start()
    if away:
        log_ref[...] = column_of(packed[0:1, :])[:rows]
        term_ref[...] = column_of(packed[1:2, :])[:rows]
    for copy in begin:
        copy.wait()

    def tile(keys, values, span, mask):
        found = dot(query[...], keys, NT)
        back = dot(grad[...], values, NT)
        logs = log_ref[...]
        terms = term_ref[...]
        kept = []
        slopes = []
        for at in range(0, span, 128):
            end = min(at + 128, span)
            weight = jnp.exp2(found[:, at:end] * turn - logs[:, : end - at])
            if mask is not None:
                weight = jnp.where(mask, weight, 0.0)
            kept.append(weight.astype(LOW))
            slopes.append((weight * (back[:, at:end] - terms[:, : end - at])).astype(LOW))
        kept = kept[0] if len(kept) == 1 else jnp.concatenate(kept, axis=1)
        slopes = slopes[0] if len(slopes) == 1 else jnp.concatenate(slopes, axis=1)
        return slopes, dot(slopes, query[...], TN) * scaling, dot(kept, grad[...], TN)

    active = blocks > held[0]

    @pl.when(jnp.logical_not(active))
    def _():
        if given_query is None:
            query_ref[...] = jnp.zeros_like(query_ref)
        else:
            query_ref[...] = given_query[...].astype(query_ref.dtype)
        if not away:
            stage_tails[...] = jnp.zeros_like(stage_tails)

    @pl.when(active)
    def _():
        keys = tails[:, :inner]
        lane = lax.broadcasted_iota(jnp.int32, (rows, wide), 1)
        ok = lane < (blocks - held[0]) * rest
        slopes, key_part, value_part = tile(keys, tails[:, inner:], wide, ok)
        total[...] = dot(slopes, keys)
        if away:
            key_part = key_part + stage_tails[:, :inner].astype(F32)
            value_part = value_part + stage_tails[:, inner:].astype(F32)
        stage_tails[:, :inner] = key_part.astype(LOW)
        stage_tails[:, inner:] = value_part.astype(LOW)

    def columns(which, part):
        width = 2 * inner // len(outs[which])
        return pl.ds(part * width, width)

    def main_outs(which):
        return [
            pltpu.make_async_copy(
                stage.at[which, :, columns(which, part)], main_of(ref), out_sems.at[0, which, part]
            )
            for part, ref in enumerate(outs[which])
        ]

    def one_block(index, _):
        pltpu.make_async_copy(main_of(blocks_in[0]), pairs.at[index], sems.at[0, index]).wait()
        if away:
            pltpu.make_async_copy(main_of(given[0]), stage.at[index], in_sems.at[0, index]).wait()

        @pl.when(index < blocks - held[0])
        def _():
            block = pairs[index, :, :inner]
            slopes, key_part, value_part = tile(block, pairs[index, :, inner:], full, None)
            total[...] += dot(slopes, block)
            if away:
                key_part = key_part + stage[index, :, :inner].astype(F32)
                value_part = value_part + stage[index, :, inner:].astype(F32)
            stage[index, :, :inner] = key_part.astype(LOW)
            stage[index, :, inner:] = value_part.astype(LOW)

        if not away:

            @pl.when(index >= blocks - held[0])
            def _():
                stage[index] = jnp.zeros(stage.shape[1:], LOW)

        for which in range(size):

            @pl.when(index == which)
            def _():
                for copy in main_outs(which):
                    copy.start()

        return 0

    lax.fori_loop(0, size, one_block, 0)
    ends = [
        pltpu.make_async_copy(
            stage_tails.at[tail_at(index), columns(index, part)],
            tail_of(ref),
            out_sems.at[1, index, part],
        )
        for index in range(size)
        for part, ref in enumerate(outs[index])
    ]
    for copy in ends:
        copy.start()

    @pl.when(active)
    def _():
        found = total[...] * scaling
        if given_query is not None:
            found = found + given_query[...]
        query_ref[...] = found.astype(query_ref.dtype)

    for index in range(size):
        for copy in main_outs(index):
            copy.wait()
    for copy in ends:
        copy.wait()


def attend_back(
    count, query, grad, terms, blocks, held, given, given_query, out_type, split=()
):
    rows, inner = query.shape
    full = rows // 256 * 256
    rest = rows - full
    away = given is not None
    size = len(held)
    more = () if given_query is None else (given_query,)
    near = (count, query, grad) + tuple(terms) + more
    distant = tuple(blocks) + (tuple(given) if away else ())
    scratch = [
        pltpu.VMEM((size, full, 2 * inner), LOW),
        pltpu.VMEM((size * rest, 2 * inner), LOW),
        pltpu.VMEM((size, full, 2 * inner), LOW),
        pltpu.VMEM((size * rest, 2 * inner), LOW),
        pltpu.VMEM((rows, inner), F32),
        pltpu.SemaphoreType.DMA((2, size)),
        pltpu.SemaphoreType.DMA((2, size, 2)),
    ]
    widths = []
    for at in held:
        widths += [inner] * 2 if at in split else [2 * inner]
    if away:
        scratch += [pltpu.VMEM((rows, 128), F32)] * 2 + [pltpu.SemaphoreType.DMA((2, size))]
    found = call(
        functools.partial(attend_back_kernel, away, held, split),
        [((rows, inner), out_type)] + [((rows, width), LOW) for width in widths],
        near + distant,
        scratch=scratch,
        vmem=36,
        far=tuple(range(len(near), len(near) + len(distant))),
        far_out=tuple(range(1, 1 + len(widths))),
        micros=17,
    )
    return found[0], found[1:]


def column_of(row):
    return jnp.transpose(jnp.broadcast_to(row, (128, row.shape[1])))


def row_of(column, span):
    tall = jnp.concatenate([column, jnp.zeros((span - column.shape[0], 128), F32)], axis=0)
    return jnp.transpose(tall)[0:8, :]


def merge_kernel(
    flags, own, own_log, far, far_log, weights, cot, out_ref, log_ref, sums_ref
):
    rows, inner = own.shape
    logs = own_log[...]
    others = column_of(far_log[0:1, :])[:rows]
    top = jnp.maximum(logs, others)
    whole = top + jnp.log2(jnp.exp2(logs - top) + jnp.exp2(others - top))
    log_ref[...] = whole
    share = jnp.exp2(logs - whole)
    other = jnp.exp2(others - whole)
    for at in range(0, inner, 128):
        out_ref[:, at : at + 128] = (
            own[:, at : at + 128].astype(F32) * share + (far[:, at : at + 128].astype(F32) + far_log[1:2, at : at + 128]) * other
        ).astype(LOW)
    valid = flags[0]
    for at in range(0, weights.shape[1], 256):
        out = dot(out_ref[...], weights[:, at : at + 256])
        grad = cot[:, at : at + 256].astype(F32)
        sums_ref[0:1, at : at + 256] = column_sums(out) * valid
        sums_ref[1:2, at : at + 256] = column_sums(out * out) * valid
        sums_ref[2:3, at : at + 256] = column_sums(grad) * valid
        sums_ref[3:4, at : at + 256] = column_sums(grad * out) * valid
    sums_ref[4:5, :] = jnp.zeros((1, weights.shape[1]), F32)
    sums_ref[4:5, :inner] = column_sums(out_ref[...].astype(F32)) * valid


def merge(flags, own, own_log, far, far_log, weights, cot):
    rows, inner = own.shape
    width = weights.shape[1]
    return call(
        merge_kernel,
        [((rows, inner), LOW), ((rows, 128), F32), ((5, width), F32)],
        (flags, own, own_log, far, far_log, weights, cot),
    )


def outer_kernel(
    flags,
    att,
    weights,
    sums,
    gains,
    cot,
    res,
    logs,
    mixed_ref,
    grad_ref,
    back_ref,
    term_ref,
    rows_ref,
    norm_ref,
):
    valid = flags[0]
    inverse = flags[3]
    width = weights.shape[1]
    for at in range(0, width, 256):
        span = slice(at, at + 256)
        mean, scale = moments(sums[0:2, span], inverse)
        normal = (dot(att[...], weights[:, span]) - mean) * scale
        gain = gains[0:1, span]
        mixed_ref[:, span] = (
            (res[:, span].astype(F32) + (normal * gain + gains[1:2, span])) * valid
        ).astype(LOW)
        shift_grad = sums[2:3, span]
        gain_grad = scale * (sums[3:4, span] - mean * shift_grad)
        norm_ref[0:1, span] = gain_grad
        norm_ref[1:2, span] = shift_grad
        removed = (shift_grad + normal * gain_grad) * inverse
        grad = ((gain * scale * valid) * (cot[:, span].astype(F32) - removed)).astype(LOW)
        grad_ref[:, span] = grad
        norm_ref[2:3, span] = column_sums(grad.astype(F32))
    back = dot(grad_ref[...], weights[...], NT).astype(LOW)
    back_ref[...] = back
    term = jnp.sum(back.astype(F32) * att[...].astype(F32), axis=1, keepdims=True)
    term = jnp.broadcast_to(term, term_ref.shape)
    term_ref[...] = term
    rows_ref[...] = row_of(logs[...], rows_ref.shape[1])
    rows_ref[1:2, :] = row_of(term, rows_ref.shape[1])[0:1]


def outer(flags, att, weights, sums, gains, cot, res, logs):
    rows, inner = att.shape
    width = weights.shape[1]
    span = -(-rows // 128) * 128
    return call(
        outer_kernel,
        [
            ((rows, width), LOW),
            ((rows, width), LOW),
            ((rows, inner), LOW),
            ((rows, 128), F32),
            ((8, span), F32),
            ((3, width), F32),
        ],
        (flags, att, weights, sums, gains, cot, res, logs),
        micros=5,
    )


def project_kernel(
    flags,
    query_own,
    query_far,
    keep,
    near_keys,
    near_values,
    far,
    act,
    cells,
    weights,
    sums,
    gains,
    embed_far,
    cot_far,
    proj_ref,
    pre_ref,
    sums_ref,
    embed,
    cot,
    sems,
):
    valid = flags[0]
    inner = query_own.shape[1]
    copies = [
        pltpu.make_async_copy(embed_far, embed, sems.at[0]),
        pltpu.make_async_copy(cot_far, cot, sems.at[1]),
    ]
    for copy in copies:
        copy.start()
    proj_ref[:, :inner] = (query_own[...].astype(F32) + query_far[...].astype(F32)).astype(LOW)
    for at in range(0, 2 * inner, 256):
        span = slice(at, at + 256)
        near = near_keys[:, span] if at < inner else near_values[:, at - inner : at - inner + 256]
        proj_ref[:, inner + at : inner + at + 256] = (
            keep[:, span].astype(F32) + near.astype(F32) + far[:, span].astype(F32)
        ).astype(LOW)
    for copy in copies:
        copy.wait()
    for at in range(0, weights.shape[1], 256):
        span = slice(at, at + 256)
        normal, pre, _ = residual_tile(flags, act, cells, weights, sums, gains, at)
        grad = cot[:, span].astype(F32) + dot(proj_ref[...], embed[span, :], NT)
        out = grad * valid * slope(pre)
        pre_ref[:, span] = out
        sums_ref[0:1, span] = column_sums(out)
        sums_ref[1:2, span] = column_sums(out * normal)


def project_back(flags, query_own, query_far, keep, near_keys, near_values, far, act, cells, weights, sums, gains, embed, cot):
    rows, width = cells.shape
    inner = query_own.shape[1]
    return call(
        project_kernel,
        [((rows, 3 * inner), LOW), ((rows, width), F32), ((2, width), F32)],
        (flags, query_own, query_far, keep, near_keys, near_values, far, act, cells, weights, sums, gains, embed, cot),
        scratch=[
            pltpu.VMEM(embed.shape, LOW),
            pltpu.VMEM(cot.shape, LOW),
            pltpu.SemaphoreType.DMA((2,)),
        ],
        far=(12, 13),
        micros=10,
    )


def last_back_kernel(
    flags, pre_grad, act, weights, sums, gains, back_sums, pre_two, sums_two, gains_two, grad_ref, two_ref, sums_ref
):
    valid = flags[0]
    inverse = flags[3]
    two = None
    for at in range(0, weights.shape[1], 256):
        span = slice(at, at + 256)
        mean, scale = moments(sums[:, span], inverse)
        normal = (dot(act[...], weights[:, span]) - mean) * scale
        removed = (back_sums[0:1, span] + normal * back_sums[1:2, span]) * inverse
        grad = ((gains[0:1, span] * scale * valid) * (pre_grad[:, span] - removed)).astype(LOW)
        grad_ref[:, span] = grad
        part = dot(grad, weights[:, span], NT)
        two = part if two is None else two + part
    normal, active, _ = act_of(flags, pre_two[...], sums_two[...], gains_two[...])
    two = two * valid * slope(active)
    two_ref[...] = two
    sums_ref[0:1, :] = column_sums(two)
    sums_ref[1:2, :] = column_sums(two * normal)


def last_back(flags, pre_grad, act, weights, sums, gains, back_sums, pre_two, sums_two, gains_two):
    rows, width = pre_grad.shape
    narrow = act.shape[1]
    return call(
        last_back_kernel,
        [((rows, width), LOW), ((rows, narrow), F32), ((2, narrow), F32)],
        (flags, pre_grad, act, weights, sums, gains, back_sums, pre_two, sums_two, gains_two),
    )


def middle_back_kernel(
    flags, two, back_sums, pre_two, sums_two, gains_two, pre_one, sums_one, gains_one, weights, edges,
    grad_ref, one_ref, sums_ref, buffer, columns
):
    rows, narrow = two.shape
    valid = flags[0]
    inverse = flags[3]
    normal, _, scale = act_of(flags, pre_two[...], sums_two[...], gains_two[...])
    removed = (back_sums[0:1] + normal * back_sums[1:2]) * inverse
    grad = (gains_two[0:1, :] * scale * valid) * (two[...] - removed)
    grad_ref[...] = grad.astype(LOW)
    spread(grad, edges[...], buffer, columns, rows)
    one = None
    for tap in range(9):
        part = dot(columns[:, tap * narrow : (tap + 1) * narrow], tap_of(weights, 8 - tap), NT)
        one = part if one is None else one + part
    normal, active, _ = act_of(flags, pre_one[...], sums_one[...], gains_one[...])
    one = one * valid * slope(active)
    one_ref[...] = one
    sums_ref[0:1, :] = column_sums(one)
    sums_ref[1:2, :] = column_sums(one * normal)


def middle_back(flags, two, back_sums, pre_two, sums_two, gains_two, pre_one, sums_one, gains_one, weights, edges):
    rows, narrow = two.shape
    return call(
        middle_back_kernel,
        [((rows, narrow), LOW), ((rows, narrow), F32), ((2, narrow), F32)],
        (flags, two, back_sums, pre_two, sums_two, gains_two, pre_one, sums_one, gains_one, weights, edges),
        scratch=spread_scratch(rows, narrow),
    )


def middle_weight_kernel(flags, pre_one, sums_one, gains_one, grad, edges, out_ref, buffer, columns):
    rows, narrow = pre_one.shape
    _, act, _ = act_of(flags, pre_one[...], sums_one[...], gains_one[...])
    spread(act * sig(act) * flags[0], edges[...], buffer, columns, rows)
    for tap in range(9):
        out_ref[pl.ds(tap * narrow, narrow), :] = dot(
            columns[:, tap * narrow : (tap + 1) * narrow], grad[...], TN
        ).astype(LOW)


def middle_weight(flags, pre_one, sums_one, gains_one, grad, edges):
    rows, narrow = pre_one.shape
    return call(
        middle_weight_kernel,
        [((9 * narrow, narrow), LOW)],
        (flags, pre_one, sums_one, gains_one, grad, edges),
        scratch=spread_scratch(rows, narrow),
    )[0]


def first_grad_kernel(flags, one, back_sums, pre_one, sums_one, gains_one, grad_ref):
    normal, _, scale = act_of(flags, pre_one[...], sums_one[...], gains_one[...])
    removed = (back_sums[0:1] + normal * back_sums[1:2]) * flags[3]
    grad_ref[...] = (
        (gains_one[0:1, :] * scale * flags[0]) * (one[...] - removed)
    ).astype(LOW)


def first_grad_of(flags, one, back_sums, pre_one, sums_one, gains_one):
    rows, narrow = one.shape
    return call(
        first_grad_kernel,
        [((rows, narrow), LOW)],
        (flags, one, back_sums, pre_one, sums_one, gains_one),
    )[0]


def first_back_kernel(
    place, flags, grad, before, after, cells, middle, last, mine, others, cols_ref, buffer, halves, sems
):
    rows, narrow = grad.shape
    width = cells.shape[1]
    spots = before.shape[0]
    buffer[pl.ds(0, spots), :] = before[...].astype(F32) * flags[1]
    buffer[pl.ds(spots, rows), :] = grad[...].astype(F32)
    buffer[pl.ds(spots + rows, spots), :] = after[...].astype(F32) * flags[2]
    at = middle.shape[0]
    put_rows(halves, 0, middle[...])
    for tap in range(3):
        part = (buffer[pl.ds(spots * (2 - tap), rows), :] * flags[0]).astype(LOW)
        cols_ref[:, tap * narrow : (tap + 1) * narrow] = part
        put_rows(halves, at, dot(cells[...], part, TN).astype(LOW))
        at += width
    put_rows(halves, at, last[...])
    deal(place, halves, mine, others, sems)


def first_back(place, flags, grad, before, after, cells, middle, last):
    rows, narrow = grad.shape
    spots = before.shape[0]
    width = cells.shape[1]
    mine, others, cols = halves_call(
        first_back_kernel,
        middle.shape[0] + 3 * width + last.shape[0],
        [((rows, 3 * narrow), LOW)],
        (place, flags, grad, before, after, cells, middle, last),
        scratch=[pltpu.VMEM((rows + 2 * spots, narrow), F32)],
    )
    return (mine, others), cols


def early_weight_kernel(
    place, flags, res, proj, att, sums, grad, mine, others, halves, sems
):
    height, inner = res.shape[1], att.shape[1]
    left = (att[...].astype(F32) - sums[...] * flags[3]).astype(LOW)
    at = 0
    for index in range(proj.shape[1] // 256):
        put_rows(
            halves, at, dot(res[...], proj[:, index * 256 : (index + 1) * 256], TN).astype(LOW)
        )
        at += height
    for index in range(grad.shape[1] // 256):
        put_rows(
            halves, at, dot(left, grad[:, index * 256 : (index + 1) * 256], TN).astype(LOW)
        )
        at += inner
    deal(place, halves, mine, others, sems)


def halves_call(kernel, height, outs, args, scratch=()):
    shape = (height // 2, 256)
    return call(
        kernel,
        [(shape, LOW), (shape, LOW)] + outs,
        args,
        scalars=2,
        scratch=list(scratch)
        + [pltpu.VMEM((2,) + shape, LOW), pltpu.SemaphoreType.DMA((2,))],
        far_out=(0, 1),
        micros=8,
    )


def early_weight(place, flags, res, proj, att, sums, grad):
    height = res.shape[1] * proj.shape[1] // 256 + att.shape[1] * grad.shape[1] // 256
    return halves_call(
        early_weight_kernel, height, [], (place, flags, res, proj, att, sums, grad)
    )


def weight_kernel(left, right, out_ref):
    height = left.shape[1]
    for index in range(right.shape[1] // 256):
        out_ref[pl.ds(index * height, height), :] = dot(
            left[...], right[:, index * 256 : (index + 1) * 256], TN
        ).astype(LOW)


def weight_grad(left, right):
    rows, height = left.shape
    width = right.shape[1]
    return call(
        weight_kernel,
        [((height * width // 256, 256), LOW)],
        (left, right),
        scalars=0,
    )[0]


def pieces_of(low_half, high_half, start, stop):
    middle = low_half.shape[0]
    if start < middle:
        yield 0, low_half[pl.ds(start, min(stop, middle) - start), :]
    if stop > middle:
        begin = max(start, middle)
        yield begin - start, high_half[pl.ds(begin - middle, stop - begin), :]


def squares_of(values):
    return jnp.sum((values * values).reshape(-1, 8, values.shape[-1]), axis=0)


def emit(place, half, other, shares, squares):
    def write(low_half, high_half):
        squares[...] = jnp.zeros_like(squares)
        for start, stop, store, extra in shares:
            for offset, rows in pieces_of(low_half, high_half, start, stop):
                values = rows.astype(F32)
                if extra is not None:
                    values = values + extra[offset : offset + values.shape[0]]
                squares[...] += squares_of(values)
                store(offset, values)

    @pl.when(place[0] == 0)
    def _():
        write(half, other)

    @pl.when(place[0] == 1)
    def _():
        write(other, half)


def store_rows(ref, lead, cols):
    def store(offset, values):
        ref[lead + (pl.ds(offset, values.shape[0]), cols)] = values

    return store


def early_shares(embed_ref, back_ref, mean, grad_sum):
    width, inner = embed_ref.shape[1], embed_ref.shape[2]
    shares = []
    at = 0
    for index in range(3 * inner // 256):
        part, col = divmod(index * 256, inner)
        shares.append((at, at + width, store_rows(embed_ref, (part,), slice(col, col + 256)), None))
        at += width
    for index in range(width // 256):
        cols = slice(index * 256, index * 256 + 256)
        extra = mean[:, 0:1] * grad_sum[0:1, cols]
        shares.append((at, at + inner, store_rows(back_ref, (), cols), extra))
        at += inner
    return shares


def early_kernel(place, flags, half, other, sums, grad_sum, embed_ref, back_ref, embed_own, back_own, squares_ref):
    mean = sums[...] * flags[3]
    emit(place, half, other, early_shares(embed_ref, back_ref, column_of(mean), grad_sum), squares_ref)
    span = embed_own.shape[1]
    embed_own[...] = embed_ref[:, pl.ds(pl.multiple_of(place[1] * span, span), span), :]
    span = back_own.shape[0]
    back_own[...] = back_ref[pl.ds(pl.multiple_of(place[1] * span, span), span), :]


def early_grads(place, flags, half, other, sums, grad_sum, width, inner, shards):
    return call(
        early_kernel,
        [
            ((3, width, inner), F32),
            ((inner, width), F32),
            ((3, width // shards, inner), F32),
            ((inner // shards, width), F32),
            ((8, 256), F32),
        ],
        (place, flags, half, other, sums, grad_sum),
        scalars=2,
        micros=6,
    )


def late_shares(first_ref, middle_ref, last_ref):
    shares = []
    at = 0
    for ref in (middle_ref, first_ref):
        for index in range(ref.shape[0]):
            shares.append((at, at + ref.shape[1], store_rows(ref, (index,), slice(None)), None))
            at += ref.shape[1]
    for index in range(last_ref.shape[1] // 256):
        cols = slice(index * 256, index * 256 + 256)
        shares.append((at, at + last_ref.shape[0], store_rows(last_ref, (), cols), None))
        at += last_ref.shape[0]
    return shares


def late_kernel(rates, place, half, other, squares, extra, embed_own, back_own, *refs):
    given = [refs[3 * index : 3 * index + 3] for index in range(5)]
    first_ref, middle_ref, last_ref, norm_ref = refs[15:19]
    made = [refs[19 + 3 * index : 22 + 3 * index] for index in range(5)]
    tally = refs[34]
    emit(place, half, other, late_shares(first_ref, middle_ref, last_ref), tally)
    found = jnp.sum(tally[...] + squares[...], axis=0, keepdims=True)
    norm = jnp.sqrt(jnp.sum(found, axis=1, keepdims=True) + extra[0:1, 0:1])
    factor = jnp.minimum(1.0, CLIP_AT / (norm + 1e-06))
    norm_ref[0:1, :] = jnp.broadcast_to(norm, (1, 128))
    norm_ref[1:2, :] = jnp.broadcast_to(factor, (1, 128))

    def mine(span):
        return pl.ds(pl.multiple_of(place[1] * span, span), span)

    def own(index, part):
        if index == 0:
            return first_ref[part, mine(given[0][0].shape[1]), :]
        if index == 1:
            return middle_ref[part, mine(given[1][0].shape[1]), :]
        if index == 2:
            return last_ref[mine(given[2][0].shape[0]), :]
        return embed_own[part] if index == 3 else back_own[...]

    for index in range(5):
        master, moment, second = given[index]
        outs = made[index]
        for part in range(master.shape[0]) if len(master.shape) == 3 else (slice(None),):
            values = adam_step(
                master[part], own(index, part), moment[part], second[part], factor, rates[index]
            )
            for ref, value in zip(outs, values):
                ref[part] = value


def late_grads(rates, place, half, other, squares, extra, embed_own, back_own, states, shapes):
    flat = tuple(item for state in states for item in state)
    outs = [(shape, F32) for shape in shapes] + [((2, 128), F32)]
    outs += [(state[0].shape, F32) for state in states for _ in range(3)]
    found = call(
        functools.partial(late_kernel, rates),
        outs,
        (place, half, other, squares, extra, embed_own, back_own) + flat,
        scratch=[pltpu.VMEM((8, 256), F32)],
        micros=8,
    )
    return found[:3], found[3], [found[4 + 3 * index : 7 + 3 * index] for index in range(5)]


def unfold(value, height):
    return jnp.moveaxis(value.reshape(-1, height, 256), 0, 1).reshape(height, -1)


def plain_tail(early, late, mean, grad_sum, sizes, norm_square, states, rates, chan_at):
    width, inner, narrow = sizes
    core = chan_at & 1
    early, late = [
        jnp.where(core == 0, jnp.concatenate([half, other]), jnp.concatenate([other, half])).astype(
            F32
        )
        for half, other in (early, late)
    ]
    cut = 3 * inner * width // 256
    embed = unfold(early[:cut], width).reshape(width, 3, inner)
    back = unfold(early[cut:], inner) + mean[:, None] * grad_sum[None, :]
    middle = late[: 9 * narrow].reshape(9, narrow, narrow)
    first = late[9 * narrow : 9 * narrow + 3 * width].reshape(3, width, narrow)
    last = unfold(late[9 * narrow + 3 * width :], narrow)
    grads = (first, middle, last, jnp.moveaxis(embed, 1, 0), back)
    norm = jnp.sqrt(sum(jnp.sum(item * item) for item in grads) + norm_square)
    factor = jnp.minimum(1.0, CLIP_AT / (norm + 1e-06))
    made = []
    for grad, state, rate in zip(grads, states, rates):
        axis = grad.ndim - 2
        span = state[0].shape[axis]
        owned = lax.dynamic_slice_in_dim(grad, chan_at * span, span, axis)
        made.append(adam_step(state[0], owned, state[1], state[2], factor, rate))
    return grads, norm, factor, made


def input_kernel(cols, weights, pre_grad, out_ref):
    shards, _, span, narrow = weights.shape
    each = 256 // span
    for at in range(0, pre_grad.shape[1], 256):
        out = pre_grad[:, at : at + 256]
        begin = at // span
        for tap in range(3):
            rows = weights[pl.ds(begin, each), tap].reshape(256, narrow)
            out = out + dot(cols[:, tap * narrow : (tap + 1) * narrow], rows, NT)
        span_at = slice(at, at + 256)
        out_ref[:, span_at] = out.astype(LOW)


def input_grad(cols, weights, pre_grad):
    rows, width = pre_grad.shape
    return call(
        input_kernel,
        [((rows, width), LOW)],
        (cols, weights, pre_grad),
        scalars=0,
    )[0]


def adam_step(master, gradient, moment, second, factor, rate):
    clipped = gradient * factor
    moment_new = BETA_ONE * moment + (1.0 - BETA_ONE) * clipped
    second_new = BETA_TWO * second + (1.0 - BETA_TWO) * clipped * clipped
    moment_hat = moment_new / (1.0 - BETA_ONE**STEP)
    second_hat = second_new / (1.0 - BETA_TWO**STEP)
    master_new = master - rate * (
        moment_hat / (jnp.sqrt(second_hat) + ADAM_EPS) + WEIGHT_DECAY * master
    )
    return (moment_new, second_new, master_new)


def body(
    features,
    cotangent,
    frame_counts,
    weight_first,
    weight_middle,
    weight_last,
    weight_embed,
    weight_back,
    norm_params,
    moment_first,
    moment_middle,
    moment_last,
    moment_embed,
    moment_back,
    moment_norm,
    second_first,
    second_middle,
    second_last,
    second_embed,
    second_back,
    second_norm,
):
    chan_at = lax.axis_index("chan")
    device = lax.axis_index("clip") * lax.axis_size("chan") + chan_at
    frames, spot_count, model_width = features.shape
    row_count = frames * spot_count
    narrow = BOT
    inner_width = INNER
    clip_place = chan_at % DPC
    clip_at = device // DPC
    clip_ids = jnp.arange(frame_counts.shape[0], dtype=jnp.int32)
    length = jnp.sum(jnp.where(clip_ids == clip_at, frame_counts, 0))

    def valid_at(place):
        return ((place >= 0) & (place < DPC) & (place * frames < length)).astype(jnp.float32)

    place = jnp.stack([chan_at & 1, chan_at]).astype(jnp.int32)
    own_ok = valid_at(clip_place)
    row_total = jnp.sum(frame_counts).astype(jnp.float32) * spot_count
    zero = jnp.zeros((), jnp.float32)
    flags = jnp.stack(
        [own_ok, valid_at(clip_place - 1), valid_at(clip_place + 1), 1.0 / row_total]
        + [valid_at(clip_place ^ 2)] + [zero] * 3
    )
    held = sum(valid_at(clip_place ^ turn) for turn in range(4)) * own_ok
    blocks_own = held.astype(jnp.int32).reshape(1)
    blocks_far = (held * valid_at(clip_place ^ 4)).astype(jnp.int32).reshape(1)
    span_list = [narrow] * 4 + [model_width] * 4
    starts = [sum(span_list[:index]) for index in range(8)]
    gains_one, gains_two, gains_three, gains_four = [
        norm_params[starts[index] : starts[index] + 2 * span_list[index]].reshape(2, -1)
        for index in range(0, 8, 2)
    ]
    shards = lax.axis_size("chan")
    first_low = whole_of(weight_first)
    tall = weight_middle.shape[0] * weight_middle.shape[1]
    packed = jnp.concatenate(
        [
            weight_middle.reshape(tall, narrow),
            jnp.moveaxis(weight_last.reshape(-1, model_width // 256, 256), 1, 0).reshape(-1, 256),
        ]
    ).astype(LOW)
    packed = lax.all_gather(packed, "chan", axis=0, tiled=False)
    middle_low = packed[:, :tall].reshape((shards,) + weight_middle.shape)
    last_low = jnp.moveaxis(
        packed[:, tall:].reshape(shards, model_width // 256, -1, 256), 1, 2
    ).reshape(narrow, model_width)
    if weight_middle.shape[1] % 16:
        middle_low = jnp.moveaxis(middle_low, 0, 1).reshape(1, 9, narrow, narrow)
    embed_low, back_low = (
        lax.all_gather(weight_embed.astype(LOW).reshape(-1, 3 * inner_width), "chan", axis=0, tiled=True),
        lax.all_gather(weight_back.astype(LOW), "chan", axis=0, tiled=True),
    )
    spots = np.arange(row_count)
    across, down = spots % WW, spots // WW % HH
    edges = jnp.asarray(
        np.stack([across > 0, across < WW - 1, down > 0, down < HH - 1] + [across < 0] * 4, axis=1)
        .astype(np.float32)
    )
    cells = features.reshape(row_count, model_width)
    cot = cotangent.reshape(row_count, model_width)
    before, after = beside(features, spot_count)
    pre_one, sums_one = first_conv(flags, cells, before, after, first_low)
    sums_one = total(sums_one)
    pre_two, sums_two = middle_conv(
        flags, pre_one, sums_one, gains_one, middle_low, edges
    )
    sums_two = total(sums_two)
    act_two, sums_three = last_conv(flags, pre_two, sums_two, gains_two, last_low)
    sums_three, cot = tied(total(sums_three), cot)
    residual_low, query, pair_own = embed_rows(
        flags, act_two, cells, last_low, sums_three, gains_three, embed_low
    )
    pair_core = flipped(pair_own, "chan", 1)
    query_far, pair_far = flipped(query, "chan", 4), flipped(pair_own, "chan", 2)
    query_far, pair_far, back_low = tied(query_far, pair_far, back_low)
    blocks = (pair_own, pair_core, pair_far, flipped(pair_far, "chan", 1))
    part_far, log_far = attend(blocks_far, query_far, blocks, True)
    part_far = flipped(part_far, "chan", 4)
    log_far = flipped(log_far, "chan", 4)
    part_own, log_own = attend(blocks_own, query, blocks, False)
    attended, logs, sums_four = merge(flags, part_own, log_own, part_far, log_far, back_low, cot)
    sums_four = total(sums_four)
    mixed, attn_grad, attended_grad, terms, packed, norm_four = outer(
        flags, attended, back_low, sums_four, gains_four, cot, residual_low, logs
    )
    mixed = laid_out(mixed, frames)
    attended_grad_far = flipped(attended_grad, "chan", 4)
    packed_far = flipped(packed, "chan", 4)
    query_own, held = attend_back(
        blocks_own, query, attended_grad, (logs, terms), blocks, (0, 1, 2, 3), None, None, F32
    )
    query_part, (far, far_core) = attend_back(
        blocks_far, query_far, attended_grad_far, (packed_far,), blocks[2:], (2, 3), held[2:], None, F32
    )
    far = (far.astype(F32) + flipped(far_core, "chan", 1).astype(F32)).astype(LOW)
    far, near_own = tied(far, held[0])
    far = flipped(far, "chan", 2)
    query_part, (keep, give_keys, give_values) = attend_back(
        blocks_far, query_far, attended_grad_far, (packed_far,), blocks[:2], (0, 1), (near_own, held[1]),
        query_part, LOW, (1,),
    )
    query_part = flipped(query_part, "chan", 4)
    near_keys, near_values = flipped(give_keys, "chan", 1), flipped(give_values, "chan", 1)
    projected_grad, pre_grad, back_three = project_back(
        flags, query_own, query_part, keep, near_keys, near_values, far, act_two, cells, last_low, sums_three,
        gains_three, embed_low, cot,
    )
    early = early_weight(
        place, flags, residual_low, projected_grad, attended, sums_four[4:5, :inner_width], attn_grad
    )
    back_three = total(jnp.concatenate([back_three, norm_four[2:3]]))
    early, back_three = tied(early, back_three)
    last_grad, two_grad, back_two = last_back(
        flags, pre_grad, act_two, last_low, sums_three, gains_three, back_three, pre_two, sums_two,
        gains_two,
    )
    back_two = total(back_two)
    last_local = weight_grad(act_two, last_grad)
    middle_grad, one_grad, back_one = middle_back(
        flags, two_grad, back_two, pre_two, sums_two, gains_two, pre_one, sums_one, gains_one,
        middle_low, edges,
    )
    back_one = total(back_one)
    middle_local = middle_weight(flags, pre_one, sums_one, gains_one, middle_grad, edges)
    first_grad = first_grad_of(flags, one_grad, back_one, pre_one, sums_one, gains_one)
    before, after = beside(first_grad.reshape(frames, spot_count, narrow), spot_count)
    late, grad_cols = first_back(place, flags, first_grad, before, after, cells, middle_local, last_local)
    features_gradient = laid_out(input_grad(grad_cols, first_low, pre_grad), frames)
    gain_one_grad, shift_one_grad = back_one[1], back_one[0]
    gain_two_grad, shift_two_grad = back_two[1], back_two[0]
    gain_three_grad, shift_three_grad = back_three[1], back_three[0]
    gain_four_grad, shift_four_grad = norm_four[0], norm_four[1]
    norm_gradient = jnp.concatenate(
        [
            gain_one_grad,
            shift_one_grad,
            gain_two_grad,
            shift_two_grad,
            gain_three_grad,
            shift_three_grad,
            gain_four_grad,
            shift_four_grad,
        ]
    )
    groups = [list(range(core, shards, 2)) for core in range(2)]
    early = lax.psum_scatter(core_step(*early), "clip", scatter_dimension=0, tiled=True)
    early = lax.psum(early, "chan", axis_index_groups=groups)
    steps = level_steps()[1:]
    late = scatter_sum(core_step(*late), steps)
    early, late = tied(early, late)
    early = lax.all_gather(early, "clip", axis=0, tiled=True)
    late = gather_sum(late, steps)
    early, late, mixed, features_gradient = tied(early, late, mixed, features_gradient)
    early = (early, flipped(early, "chan", 1))
    late = (late, flipped(late, "chan", 1))
    fans = (3 * D, 9 * BOT, BOT, D, INNER)
    rates = tuple(0.5 * fan ** (-0.5) for fan in fans)
    states = (
        (weight_first, moment_first, second_first),
        (weight_middle, moment_middle, second_middle),
        (weight_last, moment_last, second_last),
        tuple(jnp.moveaxis(item, 1, 0) for item in (weight_embed, moment_embed, second_embed)),
        (weight_back, moment_back, second_back),
    )
    norm_square = jnp.sum(norm_gradient * norm_gradient)
    if weight_middle.shape[1] % 16 == 0:
        embed, back, embed_own, back_own, squares = early_grads(
            place,
            flags,
            *early,
            sums_four[4:5, :inner_width],
            back_three[2:3],
            model_width,
            inner_width,
            shards,
        )
        shapes = ((3, model_width, narrow), (9, narrow, narrow), (narrow, model_width))
        (first, middle, last), norm_row, results = late_grads(
            rates, place, *late, squares, norm_square.reshape(1, 1), embed_own, back_own, states, shapes
        )
        gradient_norm, factor = norm_row[0, 0], norm_row[1, 0]
    else:
        (first, middle, last, embed, back), gradient_norm, factor, results = plain_tail(
            early,
            late,
            sums_four[4, :inner_width] * flags[3],
            back_three[2],
            (model_width, inner_width, narrow), norm_square, states, rates, chan_at
        )
    results = list(results)
    results[3] = tuple(jnp.moveaxis(item, 0, 1) for item in results[3])
    results.append(adam_step(norm_params, norm_gradient, moment_norm, second_norm, factor, GAIN_RATE))
    return (
        mixed,
        features_gradient,
        first,
        middle,
        last,
        jnp.moveaxis(embed, 0, 1),
        back,
        norm_gradient,
    ) + tuple(results[index][kind] for kind in range(3) for index in range(6)) + (gradient_norm,)


def solution(mesh):
    placed = (
        P(("clip", "chan"), None, None),
        P(("clip", "chan"), None, None),
        P(),
        P(None, "chan", None),
        P(None, "chan", None),
        P("chan", None),
        P("chan", None, None),
        P("chan", None),
        P(),
        P(None, "chan", None),
        P(None, "chan", None),
        P("chan", None),
        P("chan", None, None),
        P("chan", None),
        P(),
        P(None, "chan", None),
        P(None, "chan", None),
        P("chan", None),
        P("chan", None, None),
        P("chan", None),
        P(),
    )
    return jax.shard_map(
        body,
        mesh=mesh,
        in_specs=placed,
        out_specs=(
            P(("clip", "chan"), None, None),
            P(("clip", "chan"), None, None),
            P(),
            P(),
            P(),
            P(),
            P(),
            P(),
            P(None, "chan", None),
            P(None, "chan", None),
            P("chan", None),
            P("chan", None, None),
            P("chan", None),
            P(),
            P(None, "chan", None),
            P(None, "chan", None),
            P("chan", None),
            P("chan", None, None),
            P("chan", None),
            P(),
            P(None, "chan", None),
            P(None, "chan", None),
            P("chan", None),
            P("chan", None, None),
            P("chan", None),
            P(),
            P(),
        ),
        check_vma=False,
    )
```

profile of v0, /device:TPU:0, one launch (start us, length us, event | category | flops | bytes accessed | tf_op | source)
XLA Modules:
  0.0 592.5 jit_solution(4447740218662777316)
XLA Ops:
  13.7 2.4 collective-permute-start
  23.3 18.9 %all-gather.15.cloned.1.call-done = bf16[24,128,256]{2,1,0:T(8,128)(2,1)} async-done(((bf16[3,128,256]{2,1,0:T(8,128)(2,1)}), bf16[24,128,256]{2,1,0:T(8,128)(2,1)}) %all-gather.15.cloned.1.call-update) | async-done | bytes 1572880 | tf_op jit(solution)/shard_map/all_gather | solution.py:37
  43.6 2.3 shard_map.421
  49.1 2.5 collective-permute-start.5
  59.6 2.4 collective-permute-done.8
  62.0 7.8 %all-gather.7.cloned.1.call-done = bf16[8,416,256]{2,1,0:T(8,128)(2,1)} async-done(((bf16[1,416,256]{2,1,0:T(8,128)(2,1)}), bf16[8,416,256]{2,1,0:T(8,128)(2,1)}) %all-gather.7.cloned.1.call-update) | async-done | bytes 1703952 | tf_op jit(solution)/shard_map/all_gather | solution.py:1311
  72.7 2.2 shard_map.422
  89.3 2.4 collective-permute-done.15
  94.3 2.3 collective-permute-start.18
  96.6 2.0 collective-permute-start.19
  100.2 2.1 collective-permute-done.19
  103.6 2.2 collective-permute-start.22
  106.4 3.1 copy.71
  116.5 5.8 shard_map.424
  123.5 2.7 collective-permute-start.24
  126.2 26.6 %all-gather.11.cloned.1.call-done.weights = bf16[512,1024]{1,0:T(8,128)(2,1)} async-done(((bf16[64,1024]{1,0:T(8,128)(2,1)}), bf16[512,1024]{1,0:T(8,128)(2,1)}) %all-gather.11.cloned.1.call-update) | async-done | bytes 1048592 | tf_op jit(solution)/shard_map/all_gather | solution.py:1320
  152.8 26.9 %collective-permute-done.24.query = bf16[784,512]{1,0:T(8,128)(2,1)} collective-permute-done((bf16[784,512]{1,0:T(8,128)(2,1)}, bf16[784,512]{1,0:T(8,128)(2,1)}, u32[]{:S(2)}, u32[]{:S(2)}) %collective-permute-start.24) | collective-permute-done | bytes 802848 | tf_op jit(solution)/shard_map/ppermute | solution.py:33
  179.6 2.3 collective-permute-done.25.three.refs_4_.refs_1_
  185.8 3.6 shard_map.426
  192.4 7.4 %shard_map.425 = (bf16[784,512]{1,0:T(8,128)(2,1)S(1)}, f32[784,128]{1,0:T(8,128)S(1)}) custom-call(s32[1]{0:T(128)} %bitcast.17.count, bf16[784,512]{1,0:T(8,128)(2,1)} %get-tuple-element.123.query, bf16[784,1024]{1,0:T(8,128)(2,1)} %get-tuple-element.124.one.refs_2_, bf16[784,1024]{1,0:T(8,128)(2,1)S(1)} %collective-permute-done.23.two.refs_3_, ...), custom_call_target="tpu_custom_call" | custom-call | flops 10000000000 | tf_op jit(solution)/shard_map/pallas_call | solution.py:196
  199.7 29.0 %collective-permute-done.28.far_log = f32[8,896]{1,0:T(8,128)S(1)} collective-permute-done((f32[8,896]{1,0:T(8,128)S(1)}, f32[8,896]{1,0:T(8,128)S(1)}, u32[]{:S(2)}, u32[]{:S(2)}) %collective-permute-start.28) | collective-permute-done | bytes 28704 | tf_op jit(solution)/shard_map/ppermute | solution.py:33
  228.7 2.5 shard_map.427
  234.1 2.5 collective-permute-start.31
  239.6 2.7 collective-permute-done.32
  242.3 8.7 %collective-permute-start.33 = (f32[5,1024]{1,0:T(8,128)S(1)}, f32[5,1024]{1,0:T(8,128)}, u32[]{:S(2)}, u32[]{:S(2)}) collective-permute-start(f32[5,1024]{1,0:T(8,128)S(1)} %add_add_fusion.1), channel_id=1, source_target_pairs={{0,8},{8,0},{16,24},{24,16},{1,9},{9,1},{17,25},{25,17},{2,10},{10... | collective-permute-start | bytes 61448 | tf_op jit(solution)/shard_map/ppermute | solution.py:33
  255.1 2.4 collective-permute-done.35
  263.1 4.0 shard_map.428
  269.5 2.9 collective-permute-start.37
  272.4 12.0 %shard_map.429 = (f32[784,512]{1,0:T(8,128)S(1)}, bf16[784,1024]{1,0:T(8,128)(2,1)S(1)}, bf16[784,1024]{1,0:T(8,128)(2,1)S(1)}, bf16[784,1024]{1,0:T(8,128)(2,1)S(1)}, bf16[784,1024]{1,0:T(8,128)(2,1)S(1)}) custom-call(s32[1]{0:T(128)} %bitcast.17.count, bf16[784,512]{1,0:T(8,128)(2,1)} %get-tuple-element.123.query, ...), custom_call_target="tpu_custom_call" | custom-call | flops 16999999488 | tf_op jit(solution)/shard_map/pallas_call | solution.py:196
  285.6 18.9 %collective-permute-done.37.refs_0_ = f32[8,896]{1,0:T(8,128)S(1)} collective-permute-done((f32[8,896]{1,0:T(8,128)S(1)}, f32[8,896]{1,0:T(8,128)S(1)}, u32[]{:S(2)}, u32[]{:S(2)}) %collective-permute-start.37) | collective-permute-done | bytes 28704 | tf_op jit(solution)/shard_map/ppermute | solution.py:33
  304.4 3.4 shard_map.430
  308.0 3.4 collective-permute-done.38
  313.3 4.2 shard_map.431
  320.3 44.1 %collective-permute-done.39.query_far = bf16[784,512]{1,0:T(8,128)(2,1)S(1)} collective-permute-done((bf16[784,512]{1,0:T(8,128)(2,1)S(1)}, bf16[784,512]{1,0:T(8,128)(2,1)S(1)}, u32[]{:S(2)}, u32[]{:S(2)}) %collective-permute-start.39) | collective-permute-done | bytes 802848 | tf_op jit(solution)/shard_map/ppermute | solution.py:33
  364.3 2.2 collective-permute-done.42.far
  366.6 5.1 shard_map.432
  381.7 2.6 collective-permute-done.46
  384.3 8.5 %collective-permute-start.47 = (f32[3,1024]{1,0:T(4,128)S(1)}, f32[3,1024]{1,0:T(4,128)S(1)}, u32[]{:S(2)}, u32[]{:S(2)}) collective-permute-start(f32[3,1024]{1,0:T(4,128)S(1)} %add_add_fusion.3), channel_id=1, source_target_pairs={{0,8},{8,0},{16,24},{24,16},{1,9},{9,1},{17,25},{25,17},{2,10},{10... | collective-permute-start | bytes 36872 | tf_op jit(solution)/shard_map/ppermute | solution.py:33
  400.0 5.7 shard_map.433
  405.9 2.2 shard_map.435
  410.0 2.3 collective-permute-start.53
  412.2 2.1 collective-permute-start.54
  414.4 3.2 collective-permute-done.54
  417.6 1.9 collective-permute-start.55
  424.6 2.4 shard_map.436
  429.9 2.7 collective-permute-start.60
  447.6 3.2 shard_map.438.middle
  450.9 3.0 shard_map.440
  457.1 3.3 collective-permute-done.67.arrived
  464.0 2.0 collective-permute-start.68
  467.6 4.4 reduce-scatter.2.cloned.1.call-done
  472.4 5.7 collective-permute-done.68
  478.0 9.5 %collective-permute-done.70 = bf16[800,256]{1,0:T(8,128)(2,1)} collective-permute-done((bf16[800,256]{1,0:T(8,128)(2,1)S(1)}, bf16[800,256]{1,0:T(8,128)(2,1)}, u32[]{:S(2)}, u32[]{:S(2)}) %collective-permute-start.70) | collective-permute-done | bytes 409632 | tf_op jit(solution)/shard_map/ppermute | solution.py:33
  490.6 2.4 collective-permute-start.72
  493.5 2.7 collective-permute-done.71
  496.2 5.5 collective-permute-done.72
  501.8 13.5 %all-reduce.2.cloned.1.call-done = bf16[1024,256]{1,0:T(8,128)(2,1)} async-done(((bf16[1024,256]{1,0:T(8,128)(2,1)}), bf16[1024,256]{1,0:T(8,128)(2,1)}) %all-reduce.2.cloned.1.call-update) | async-done | bytes 524304 | tf_op jit(solution)/shard_map/psum | solution.py:1416
  521.8 4.5 collective-permute-done.75
  530.4 4.0 copy.74
  539.9 3.8 copy.75
  548.1 13.5 %collective-permute-done.79 = bf16[800,256]{1,0:T(8,128)(2,1)S(1)} collective-permute-done((bf16[800,256]{1,0:T(8,128)(2,1)}, bf16[800,256]{1,0:T(8,128)(2,1)S(1)}, u32[]{:S(2)}, u32[]{:S(2)}) %collective-permute-start.79) | collective-permute-done | bytes 409632 | tf_op jit(solution)/shard_map/ppermute | solution.py:33
  564.3 4.7 collective-permute-done.81.other
  570.7 6.4 %shard_map.443 = (f32[3,1024,512]{2,1,0:T(8,128)}, f32[512,1024]{1,0:T(8,128)}, f32[3,128,512]{2,1,0:T(8,128)S(1)}, f32[64,1024]{1,0:T(8,128)S(1)}, f32[8,256]{1,0:T(8,128)S(1)}) custom-call(s32[2]{0:T(128)S(1)} %pad_add_fusion.place, f32[8]{0:T(128)S(1)} %stack.43.flags, bf16[4096,256]{1,0:T(8,128)(2,1)S(1)} %copy-done.27, ...), custom_call_target="tpu_custom_call" | custom-call | flops 6000000000 | tf_op jit(solution)/shard_map/pallas_call | solution.py:196
  577.3 6.1 %shard_map.444 = (f32[3,1024,256]{2,1,0:T(8,128)}, f32[9,256,256]{2,1,0:T(8,128)}, f32[256,1024]{1,0:T(8,128)}, f32[2,128]{1,0:T(2,128)S(1)}, f32[3,128,256]{2,1...) custom-call(s32[2]{0:T(128)S(1)} %pad_add_fusion.place, ...), custom_call_target="tpu_custom_call" | custom-call | flops 8000000000 | tf_op jit(solution)/shard_map/pallas_call | solution.py:196
  (412 shorter events, 163.7 us)
Async XLA Ops:
  7.2 35.0 %all-gather.15.cloned.1.call-start = ((), (), s32[]{:S(2)}) async-start(), calls=%async_computation.7 | async-start | bytes 1769472 | tf_op jit(solution)/shard_map/all_gather | solution.py:37
  9.0 60.8 %all-gather.7.cloned.1.call-start = ((), (), s32[]{:S(2)}) async-start(), calls=%async_computation.1 | async-start | bytes 1916928 | tf_op jit(solution)/shard_map/all_gather | solution.py:1311
  11.9 100.7 %all-gather.9.cloned.1.call-start = ((), (), s32[]{:S(2)}) async-start(), calls=%async_computation.2 | async-start | bytes 3538944 | tf_op jit(solution)/shard_map/all_gather | solution.py:1319
  13.1 139.7 %all-gather.11.cloned.1.call-start = ((), (), s32[]{:S(2)}) async-start(), calls=%async_computation.3 | async-start | bytes 1179648 | tf_op jit(solution)/shard_map/all_gather | solution.py:1320
  13.7 9.6 %collective-permute-start = (bf16[1,196,1024]{2,1,0:T(8,128)(2,1)S(1)}, bf16[1,196,1024]{2,1,0:T(8,128)(2,1)S(1)}, u32[]{:S(2)}, u32[]{:S(2)}) collective-permute-start(bf16[1,196,1024]{2,1,0:T(8,128)(2,1)S(1)} %get-tuple-element.212), channel_id=1, source_target_pairs={{0,1},{1,2},{2,3},{3,4},{4,5},{5,6},{6,7},{8,9},{9,10},{10,11},{11... | collective-permute-start | bytes 1204232 | tf_op jit(solution)/shard_map/ppermute | solution.py:49
  16.1 7.2 %collective-permute-start.1 = (bf16[1,196,1024]{2,1,0:T(8,128)(2,1)S(1)}, bf16[1,196,1024]{2,1,0:T(8,128)(2,1)S(1)}, u32[]{:S(2)}, u32[]{:S(2)}) collective-permute-start(bf16[1,196,1024]{2,1,0:T(8,128)(2,1)S(1)} %get-tuple-element.211), channel_id=1, source_target_pairs={{1,0},{2,1},{3,2},{4,3},{5,4},{6,5},{7,6},{9,8},{10,9},{11,10},{12... | collective-permute-start | bytes 1204232 | tf_op jit(solution)/shard_map/ppermute | solution.py:50
  48.8 4.5 collective-permute-start.4
  49.1 5.5 collective-permute-start.5
  57.5 4.5 collective-permute-start.8
  77.8 4.6 collective-permute-start.11
  78.7 5.5 collective-permute-start.12
  94.3 5.3 collective-permute-start.17
  94.3 5.9 collective-permute-start.18
  96.6 5.6 collective-permute-start.19
  99.4 372.7 %reduce-scatter.2.cloned.1.call-start = ((), (), s32[]{:S(2)}) async-start(), calls=%async_computation.4 | async-start | bytes 2621440 | tf_op jit(solution)/shard_map/reduce_scatter | solution.py:1415
  102.3 8.8 %collective-permute-start.20 = (f32[2,1024]{1,0:T(2,128)S(1)}, f32[2,1024]{1,0:T(2,128)S(1)}, u32[]{:S(2)}, u32[]{:S(2)}) collective-permute-start(f32[2,1024]{1,0:T(2,128)S(1)} %add_add_fusion.5), channel_id=1, source_target_pairs={{0,8},{8,0},{16,24},{24,16},{1,9},{9,1},{17,25},{25,17},{2,10},{10... | collective-permute-start | bytes 24584 | tf_op jit(solution)/shard_map/ppermute | solution.py:33
  102.9 8.2 %collective-permute-start.21 = (f32[2,1024]{1,0:T(2,128)S(1)}, f32[2,1024]{1,0:T(2,128)}, u32[]{:S(2)}, u32[]{:S(2)}) collective-permute-start(f32[2,1024]{1,0:T(2,128)S(1)} %add_add_fusion.5), channel_id=1, source_target_pairs={{0,16},{8,24},{16,0},{24,8},{1,17},{9,25},{17,1},{25,9},{2,18},{10... | collective-permute-start | bytes 24584 | tf_op jit(solution)/shard_map/ppermute | solution.py:33
  103.6 8.2 %collective-permute-start.22 = (f32[2,1024]{1,0:T(2,128)S(1)}, f32[2,1024]{1,0:T(2,128)}, u32[]{:S(2)}, u32[]{:S(2)}) collective-permute-start(f32[2,1024]{1,0:T(2,128)S(1)} %add_add_fusion.5), channel_id=1, source_target_pairs={{0,24},{8,16},{16,8},{24,0},{1,25},{9,17},{17,9},{25,1},{2,26},{10... | collective-permute-start | bytes 24584 | tf_op jit(solution)/shard_map/ppermute | solution.py:33
  123.5 58.5 %collective-permute-start.25 = (bf16[784,1024]{1,0:T(8,128)(2,1)}, bf16[784,1024]{1,0:T(8,128)(2,1)}, u32[]{:S(2)}, u32[]{:S(2)}) collective-permute-start(bf16[784,1024]{1,0:T(8,128)(2,1)} %get-tuple-element.124.one.refs_2_), channel_id=1, source_target_pairs={{0,2},{1,3},{2,0},{3,1},{4,6},{5,7},{6,4},{7,5},{8,10},{9,11},{10,... | collective-permute-start | bytes 4816904 | tf_op jit(solution)/shard_map/ppermute | solution.py:33
  123.5 56.1 %collective-permute-start.24 = (bf16[784,512]{1,0:T(8,128)(2,1)}, bf16[784,512]{1,0:T(8,128)(2,1)}, u32[]{:S(2)}, u32[]{:S(2)}) collective-permute-start(bf16[784,512]{1,0:T(8,128)(2,1)} %get-tuple-element.123.query), channel_id=1, source_target_pairs={{0,4},{1,5},{2,6},{3,7},{4,0},{5,1},{6,2},{7,3},{8,12},{9,13},{10,... | collective-permute-start | bytes 2408456 | tf_op jit(solution)/shard_map/ppermute | solution.py:33
  126.2 57.8 %collective-permute-start.23 = (bf16[784,1024]{1,0:T(8,128)(2,1)}, bf16[784,1024]{1,0:T(8,128)(2,1)S(1)}, u32[]{:S(2)}, u32[]{:S(2)}) collective-permute-start(bf16[784,1024]{1,0:T(8,128)(2,1)} %get-tuple-element.124.one.refs_2_), channel_id=1, source_target_pairs={{0,1},{1,0},{2,3},{3,2},{4,5},{5,4},{6,7},{7,6},{8,9},{9,8},{10,11... | collective-permute-start | bytes 4816904 | tf_op jit(solution)/shard_map/ppermute | solution.py:33
  189.4 39.3 %collective-permute-start.27 = (bf16[784,512]{1,0:T(8,128)(2,1)S(1)}, bf16[784,512]{1,0:T(8,128)(2,1)S(1)}, u32[]{:S(2)}, u32[]{:S(2)}) collective-permute-start(bf16[784,512]{1,0:T(8,128)(2,1)S(1)} %get-tuple-element.129), channel_id=1, source_target_pairs={{0,4},{1,5},{2,6},{3,7},{4,0},{5,1},{6,2},{7,3},{8,12},{9,13},{10,... | collective-permute-start | bytes 2408456 | tf_op jit(solution)/shard_map/ppermute | solution.py:33
  190.5 38.2 %collective-permute-start.28 = (f32[8,896]{1,0:T(8,128)S(1)}, f32[8,896]{1,0:T(8,128)S(1)}, u32[]{:S(2)}, u32[]{:S(2)}) collective-permute-start(f32[8,896]{1,0:T(8,128)S(1)} %get-tuple-element.130), channel_id=1, source_target_pairs={{0,4},{1,5},{2,6},{3,7},{4,0},{5,1},{6,2},{7,3},{8,12},{9,13},{10,... | collective-permute-start | bytes 86024 | tf_op jit(solution)/shard_map/ppermute | solution.py:33
  234.1 5.6 collective-permute-start.31
  236.6 5.7 collective-permute-start.32
  242.3 11.0 %collective-permute-start.33 = (f32[5,1024]{1,0:T(8,128)S(1)}, f32[5,1024]{1,0:T(8,128)}, u32[]{:S(2)}, u32[]{:S(2)}) collective-permute-start(f32[5,1024]{1,0:T(8,128)S(1)} %add_add_fusion.1), channel_id=1, source_target_pairs={{0,8},{8,0},{16,24},{24,16},{1,9},{9,1},{17,25},{25,17},{2,10},{10... | collective-permute-start | bytes 61448 | tf_op jit(solution)/shard_map/ppermute | solution.py:33
  252.5 4.9 collective-permute-start.35
  269.5 35.0 %collective-permute-start.36 = (bf16[784,512]{1,0:T(8,128)(2,1)S(1)}, bf16[784,512]{1,0:T(8,128)(2,1)S(1)}, u32[]{:S(2)}, u32[]{:S(2)}) collective-permute-start(bf16[784,512]{1,0:T(8,128)(2,1)S(1)} %get-tuple-element.136.grad), channel_id=1, source_target_pairs={{0,4},{1,5},{2,6},{3,7},{4,0},{5,1},{6,2},{7,3},{8,12},{9,13},{10,... | collective-permute-start | bytes 2408456 | tf_op jit(solution)/shard_map/ppermute | solution.py:33
  269.5 35.0 %collective-permute-start.37 = (f32[8,896]{1,0:T(8,128)S(1)}, f32[8,896]{1,0:T(8,128)S(1)}, u32[]{:S(2)}, u32[]{:S(2)}) collective-permute-start(f32[8,896]{1,0:T(8,128)S(1)} %get-tuple-element.139), channel_id=1, source_target_pairs={{0,4},{1,5},{2,6},{3,7},{4,0},{5,1},{6,2},{7,3},{8,12},{9,13},{10,... | collective-permute-start | bytes 86024 | tf_op jit(solution)/shard_map/ppermute | solution.py:33
  312.1 54.4 %collective-permute-start.42 = (bf16[784,1024]{1,0:T(8,128)(2,1)S(1)}, bf16[784,1024]{1,0:T(8,128)(2,1)S(1)}, u32[]{:S(2)}, u32[]{:S(2)}) collective-permute-start(bf16[784,1024]{1,0:T(8,128)(2,1)S(1)} %add_convert_fusion), channel_id=1, source_target_pairs={{0,2},{1,3},{2,0},{3,1},{4,6},{5,7},{6,4},{7,5},{8,10},{9,11},{10,... | collective-permute-start | bytes 4816904 | tf_op jit(solution)/shard_map/ppermute | solution.py:33
  317.5 46.8 %collective-permute-start.39 = (bf16[784,512]{1,0:T(8,128)(2,1)S(1)}, bf16[784,512]{1,0:T(8,128)(2,1)S(1)}, u32[]{:S(2)}, u32[]{:S(2)}) collective-permute-start(bf16[784,512]{1,0:T(8,128)(2,1)S(1)} %get-tuple-element.148), channel_id=1, source_target_pairs={{0,4},{1,5},{2,6},{3,7},{4,0},{5,1},{6,2},{7,3},{8,12},{9,13},{10,... | collective-permute-start | bytes 2408456 | tf_op jit(solution)/shard_map/ppermute | solution.py:33
  319.2 45.2 %collective-permute-start.40 = (bf16[784,512]{1,0:T(8,128)(2,1)S(1)}, bf16[784,512]{1,0:T(8,128)(2,1)S(1)}, u32[]{:S(2)}, u32[]{:S(2)}) collective-permute-start(bf16[784,512]{1,0:T(8,128)(2,1)S(1)} %get-tuple-element.150), channel_id=1, source_target_pairs={{0,1},{1,0},{2,3},{3,2},{4,5},{5,4},{6,7},{7,6},{8,9},{9,8},{10,11... | collective-permute-start | bytes 2408456 | tf_op jit(solution)/shard_map/ppermute | solution.py:33
  319.2 45.2 %collective-permute-start.41 = (bf16[784,512]{1,0:T(8,128)(2,1)S(1)}, bf16[784,512]{1,0:T(8,128)(2,1)S(1)}, u32[]{:S(2)}, u32[]{:S(2)}) collective-permute-start(bf16[784,512]{1,0:T(8,128)(2,1)S(1)} %get-tuple-element.151), channel_id=1, source_target_pairs={{0,1},{1,0},{2,3},{3,2},{4,5},{5,4},{6,7},{7,6},{8,9},{9,8},{10,11... | collective-permute-start | bytes 2408456 | tf_op jit(solution)/shard_map/ppermute | solution.py:33
  376.0 4.5 collective-permute-start.44
  377.1 4.6 collective-permute-start.45
  378.8 5.5 collective-permute-start.46
  384.3 21.4 %collective-permute-start.47 = (f32[3,1024]{1,0:T(4,128)S(1)}, f32[3,1024]{1,0:T(4,128)S(1)}, u32[]{:S(2)}, u32[]{:S(2)}) collective-permute-start(f32[3,1024]{1,0:T(4,128)S(1)} %add_add_fusion.3), channel_id=1, source_target_pairs={{0,8},{8,0},{16,24},{24,16},{1,9},{9,1},{17,25},{25,17},{2,10},{10... | collective-permute-start | bytes 36872 | tf_op jit(solution)/shard_map/ppermute | solution.py:33
  392.8 12.9 %collective-permute-start.48 = (f32[3,1024]{1,0:T(4,128)S(1)}, f32[3,1024]{1,0:T(4,128)S(1)}, u32[]{:S(2)}, u32[]{:S(2)}) collective-permute-start(f32[3,1024]{1,0:T(4,128)S(1)} %add_add_fusion.3), channel_id=1, source_target_pairs={{0,16},{8,24},{16,0},{24,8},{1,17},{9,25},{17,1},{25,9},{2,18},{10... | collective-permute-start | bytes 36872 | tf_op jit(solution)/shard_map/ppermute | solution.py:33
  393.3 12.4 %collective-permute-start.49 = (f32[3,1024]{1,0:T(4,128)S(1)}, f32[3,1024]{1,0:T(4,128)S(1)}, u32[]{:S(2)}, u32[]{:S(2)}) collective-permute-start(f32[3,1024]{1,0:T(4,128)S(1)} %add_add_fusion.3), channel_id=1, source_target_pairs={{0,24},{8,16},{16,8},{24,0},{1,25},{9,17},{17,9},{25,1},{2,26},{10... | collective-permute-start | bytes 36872 | tf_op jit(solution)/shard_map/ppermute | solution.py:33
  405.7 28.6 %collective-permute-start.50 = (bf16[4096,256]{1,0:T(8,128)(2,1)S(1)}, bf16[4096,256]{1,0:T(8,128)(2,1)S(1)}, u32[]{:S(2)}, u32[]{:S(2)}) collective-permute-start(bf16[4096,256]{1,0:T(8,128)(2,1)S(1)} %get-tuple-element.160), channel_id=1, source_target_pairs={{0,1},{1,0},{2,3},{3,2},{4,5},{5,4},{6,7},{7,6},{8,9},{9,8},{10,11... | collective-permute-start | bytes 6291464 | tf_op jit(solution)/shard_map/ppermute | solution.py:33
  410.0 4.5 collective-permute-start.53
  412.2 5.4 collective-permute-start.54
  429.9 6.3 %collective-permute-start.59 = (f32[2,256]{1,0:T(2,128)S(1)}, f32[2,256]{1,0:T(2,128)S(1)}, u32[]{:S(2)}, u32[]{:S(2)}) collective-permute-start(f32[2,256]{1,0:T(2,128)S(1)} %add.307), channel_id=1, source_target_pairs={{0,2},{1,3},{2,0},{3,1},{4,6},{5,7},{6,4},{7,5},{8,10},{9,11},{10,... | collective-permute-start | bytes 6152 | tf_op jit(solution)/shard_map/ppermute | solution.py:33
  429.9 6.3 %collective-permute-start.60 = (f32[2,256]{1,0:T(2,128)S(1)}, f32[2,256]{1,0:T(2,128)S(1)}, u32[]{:S(2)}, u32[]{:S(2)}) collective-permute-start(f32[2,256]{1,0:T(2,128)S(1)} %add.307), channel_id=1, source_target_pairs={{0,4},{1,5},{2,6},{3,7},{4,0},{5,1},{6,2},{7,3},{8,12},{9,13},{10,... | collective-permute-start | bytes 6152 | tf_op jit(solution)/shard_map/ppermute | solution.py:33
  432.5 5.4 collective-permute-start.61
  436.1 79.1 %all-reduce.2.cloned.1.call-start = ((), (), s32[]{:S(2)}) async-start(), calls=%async_computation.5 | async-start | bytes 1048576 | tf_op jit(solution)/shard_map/psum | solution.py:1416
  439.5 4.6 collective-permute-start.64
  444.9 5.9 collective-permute-start.65
  446.3 4.6 collective-permute-start.66
  464.0 14.0 %collective-permute-start.68 = (bf16[800,256]{1,0:T(8,128)(2,1)S(1)}, bf16[800,256]{1,0:T(8,128)(2,1)}, u32[]{:S(2)}, u32[]{:S(2)}) collective-permute-start(bf16[800,256]{1,0:T(8,128)(2,1)S(1)} %get-tuple-element.208), channel_id=1, source_target_pairs={{0,8},{8,0},{16,24},{24,16},{1,9},{9,1},{17,25},{25,17},{2,10},{10... | collective-permute-start | bytes 1228808 | tf_op jit(solution)/shard_map/ppermute | solution.py:33
  466.1 12.0 %collective-permute-start.69 = (bf16[800,256]{1,0:T(8,128)(2,1)S(1)}, bf16[800,256]{1,0:T(8,128)(2,1)}, u32[]{:S(2)}, u32[]{:S(2)}) collective-permute-start(bf16[800,256]{1,0:T(8,128)(2,1)S(1)} %get-tuple-element.210), channel_id=1, source_target_pairs={{0,16},{8,24},{16,0},{24,8},{1,17},{9,25},{17,1},{25,9},{2,18},{10... | collective-permute-start | bytes 1228808 | tf_op jit(solution)/shard_map/ppermute | solution.py:33
  466.3 21.2 %collective-permute-start.70 = (bf16[800,256]{1,0:T(8,128)(2,1)S(1)}, bf16[800,256]{1,0:T(8,128)(2,1)}, u32[]{:S(2)}, u32[]{:S(2)}) collective-permute-start(bf16[800,256]{1,0:T(8,128)(2,1)S(1)} %get-tuple-element.209), channel_id=1, source_target_pairs={{0,24},{8,16},{16,8},{24,0},{1,25},{9,17},{17,9},{25,1},{2,26},{10... | collective-permute-start | bytes 1228808 | tf_op jit(solution)/shard_map/ppermute | solution.py:33
  472.1 90.9 %all-gather.13.cloned.1.call-start = ((), (), s32[]{:S(2)}) async-start(), calls=%async_computation.6 | async-start | bytes 2621440 | tf_op jit(solution)/shard_map/all_gather | solution.py:1420
  489.1 7.1 %collective-permute-start.71 = (bf16[200,256]{1,0:T(8,128)(2,1)S(1)}, bf16[200,256]{1,0:T(8,128)(2,1)S(1)}, u32[]{:S(2)}, u32[]{:S(2)}) collective-permute-start(bf16[200,256]{1,0:T(8,128)(2,1)S(1)} %get-tuple-element.213), channel_id=1, source_target_pairs={{0,2},{1,3},{2,0},{3,1},{4,6},{5,7},{6,4},{7,5},{8,10},{9,11},{10,... | collective-permute-start | bytes 307208 | tf_op jit(solution)/shard_map/ppermute | solution.py:33
  490.6 11.1 %collective-permute-start.72 = (bf16[200,256]{1,0:T(8,128)(2,1)S(1)}, bf16[200,256]{1,0:T(8,128)(2,1)S(1)}, u32[]{:S(2)}, u32[]{:S(2)}) collective-permute-start(bf16[200,256]{1,0:T(8,128)(2,1)S(1)} %get-tuple-element.215), channel_id=1, source_target_pairs={{0,4},{1,5},{2,6},{3,7},{4,0},{5,1},{6,2},{7,3},{8,12},{9,13},{10,... | collective-permute-start | bytes 307208 | tf_op jit(solution)/shard_map/ppermute | solution.py:33
  493.0 8.6 %collective-permute-start.73 = (bf16[200,256]{1,0:T(8,128)(2,1)S(1)}, bf16[200,256]{1,0:T(8,128)(2,1)S(1)}, u32[]{:S(2)}, u32[]{:S(2)}) collective-permute-start(bf16[200,256]{1,0:T(8,128)(2,1)S(1)} %get-tuple-element.214), channel_id=1, source_target_pairs={{0,6},{1,7},{2,4},{3,5},{4,2},{5,3},{6,0},{7,1},{8,14},{9,15},{10,... | collective-permute-start | bytes 307208 | tf_op jit(solution)/shard_map/ppermute | solution.py:33
  515.3 5.9 collective-permute-start.74
  516.6 9.7 %collective-permute-start.75 = (bf16[200,256]{1,0:T(8,128)(2,1)S(1)}, bf16[200,256]{1,0:T(8,128)(2,1)S(1)}, u32[]{:S(2)}, u32[]{:S(2)}) collective-permute-start(bf16[200,256]{1,0:T(8,128)(2,1)S(1)} %add_convert_fusion.2), channel_id=1, source_target_pairs={{0,4},{1,5},{2,6},{3,7},{4,0},{5,1},{6,2},{7,3},{8,12},{9,13},{10,... | collective-permute-start | bytes 307208 | tf_op jit(solution)/shard_map/ppermute | solution.py:33
  518.3 8.6 %collective-permute-start.76 = (bf16[200,256]{1,0:T(8,128)(2,1)S(1)}, bf16[200,256]{1,0:T(8,128)(2,1)S(1)}, u32[]{:S(2)}, u32[]{:S(2)}) collective-permute-start(bf16[200,256]{1,0:T(8,128)(2,1)S(1)} %add_convert_fusion.2), channel_id=1, source_target_pairs={{0,6},{1,7},{2,4},{3,5},{4,2},{5,3},{6,0},{7,1},{8,14},{9,15},{10,... | collective-permute-start | bytes 307208 | tf_op jit(solution)/shard_map/ppermute | solution.py:33
  527.6 17.9 %collective-permute-start.77 = (bf16[800,256]{1,0:T(8,128)(2,1)}, bf16[800,256]{1,0:T(8,128)(2,1)}, u32[]{:S(2)}, u32[]{:S(2)}) collective-permute-start(bf16[800,256]{1,0:T(8,128)(2,1)} %bitcast.28), channel_id=1, source_target_pairs={{0,8},{8,0},{16,24},{24,16},{1,9},{9,1},{17,25},{25,17},{2,10},{10... | collective-permute-start | bytes 1228808 | tf_op jit(solution)/shard_map/ppermute | solution.py:33
  534.3 12.7 %collective-permute-start.78 = (bf16[800,256]{1,0:T(8,128)(2,1)}, bf16[800,256]{1,0:T(8,128)(2,1)}, u32[]{:S(2)}, u32[]{:S(2)}) collective-permute-start(bf16[800,256]{1,0:T(8,128)(2,1)} %bitcast.28), channel_id=1, source_target_pairs={{0,16},{8,24},{16,0},{24,8},{1,17},{9,25},{17,1},{25,9},{2,18},{10... | collective-permute-start | bytes 1228808 | tf_op jit(solution)/shard_map/ppermute | solution.py:33
  543.7 17.9 %collective-permute-start.79 = (bf16[800,256]{1,0:T(8,128)(2,1)}, bf16[800,256]{1,0:T(8,128)(2,1)S(1)}, u32[]{:S(2)}, u32[]{:S(2)}) collective-permute-start(bf16[800,256]{1,0:T(8,128)(2,1)} %bitcast.28), channel_id=1, source_target_pairs={{0,24},{8,16},{16,8},{24,0},{1,25},{9,17},{17,9},{25,1},{2,26},{10... | collective-permute-start | bytes 1228808 | tf_op jit(solution)/shard_map/ppermute | solution.py:33
  563.0 6.0 %collective-permute-start.81 = (bf16[4096,256]{1,0:T(8,128)(2,1)}, bf16[4096,256]{1,0:T(8,128)(2,1)}, u32[]{:S(2)}, u32[]{:S(2)}) collective-permute-start(bf16[4096,256]{1,0:T(8,128)(2,1)} %all-gather.13.cloned.1.call-done.half), channel_id=1, source_target_pairs={{0,1},{1,0},{2,3},{3,2},{4,5},{5,4},{6,7},{7,6},{8,9},{9,8},{10,11... | collective-permute-start | bytes 6291464 | tf_op jit(solution)/shard_map/ppermute | solution.py:33
  563.0 14.1 %collective-permute-start.80 = (bf16[3200,256]{1,0:T(8,128)(2,1)S(1)}, bf16[3200,256]{1,0:T(8,128)(2,1)S(1)}, u32[]{:S(2)}, u32[]{:S(2)}) collective-permute-start(bf16[3200,256]{1,0:T(8,128)(2,1)S(1)} %bitcast.70), channel_id=1, source_target_pairs={{0,1},{1,0},{2,3},{3,2},{4,5},{5,4},{6,7},{7,6},{8,9},{9,8},{10,11... | collective-permute-start | bytes 4915208 | tf_op jit(solution)/shard_map/ppermute | solution.py:33
  (116 other events, 1211.5 us)
Sparse Core Ops, SparseCore 0:
  10.3 31.9 all-gather.14
  44.5 25.3 all-gather.6
  72.0 38.5 all-gather.8
  112.7 40.0 all-gather.10
  436.2 35.7 reduce-scatter.1
  474.4 40.8 all-reduce.1
  517.2 45.7 all-gather.12
where the time goes:
time: 601 us; the launch traced here: 592 us
  waiting for transfers between devices  298 us (50%)
  starting transfers between devices  105 us (17%)
  Pallas kernels  89.5 us (15%)
  local copies, waits for them, and re-layouts  65.2 us (11%)
  between operations  21.3 us (4%)
  other arithmetic  13 us (2%)
    ppermute x78, waiting for transfers between devices, flipped(): return lax.ppermute(value, axis, pairs)  225 us
    ppermute x78, starting transfers between devices, flipped(): return lax.ppermute(value, axis, pairs)  98.3 us
    pallas_call x24, Pallas kernels, call(): pl.pallas_call(kernel, out_shape=shapes, in_specs=spaces, out_specs=out_s...  89.5 us
    unnamed x191, local copies, waits for them, and re-layouts  39.5 us
    all_gather x1, waiting for transfers between devices, body(): lax.all_gather(weight_back.astype(LOW), 'chan', axis=0, tiled=True)  26.6 us
    all_gather x1, waiting for transfers between devices, whole_of(): lax.all_gather(shard.astype(jnp.bfloat16), 'chan', axis=0, tiled=False)  18.9 us
    psum x1, waiting for transfers between devices, body(): early = lax.psum(early, 'chan', axis_index_groups=groups)  13.5 us
  transfers between devices with their start and end apart: 89, of which 54 were waited for; matrix products, arithmetic and copies ran while one was open for 6% of the time, Pallas kernels for 11%

commit v1 on v0

--- a/solution.py
+++ b/solution.py
@@ -35,6 +35,18 @@
 
 def whole_of(shard):
     return lax.all_gather(shard.astype(jnp.bfloat16), "chan", axis=0, tiled=False)
+
+
+def quarters_of(shard):
+    span = shard.shape[1] // 4
+    piece = lax.dynamic_slice_in_dim(
+        shard.astype(jnp.bfloat16), lax.axis_index("clip") * span, span, axis=1
+    )[None]
+    chips = jnp.concatenate(
+        [piece] + [flipped(piece, "chan", 2 * turn) for turn in range(1, 4)]
+    )[None]
+    mine = jnp.concatenate([chips] + [flipped(chips, "clip", turn) for turn in range(1, 4)])
+    return mine, flipped(mine, "chan", 1)
 
 
 def tap_of(weights, tap):
@@ -206,7 +218,7 @@
     )(*args)
 
 
-def first_kernel(flags, cells, before, after, weights, pre_ref, sums_ref, early, late):
+def first_tail(flags, cells, before, after, weights, pre_ref, sums_ref, early, late):
     rows = cells.shape[0]
     spots = before.shape[0]
     valid = flags[0]
@@ -224,12 +236,39 @@
     sums_ref[1:2, :] = column_sums(pre * pre) * valid
 
 
+def first_parts_kernel(place, flags, cells, before, after, mine, others, pre_ref, sums_ref, weights, early, late):
+    for index in range(mine.shape[0]):
+        span = mine.shape[3]
+        rows = pl.ds(pl.multiple_of((place[2] ^ index) * span, span), span)
+        for turn in range(mine.shape[1]):
+            weights[place[1] ^ (2 * turn), :, rows, :] = mine[index, turn]
+            weights[place[1] ^ (2 * turn + 1), :, rows, :] = others[index, turn]
+    first_tail(flags, cells, before, after, weights, pre_ref, sums_ref, early, late)
+
+
+def first_conv_parts(place, flags, cells, before, after, mine, others):
+    rows = cells.shape[0]
+    clips, chips, taps, span, narrow = mine.shape
+    spots = before.shape[0]
+    return call(
+        first_parts_kernel,
+        [
+            ((rows, narrow), F32),
+            ((2, narrow), F32),
+            ((2 * chips, taps, clips * span, narrow), LOW),
+        ],
+        (place, flags, cells, before, after, mine, others),
+        scalars=2,
+        scratch=[pltpu.VMEM((rows + spots, narrow), F32)] * 2,
+    )
+
+
 def first_conv(flags, cells, before, after, weights):
     rows, width = cells.shape
     narrow = weights.shape[3]
     spots = before.shape[0]
     return call(
-        first_kernel,
+        first_tail,
         [((rows, narrow), F32), ((2, narrow), F32)],
         (flags, cells, before, after, weights),
         scratch=[pltpu.VMEM((rows + spots, narrow), F32)] * 2,
@@ -1282,7 +1321,7 @@
     def valid_at(place):
         return ((place >= 0) & (place < DPC) & (place * frames < length)).astype(jnp.float32)
 
-    place = jnp.stack([chan_at & 1, chan_at]).astype(jnp.int32)
+    place = jnp.stack([chan_at & 1, chan_at, lax.axis_index("clip")]).astype(jnp.int32)
     own_ok = valid_at(clip_place)
     row_total = jnp.sum(frame_counts).astype(jnp.float32) * spot_count
     zero = jnp.zeros((), jnp.float32)
@@ -1300,7 +1339,6 @@
         for index in range(0, 8, 2)
     ]
     shards = lax.axis_size("chan")
-    first_low = whole_of(weight_first)
     tall = weight_middle.shape[0] * weight_middle.shape[1]
     packed = jnp.concatenate(
         [
@@ -1328,7 +1366,13 @@
     cells = features.reshape(row_count, model_width)
     cot = cotangent.reshape(row_count, model_width)
     before, after = beside(features, spot_count)
-    pre_one, sums_one = first_conv(flags, cells, before, after, first_low)
+    if shards == 8 and lax.axis_size("clip") == 4:
+        pre_one, sums_one, first_low = first_conv_parts(
+            place, flags, cells, before, after, *quarters_of(weight_first)
+        )
+    else:
+        first_low = whole_of(weight_first)
+        pre_one, sums_one = first_conv(flags, cells, before, after, first_low)
     sums_one = total(sums_one)
     pre_two, sums_two = middle_conv(
         flags, pre_one, sums_one, gains_one, middle_low, edges

time: 601 us -> 582 us (0.968)
  waiting for transfers between devices: 298 us -> 254 us
  starting transfers between devices: 105 us -> 118 us
  Pallas kernels: 89.5 us -> 101 us
    all_gather x1, waiting for transfers between devices: 26.6 us -> 0.01 us  [body(): lax.all_gather(weight_back.astype(LOW), 'chan', axis=0, tiled=True)]
    all_gather x1 -> x0, waiting for transfers between devices: 18.9 us -> none  [whole_of(): lax.all_gather(shard.astype(jnp.bfloat16), 'chan', axis=0, tiled=False)]
    ppermute x78 -> x85, waiting for transfers between devices: 225 us -> 243 us  [flipped(): return lax.ppermute(value, axis, pairs)]
    ppermute x78 -> x85, starting transfers between devices: 98.3 us -> 110 us  [flipped(): return lax.ppermute(value, axis, pairs)]
    pallas_call x24, Pallas kernels: 89.5 us -> 101 us  [call(): pl.pallas_call(kernel, out_shape=shapes, in_specs=spaces, out_specs=out_s...]
    all_gather x1, waiting for transfers between devices: 7.78 us -> 0.01 us  [body(): packed = lax.all_gather(packed, 'chan', axis=0, tiled=False)]
    psum x1, waiting for transfers between devices: 13.5 us -> 7.32 us  [body(): early = lax.psum(early, 'chan', axis_index_groups=groups)]
    unnamed x191 -> x193, local copies, waits for them, and re-layouts: 39.5 us -> 42.9 us
  transfers between devices with their start and end apart: 89 -> 95, of which waited for: 54 -> 52; matrix products, arithmetic and copies ran while one was open for 6% -> 6% of each run, Pallas kernels for 11% -> 13%
where the time goes in v1:
time: 582 us; the launch traced here: 574 us
  waiting for transfers between devices  254 us (44%)
  starting transfers between devices  118 us (20%)
  Pallas kernels  101 us (17%)
  local copies, waits for them, and re-layouts  68.5 us (12%)
  between operations  21.3 us (4%)
  other arithmetic  11.2 us (2%)
    ppermute x85, waiting for transfers between devices, flipped(): return lax.ppermute(value, axis, pairs)  243 us
    ppermute x85, starting transfers between devices, flipped(): return lax.ppermute(value, axis, pairs)  110 us
    pallas_call x24, Pallas kernels, call(): pl.pallas_call(kernel, out_shape=shapes, in_specs=spaces, out_specs=out_s...  101 us
    unnamed x193, local copies, waits for them, and re-layouts  42.9 us
  transfers between devices with their start and end apart: 95, of which 52 were waited for; matrix products, arithmetic and copies ran while one was open for 6% of the time, Pallas kernels for 13%

profile of v1, /device:TPU:0, one launch (start us, length us, event | category | flops | bytes accessed | tf_op | source)
XLA Modules:
  0.0 574.5 jit_solution(10914292221326737331)
XLA Ops:
  12.2 3.0 collective-permute-start.2
  15.2 2.6 collective-permute-start.3
  17.8 3.3 collective-permute-done.3
  21.1 2.6 collective-permute-done.4
  27.3 3.9 collective-permute-done.5
  31.2 3.4 collective-permute-done.6
  38.5 3.2 collective-permute-start
  48.8 3.1 shard_map.421
  57.5 3.3 collective-permute-start.12
  70.6 2.2 shard_map.422
  74.3 3.8 collective-permute-start.18
  79.6 3.8 collective-permute-done.19
  93.9 3.4 collective-permute-start.26
  103.5 3.1 copy.71
  113.6 5.8 %shard_map.424 = (bf16[784,1024]{1,0:T(8,128)(2,1)S(1)}, bf16[784,512]{1,0:T(8,128)(2,1)}, bf16[784,1024]{1,0:T(8,128)(2,1)}) custom-call(f32[8]{0:T(128)S(1)} %stack.47.flags, bf16[784,256]{1,0:T(8,128)(2,1)S(1)} %copy-done.63, bf16[784,1024]{1,0:T(8,128)(2,1)S(1)} %reshape.184.cells, bf16[256,1024]{1,0:T(8,128)(2,1)S(1)} %bitcast.80, ...), custom_call_target="tpu_custom_call" | custom-call | flops 7000000000 | tf_op jit(solution)/shard_map/pallas_call | solution.py:208
  120.7 3.8 collective-permute-start.31
  124.5 46.1 %collective-permute-done.31.query = bf16[784,512]{1,0:T(8,128)(2,1)} collective-permute-done((bf16[784,512]{1,0:T(8,128)(2,1)}, bf16[784,512]{1,0:T(8,128)(2,1)}, u32[]{:S(2)}, u32[]{:S(2)}) %collective-permute-start.31) | collective-permute-done | bytes 802848 | tf_op jit(solution)/shard_map/ppermute | solution.py:33
  176.5 4.0 shard_map.426
  183.6 10.6 %shard_map.425 = (bf16[784,512]{1,0:T(8,128)(2,1)S(1)}, f32[784,128]{1,0:T(8,128)S(1)}) custom-call(s32[1]{0:T(128)} %bitcast.19.count, bf16[784,512]{1,0:T(8,128)(2,1)} %get-tuple-element.124.query, bf16[784,1024]{1,0:T(8,128)(2,1)} %get-tuple-element.125.one.refs_2_, bf16[784,1024]{1,0:T(8,128)(2,1)} %collective-permute-done.30.two.refs_3_, ...), custom_call_target="tpu_custom_call" | custom-call | flops 10000000000 | tf_op jit(solution)/shard_map/pallas_call | solution.py:208
  194.2 25.7 %collective-permute-done.35.far_log = f32[8,896]{1,0:T(8,128)S(1)} collective-permute-done((f32[8,896]{1,0:T(8,128)S(1)}, f32[8,896]{1,0:T(8,128)S(1)}, u32[]{:S(2)}, u32[]{:S(2)}) %collective-permute-start.35) | collective-permute-done | bytes 28704 | tf_op jit(solution)/shard_map/ppermute | solution.py:33
  219.9 2.5 shard_map.427
  225.3 2.9 collective-permute-start.38
  230.2 3.7 collective-permute-done.39
  233.9 7.5 %collective-permute-start.40 = (f32[5,1024]{1,0:T(8,128)S(1)}, f32[5,1024]{1,0:T(8,128)S(1)}, u32[]{:S(2)}, u32[]{:S(2)}) collective-permute-start(f32[5,1024]{1,0:T(8,128)S(1)} %add_add_fusion.1), channel_id=1, source_target_pairs={{0,8},{8,0},{16,24},{24,16},{1,9},{9,1},{17,25},{25,17},{2,10},{10... | collective-permute-start | bytes 61448 | tf_op jit(solution)/shard_map/ppermute | solution.py:33
  253.4 4.0 shard_map.428
  257.5 2.9 collective-permute-start.44
  260.4 19.5 %shard_map.429 = (f32[784,512]{1,0:T(8,128)S(1)}, bf16[784,1024]{1,0:T(8,128)(2,1)S(1)}, bf16[784,1024]{1,0:T(8,128)(2,1)S(1)}, bf16[784,1024]{1,0:T(8,128)(2,1)S(1)}, bf16[784,1024]{1,0:T(8,128)(2,1)S(1)}) custom-call(s32[1]{0:T(128)} %bitcast.19.count, bf16[784,512]{1,0:T(8,128)(2,1)} %get-tuple-element.124.query, ...), custom_call_target="tpu_custom_call" | custom-call | flops 16999999488 | tf_op jit(solution)/shard_map/pallas_call | solution.py:208
  283.3 9.1 %collective-permute-done.44.refs_0_ = f32[8,896]{1,0:T(8,128)S(1)} collective-permute-done((f32[8,896]{1,0:T(8,128)S(1)}, f32[8,896]{1,0:T(8,128)S(1)}, u32[]{:S(2)}, u32[]{:S(2)}) %collective-permute-start.44) | collective-permute-done | bytes 28704 | tf_op jit(solution)/shard_map/ppermute | solution.py:33
  292.4 3.4 shard_map.430
  295.9 3.4 collective-permute-done.45
  301.9 4.4 shard_map.431
  306.3 2.2 collective-permute-start.46
  309.6 44.0 %collective-permute-done.46.query_far = bf16[784,512]{1,0:T(8,128)(2,1)S(1)} collective-permute-done((bf16[784,512]{1,0:T(8,128)(2,1)S(1)}, bf16[784,512]{1,0:T(8,128)(2,1)S(1)}, u32[]{:S(2)}, u32[]{:S(2)}) %collective-permute-start.46) | collective-permute-done | bytes 802848 | tf_op jit(solution)/shard_map/ppermute | solution.py:33
  353.7 2.2 collective-permute-done.49.far
  357.3 5.2 shard_map.432
  369.5 2.6 collective-permute-done.53
  372.1 8.6 %collective-permute-start.54 = (f32[3,1024]{1,0:T(4,128)S(1)}, f32[3,1024]{1,0:T(4,128)S(1)}, u32[]{:S(2)}, u32[]{:S(2)}) collective-permute-start(f32[3,1024]{1,0:T(4,128)S(1)} %add_add_fusion.3), channel_id=1, source_target_pairs={{0,8},{8,0},{16,24},{24,16},{1,9},{9,1},{17,25},{25,17},{2,10},{10... | collective-permute-start | bytes 36872 | tf_op jit(solution)/shard_map/ppermute | solution.py:33
  382.3 5.7 shard_map.433
  388.8 2.2 shard_map.435
  392.4 2.3 collective-permute-start.60
  394.7 2.1 collective-permute-start.61
  396.9 3.2 collective-permute-done.61
  407.6 2.5 shard_map.436
  412.9 2.7 collective-permute-start.67
  421.9 2.5 collective-permute-start.71
  431.7 3.3 shard_map.438.middle
  435.0 3.9 shard_map.440
  442.3 3.3 collective-permute-done.74.arrived
  452.5 2.1 collective-permute-start.77
  454.9 8.8 %collective-permute-done.75 = bf16[800,256]{1,0:T(8,128)(2,1)} collective-permute-done((bf16[800,256]{1,0:T(8,128)(2,1)}, bf16[800,256]{1,0:T(8,128)(2,1)}, u32[]{:S(2)}, u32[]{:S(2)}) %collective-permute-start.75) | collective-permute-done | bytes 409632 | tf_op jit(solution)/shard_map/ppermute | solution.py:33
  463.7 8.7 %collective-permute-done.77 = bf16[800,256]{1,0:T(8,128)(2,1)} collective-permute-done((bf16[800,256]{1,0:T(8,128)(2,1)}, bf16[800,256]{1,0:T(8,128)(2,1)}, u32[]{:S(2)}, u32[]{:S(2)}) %collective-permute-start.77) | collective-permute-done | bytes 409632 | tf_op jit(solution)/shard_map/ppermute | solution.py:33
  475.8 3.2 collective-permute-start.79
  480.5 4.9 collective-permute-done.79
  485.4 4.8 collective-permute-done.80
  491.2 7.3 %all-reduce.2.cloned.1.call-done = bf16[1024,256]{1,0:T(8,128)(2,1)} async-done(((bf16[1024,256]{1,0:T(8,128)(2,1)}), bf16[1024,256]{1,0:T(8,128)(2,1)}) %all-reduce.2.cloned.1.call-update) | async-done | bytes 524304 | tf_op jit(solution)/shard_map/psum | solution.py:1460
  498.9 2.3 collective-permute-start.82
  505.6 3.4 collective-permute-done.82
  511.3 2.4 copy.74
  519.9 2.4 copy.75
  526.8 14.3 %collective-permute-done.86 = bf16[800,256]{1,0:T(8,128)(2,1)S(1)} collective-permute-done((bf16[800,256]{1,0:T(8,128)(2,1)}, bf16[800,256]{1,0:T(8,128)(2,1)S(1)}, u32[]{:S(2)}, u32[]{:S(2)}) %collective-permute-start.86) | collective-permute-done | bytes 409632 | tf_op jit(solution)/shard_map/ppermute | solution.py:33
  541.1 3.9 all-gather.11.cloned.1.call-done.half
  546.3 4.7 collective-permute-done.88.other
  552.8 6.4 %shard_map.443 = (f32[3,1024,512]{2,1,0:T(8,128)}, f32[512,1024]{1,0:T(8,128)}, f32[3,128,512]{2,1,0:T(8,128)S(1)}, f32[64,1024]{1,0:T(8,128)S(1)}, f32[8,256]{1,0:T(8,128)S(1)}) custom-call(s32[3]{0:T(128)S(1)} %copy-done.23, f32[8]{0:T(128)S(1)} %copy-done.26, bf16[4096,256]{1,0:T(8,128)(2,1)S(1)} %copy-done.29, ...), custom_call_target="tpu_custom_call" | custom-call | flops 6000000000 | tf_op jit(solution)/shard_map/pallas_call | solution.py:208
  559.3 6.1 %shard_map.444 = (f32[3,1024,256]{2,1,0:T(8,128)}, f32[9,256,256]{2,1,0:T(8,128)}, f32[256,1024]{1,0:T(8,128)}, f32[2,128]{1,0:T(2,128)S(1)}, f32[3,128,256]{2,1...) custom-call(s32[3]{0:T(128)S(1)} %copy-done.23, ...), custom_call_target="tpu_custom_call" | custom-call | flops 8000000000 | tf_op jit(solution)/shard_map/pallas_call | solution.py:208
  (427 shorter events, 164.8 us)
Async XLA Ops:
  7.2 61.9 %all-gather.5.cloned.1.call-start = ((), (), s32[]{:S(2)}) async-start(), calls=%async_computation.1 | async-start | bytes 1916928 | tf_op jit(solution)/shard_map/all_gather | solution.py:1349
  10.0 99.7 %all-gather.7.cloned.1.call-start = ((), (), s32[]{:S(2)}) async-start(), calls=%async_computation.2 | async-start | bytes 3538944 | tf_op jit(solution)/shard_map/all_gather | solution.py:1357
  11.2 113.3 %all-gather.9.cloned.1.call-start = ((), (), s32[]{:S(2)}) async-start(), calls=%async_computation.3 | async-start | bytes 1179648 | tf_op jit(solution)/shard_map/all_gather | solution.py:1358
  12.2 5.6 collective-permute-start.2
  15.2 5.9 %collective-permute-start.3 = (bf16[1,3,32,256]{3,2,1,0:T(8,128)(2,1)S(1)}, bf16[1,3,32,256]{3,2,1,0:T(8,128)(2,1)S(1)}, u32[]{:S(2)}, u32[]{:S(2)}) collective-permute-start(bf16[1,3,32,256]{3,2,1,0:T(8,128)(2,1)S(1)} %fusion), channel_id=1, source_target_pairs={{0,4},{1,5},{2,6},{3,7},{4,0},{5,1},{6,2},{7,3},{8,12},{9,13},{10,... | collective-permute-start | bytes 147464 | tf_op jit(solution)/shard_map/ppermute | solution.py:33
  17.8 5.9 %collective-permute-start.4 = (bf16[1,3,32,256]{3,2,1,0:T(8,128)(2,1)S(1)}, bf16[1,3,32,256]{3,2,1,0:T(8,128)(2,1)S(1)}, u32[]{:S(2)}, u32[]{:S(2)}) collective-permute-start(bf16[1,3,32,256]{3,2,1,0:T(8,128)(2,1)S(1)} %fusion), channel_id=1, source_target_pairs={{0,6},{1,7},{2,4},{3,5},{4,2},{5,3},{6,0},{7,1},{8,14},{9,15},{10,... | collective-permute-start | bytes 147464 | tf_op jit(solution)/shard_map/ppermute | solution.py:33
  23.8 7.4 %collective-permute-start.5 = (bf16[1,4,3,32,256]{4,3,2,1,0:T(8,128)(2,1)S(1)}, bf16[1,4,3,32,256]{4,3,2,1,0:T(8,128)(2,1)S(1)}, u32[]{:S(2)}, u32[]{:S(2)}) collective-permute-start(bf16[1,4,3,32,256]{4,3,2,1,0:T(8,128)(2,1)S(1)} %maximum_bitcast_fusion), channel_id=1, source_target_pairs={{0,8},{8,0},{16,24},{24,16},{1,9},{9,1},{17,25},{25,17},{2,10},{10... | collective-permute-start | bytes 589832 | tf_op jit(solution)/shard_map/ppermute | solution.py:33
  25.4 9.2 %collective-permute-start.6 = (bf16[1,4,3,32,256]{4,3,2,1,0:T(8,128)(2,1)S(1)}, bf16[1,4,3,32,256]{4,3,2,1,0:T(8,128)(2,1)S(1)}, u32[]{:S(2)}, u32[]{:S(2)}) collective-permute-start(bf16[1,4,3,32,256]{4,3,2,1,0:T(8,128)(2,1)S(1)} %maximum_bitcast_fusion), channel_id=1, source_target_pairs={{0,16},{8,24},{16,0},{24,8},{1,17},{9,25},{17,1},{25,9},{2,18},{10... | collective-permute-start | bytes 589832 | tf_op jit(solution)/shard_map/ppermute | solution.py:33
  26.9 7.7 %collective-permute-start.7 = (bf16[1,4,3,32,256]{4,3,2,1,0:T(8,128)(2,1)S(1)}, bf16[1,4,3,32,256]{4,3,2,1,0:T(8,128)(2,1)S(1)}, u32[]{:S(2)}, u32[]{:S(2)}) collective-permute-start(bf16[1,4,3,32,256]{4,3,2,1,0:T(8,128)(2,1)S(1)} %maximum_bitcast_fusion), channel_id=1, source_target_pairs={{0,24},{8,16},{16,8},{24,0},{1,25},{9,17},{17,9},{25,1},{2,26},{10... | collective-permute-start | bytes 589832 | tf_op jit(solution)/shard_map/ppermute | solution.py:33
  34.7 14.1 %collective-permute-start.8 = (bf16[4,4,3,32,256]{4,3,2,1,0:T(8,128)(2,1)S(1)}, bf16[4,4,3,32,256]{4,3,2,1,0:T(8,128)(2,1)S(1)}, u32[]{:S(2)}, u32[]{:S(2)}) collective-permute-start(bf16[4,4,3,32,256]{4,3,2,1,0:T(8,128)(2,1)S(1)} %pad_maximum_fusion.mine), channel_id=1, source_target_pairs={{0,1},{1,0},{2,3},{3,2},{4,5},{5,4},{6,7},{7,6},{8,9},{9,8},{10,11... | collective-permute-start | bytes 2359304 | tf_op jit(solution)/shard_map/ppermute | solution.py:33
  38.5 10.3 %collective-permute-start = (bf16[1,196,1024]{2,1,0:T(8,128)(2,1)}, bf16[1,196,1024]{2,1,0:T(8,128)(2,1)}, u32[]{:S(2)}, u32[]{:S(2)}) collective-permute-start(bf16[1,196,1024]{2,1,0:T(8,128)(2,1)} %get-tuple-element.214), channel_id=1, source_target_pairs={{0,1},{1,2},{2,3},{3,4},{4,5},{5,6},{6,7},{8,9},{9,10},{10,11},{11... | collective-permute-start | bytes 1204232 | tf_op jit(solution)/shard_map/ppermute | solution.py:61
  41.7 7.1 %collective-permute-start.1 = (bf16[1,196,1024]{2,1,0:T(8,128)(2,1)}, bf16[1,196,1024]{2,1,0:T(8,128)(2,1)}, u32[]{:S(2)}, u32[]{:S(2)}) collective-permute-start(bf16[1,196,1024]{2,1,0:T(8,128)(2,1)} %get-tuple-element.213), channel_id=1, source_target_pairs={{1,0},{2,1},{3,2},{4,3},{5,4},{6,5},{7,6},{9,8},{10,9},{11,10},{12... | collective-permute-start | bytes 1204232 | tf_op jit(solution)/shard_map/ppermute | solution.py:62
  57.5 5.4 collective-permute-start.12
  74.3 5.4 collective-permute-start.18
  78.0 5.4 collective-permute-start.19
  92.9 5.3 collective-permute-start.24
  92.9 5.3 collective-permute-start.25
  93.9 5.4 collective-permute-start.26
  98.0 356.6 %reduce-scatter.2.cloned.1.call-start = ((), (), s32[]{:S(2)}) async-start(), calls=%async_computation.4 | async-start | bytes 2621440 | tf_op jit(solution)/shard_map/reduce_scatter | solution.py:1459
  99.4 8.8 %collective-permute-start.27 = (f32[2,1024]{1,0:T(2,128)S(1)}, f32[2,1024]{1,0:T(2,128)S(1)}, u32[]{:S(2)}, u32[]{:S(2)}) collective-permute-start(f32[2,1024]{1,0:T(2,128)S(1)} %add_add_fusion.5), channel_id=1, source_target_pairs={{0,8},{8,0},{16,24},{24,16},{1,9},{9,1},{17,25},{25,17},{2,10},{10... | collective-permute-start | bytes 24584 | tf_op jit(solution)/shard_map/ppermute | solution.py:33
  100.5 7.8 %collective-permute-start.28 = (f32[2,1024]{1,0:T(2,128)S(1)}, f32[2,1024]{1,0:T(2,128)}, u32[]{:S(2)}, u32[]{:S(2)}) collective-permute-start(f32[2,1024]{1,0:T(2,128)S(1)} %add_add_fusion.5), channel_id=1, source_target_pairs={{0,16},{8,24},{16,0},{24,8},{1,17},{9,25},{17,1},{25,9},{2,18},{10... | collective-permute-start | bytes 24584 | tf_op jit(solution)/shard_map/ppermute | solution.py:33
  101.1 7.7 %collective-permute-start.29 = (f32[2,1024]{1,0:T(2,128)S(1)}, f32[2,1024]{1,0:T(2,128)}, u32[]{:S(2)}, u32[]{:S(2)}) collective-permute-start(f32[2,1024]{1,0:T(2,128)S(1)} %add_add_fusion.5), channel_id=1, source_target_pairs={{0,24},{8,16},{16,8},{24,0},{1,25},{9,17},{17,9},{25,1},{2,26},{10... | collective-permute-start | bytes 24584 | tf_op jit(solution)/shard_map/ppermute | solution.py:33
  120.6 52.2 %collective-permute-start.32 = (bf16[784,1024]{1,0:T(8,128)(2,1)}, bf16[784,1024]{1,0:T(8,128)(2,1)}, u32[]{:S(2)}, u32[]{:S(2)}) collective-permute-start(bf16[784,1024]{1,0:T(8,128)(2,1)} %get-tuple-element.125.one.refs_2_), channel_id=1, source_target_pairs={{0,2},{1,3},{2,0},{3,1},{4,6},{5,7},{6,4},{7,5},{8,10},{9,11},{10,... | collective-permute-start | bytes 4816904 | tf_op jit(solution)/shard_map/ppermute | solution.py:33
  120.7 49.9 %collective-permute-start.31 = (bf16[784,512]{1,0:T(8,128)(2,1)}, bf16[784,512]{1,0:T(8,128)(2,1)}, u32[]{:S(2)}, u32[]{:S(2)}) collective-permute-start(bf16[784,512]{1,0:T(8,128)(2,1)} %get-tuple-element.124.query), channel_id=1, source_target_pairs={{0,4},{1,5},{2,6},{3,7},{4,0},{5,1},{6,2},{7,3},{8,12},{9,13},{10,... | collective-permute-start | bytes 2408456 | tf_op jit(solution)/shard_map/ppermute | solution.py:33
  124.5 50.2 %collective-permute-start.30 = (bf16[784,1024]{1,0:T(8,128)(2,1)}, bf16[784,1024]{1,0:T(8,128)(2,1)}, u32[]{:S(2)}, u32[]{:S(2)}) collective-permute-start(bf16[784,1024]{1,0:T(8,128)(2,1)} %get-tuple-element.125.one.refs_2_), channel_id=1, source_target_pairs={{0,1},{1,0},{2,3},{3,2},{4,5},{5,4},{6,7},{7,6},{8,9},{9,8},{10,11... | collective-permute-start | bytes 4816904 | tf_op jit(solution)/shard_map/ppermute | solution.py:33
  180.6 39.3 %collective-permute-start.34 = (bf16[784,512]{1,0:T(8,128)(2,1)S(1)}, bf16[784,512]{1,0:T(8,128)(2,1)S(1)}, u32[]{:S(2)}, u32[]{:S(2)}) collective-permute-start(bf16[784,512]{1,0:T(8,128)(2,1)S(1)} %get-tuple-element.130), channel_id=1, source_target_pairs={{0,4},{1,5},{2,6},{3,7},{4,0},{5,1},{6,2},{7,3},{8,12},{9,13},{10,... | collective-permute-start | bytes 2408456 | tf_op jit(solution)/shard_map/ppermute | solution.py:33
  182.1 37.8 %collective-permute-start.35 = (f32[8,896]{1,0:T(8,128)S(1)}, f32[8,896]{1,0:T(8,128)S(1)}, u32[]{:S(2)}, u32[]{:S(2)}) collective-permute-start(f32[8,896]{1,0:T(8,128)S(1)} %get-tuple-element.131), channel_id=1, source_target_pairs={{0,4},{1,5},{2,6},{3,7},{4,0},{5,1},{6,2},{7,3},{8,12},{9,13},{10,... | collective-permute-start | bytes 86024 | tf_op jit(solution)/shard_map/ppermute | solution.py:33
  228.2 5.7 collective-permute-start.39
  233.9 9.8 %collective-permute-start.40 = (f32[5,1024]{1,0:T(8,128)S(1)}, f32[5,1024]{1,0:T(8,128)S(1)}, u32[]{:S(2)}, u32[]{:S(2)}) collective-permute-start(f32[5,1024]{1,0:T(8,128)S(1)} %add_add_fusion.1), channel_id=1, source_target_pairs={{0,8},{8,0},{16,24},{24,16},{1,9},{9,1},{17,25},{25,17},{2,10},{10... | collective-permute-start | bytes 61448 | tf_op jit(solution)/shard_map/ppermute | solution.py:33
  257.4 35.0 %collective-permute-start.43 = (bf16[784,512]{1,0:T(8,128)(2,1)S(1)}, bf16[784,512]{1,0:T(8,128)(2,1)S(1)}, u32[]{:S(2)}, u32[]{:S(2)}) collective-permute-start(bf16[784,512]{1,0:T(8,128)(2,1)S(1)} %get-tuple-element.137.grad), channel_id=1, source_target_pairs={{0,4},{1,5},{2,6},{3,7},{4,0},{5,1},{6,2},{7,3},{8,12},{9,13},{10,... | collective-permute-start | bytes 2408456 | tf_op jit(solution)/shard_map/ppermute | solution.py:33
  257.5 34.9 %collective-permute-start.44 = (f32[8,896]{1,0:T(8,128)S(1)}, f32[8,896]{1,0:T(8,128)S(1)}, u32[]{:S(2)}, u32[]{:S(2)}) collective-permute-start(f32[8,896]{1,0:T(8,128)S(1)} %get-tuple-element.140), channel_id=1, source_target_pairs={{0,4},{1,5},{2,6},{3,7},{4,0},{5,1},{6,2},{7,3},{8,12},{9,13},{10,... | collective-permute-start | bytes 86024 | tf_op jit(solution)/shard_map/ppermute | solution.py:33
  301.3 54.6 %collective-permute-start.49 = (bf16[784,1024]{1,0:T(8,128)(2,1)}, bf16[784,1024]{1,0:T(8,128)(2,1)S(1)}, u32[]{:S(2)}, u32[]{:S(2)}) collective-permute-start(bf16[784,1024]{1,0:T(8,128)(2,1)} %add_convert_fusion), channel_id=1, source_target_pairs={{0,2},{1,3},{2,0},{3,1},{4,6},{5,7},{6,4},{7,5},{8,10},{9,11},{10,... | collective-permute-start | bytes 4816904 | tf_op jit(solution)/shard_map/ppermute | solution.py:33
  306.3 47.4 %collective-permute-start.46 = (bf16[784,512]{1,0:T(8,128)(2,1)S(1)}, bf16[784,512]{1,0:T(8,128)(2,1)S(1)}, u32[]{:S(2)}, u32[]{:S(2)}) collective-permute-start(bf16[784,512]{1,0:T(8,128)(2,1)S(1)} %get-tuple-element.149), channel_id=1, source_target_pairs={{0,4},{1,5},{2,6},{3,7},{4,0},{5,1},{6,2},{7,3},{8,12},{9,13},{10,... | collective-permute-start | bytes 2408456 | tf_op jit(solution)/shard_map/ppermute | solution.py:33
  308.5 45.2 %collective-permute-start.47 = (bf16[784,512]{1,0:T(8,128)(2,1)S(1)}, bf16[784,512]{1,0:T(8,128)(2,1)S(1)}, u32[]{:S(2)}, u32[]{:S(2)}) collective-permute-start(bf16[784,512]{1,0:T(8,128)(2,1)S(1)} %get-tuple-element.151), channel_id=1, source_target_pairs={{0,1},{1,0},{2,3},{3,2},{4,5},{5,4},{6,7},{7,6},{8,9},{9,8},{10,11... | collective-permute-start | bytes 2408456 | tf_op jit(solution)/shard_map/ppermute | solution.py:33
  308.5 45.2 %collective-permute-start.48 = (bf16[784,512]{1,0:T(8,128)(2,1)S(1)}, bf16[784,512]{1,0:T(8,128)(2,1)S(1)}, u32[]{:S(2)}, u32[]{:S(2)}) collective-permute-start(bf16[784,512]{1,0:T(8,128)(2,1)S(1)} %get-tuple-element.152), channel_id=1, source_target_pairs={{0,1},{1,0},{2,3},{3,2},{4,5},{5,4},{6,7},{7,6},{8,9},{9,8},{10,11... | collective-permute-start | bytes 2408456 | tf_op jit(solution)/shard_map/ppermute | solution.py:33
  366.6 5.5 collective-permute-start.53
  372.1 15.9 %collective-permute-start.54 = (f32[3,1024]{1,0:T(4,128)S(1)}, f32[3,1024]{1,0:T(4,128)S(1)}, u32[]{:S(2)}, u32[]{:S(2)}) collective-permute-start(f32[3,1024]{1,0:T(4,128)S(1)} %add_add_fusion.3), channel_id=1, source_target_pairs={{0,8},{8,0},{16,24},{24,16},{1,9},{9,1},{17,25},{25,17},{2,10},{10... | collective-permute-start | bytes 36872 | tf_op jit(solution)/shard_map/ppermute | solution.py:33
  380.7 7.3 %collective-permute-start.55 = (f32[3,1024]{1,0:T(4,128)S(1)}, f32[3,1024]{1,0:T(4,128)S(1)}, u32[]{:S(2)}, u32[]{:S(2)}) collective-permute-start(f32[3,1024]{1,0:T(4,128)S(1)} %add_add_fusion.3), channel_id=1, source_target_pairs={{0,16},{8,24},{16,0},{24,8},{1,17},{9,25},{17,1},{25,9},{2,18},{10... | collective-permute-start | bytes 36872 | tf_op jit(solution)/shard_map/ppermute | solution.py:33
  381.8 6.2 %collective-permute-start.56 = (f32[3,1024]{1,0:T(4,128)S(1)}, f32[3,1024]{1,0:T(4,128)S(1)}, u32[]{:S(2)}, u32[]{:S(2)}) collective-permute-start(f32[3,1024]{1,0:T(4,128)S(1)} %add_add_fusion.3), channel_id=1, source_target_pairs={{0,24},{8,16},{16,8},{24,0},{1,25},{9,17},{17,9},{25,1},{2,26},{10... | collective-permute-start | bytes 36872 | tf_op jit(solution)/shard_map/ppermute | solution.py:33
  388.0 29.3 %collective-permute-start.57 = (bf16[4096,256]{1,0:T(8,128)(2,1)S(1)}, bf16[4096,256]{1,0:T(8,128)(2,1)S(1)}, u32[]{:S(2)}, u32[]{:S(2)}) collective-permute-start(bf16[4096,256]{1,0:T(8,128)(2,1)S(1)} %get-tuple-element.161), channel_id=1, source_target_pairs={{0,1},{1,0},{2,3},{3,2},{4,5},{5,4},{6,7},{7,6},{8,9},{9,8},{10,11... | collective-permute-start | bytes 6291464 | tf_op jit(solution)/shard_map/ppermute | solution.py:33
  394.7 5.4 collective-permute-start.61
  412.9 6.3 %collective-permute-start.66 = (f32[2,256]{1,0:T(2,128)S(1)}, f32[2,256]{1,0:T(2,128)S(1)}, u32[]{:S(2)}, u32[]{:S(2)}) collective-permute-start(f32[2,256]{1,0:T(2,128)S(1)} %add.311), channel_id=1, source_target_pairs={{0,2},{1,3},{2,0},{3,1},{4,6},{5,7},{6,4},{7,5},{8,10},{9,11},{10,... | collective-permute-start | bytes 6152 | tf_op jit(solution)/shard_map/ppermute | solution.py:33
  412.9 6.3 %collective-permute-start.67 = (f32[2,256]{1,0:T(2,128)S(1)}, f32[2,256]{1,0:T(2,128)S(1)}, u32[]{:S(2)}, u32[]{:S(2)}) collective-permute-start(f32[2,256]{1,0:T(2,128)S(1)} %add.311), channel_id=1, source_target_pairs={{0,4},{1,5},{2,6},{3,7},{4,0},{5,1},{6,2},{7,3},{8,12},{9,13},{10,... | collective-permute-start | bytes 6152 | tf_op jit(solution)/shard_map/ppermute | solution.py:33
  415.5 5.4 collective-permute-start.68
  419.1 79.5 %all-reduce.2.cloned.1.call-start = ((), (), s32[]{:S(2)}) async-start(), calls=%async_computation.5 | async-start | bytes 1048576 | tf_op jit(solution)/shard_map/psum | solution.py:1460
  420.9 6.7 %collective-permute-start.69 = (f32[2,256]{1,0:T(2,128)S(1)}, f32[2,256]{1,0:T(2,128)S(1)}, u32[]{:S(2)}, u32[]{:S(2)}) collective-permute-start(f32[2,256]{1,0:T(2,128)S(1)} %add_add_fusion.7), channel_id=1, source_target_pairs={{0,8},{8,0},{16,24},{24,16},{1,9},{9,1},{17,25},{25,17},{2,10},{10... | collective-permute-start | bytes 6152 | tf_op jit(solution)/shard_map/ppermute | solution.py:33
  421.0 6.6 %collective-permute-start.70 = (f32[2,256]{1,0:T(2,128)S(1)}, f32[2,256]{1,0:T(2,128)S(1)}, u32[]{:S(2)}, u32[]{:S(2)}) collective-permute-start(f32[2,256]{1,0:T(2,128)S(1)} %add_add_fusion.7), channel_id=1, source_target_pairs={{0,16},{8,24},{16,0},{24,8},{1,17},{9,25},{17,1},{25,9},{2,18},{10... | collective-permute-start | bytes 6152 | tf_op jit(solution)/shard_map/ppermute | solution.py:33
  421.9 5.7 collective-permute-start.71
  429.0 5.9 %collective-permute-start.72 = (bf16[1,196,256]{2,1,0:T(8,128)(2,1)S(1)}, bf16[1,196,256]{2,1,0:T(8,128)(2,1)S(1)}, u32[]{:S(2)}, u32[]{:S(2)}) collective-permute-start(bf16[1,196,256]{2,1,0:T(8,128)(2,1)S(1)} %get-tuple-element.219), channel_id=1, source_target_pairs={{0,1},{1,2},{2,3},{3,4},{4,5},{5,6},{6,7},{8,9},{9,10},{10,11},{11... | collective-permute-start | bytes 301064 | tf_op jit(solution)/shard_map/ppermute | solution.py:61
  451.1 12.6 %collective-permute-start.75 = (bf16[800,256]{1,0:T(8,128)(2,1)}, bf16[800,256]{1,0:T(8,128)(2,1)}, u32[]{:S(2)}, u32[]{:S(2)}) collective-permute-start(bf16[800,256]{1,0:T(8,128)(2,1)} %get-tuple-element.210), channel_id=1, source_target_pairs={{0,8},{8,0},{16,24},{24,16},{1,9},{9,1},{17,25},{25,17},{2,10},{10... | collective-permute-start | bytes 1228808 | tf_op jit(solution)/shard_map/ppermute | solution.py:33
  451.3 12.4 %collective-permute-start.76 = (bf16[800,256]{1,0:T(8,128)(2,1)}, bf16[800,256]{1,0:T(8,128)(2,1)}, u32[]{:S(2)}, u32[]{:S(2)}) collective-permute-start(bf16[800,256]{1,0:T(8,128)(2,1)} %get-tuple-element.212), channel_id=1, source_target_pairs={{0,16},{8,24},{16,0},{24,8},{1,17},{9,25},{17,1},{25,9},{2,18},{10... | collective-permute-start | bytes 1228808 | tf_op jit(solution)/shard_map/ppermute | solution.py:33
  452.5 20.0 %collective-permute-start.77 = (bf16[800,256]{1,0:T(8,128)(2,1)}, bf16[800,256]{1,0:T(8,128)(2,1)}, u32[]{:S(2)}, u32[]{:S(2)}) collective-permute-start(bf16[800,256]{1,0:T(8,128)(2,1)} %get-tuple-element.211), channel_id=1, source_target_pairs={{0,24},{8,16},{16,8},{24,0},{1,25},{9,17},{17,9},{25,1},{2,26},{10... | collective-permute-start | bytes 1228808 | tf_op jit(solution)/shard_map/ppermute | solution.py:33
  454.6 90.4 %all-gather.11.cloned.1.call-start = ((), (), s32[]{:S(2)}) async-start(), calls=%async_computation.6 | async-start | bytes 2621440 | tf_op jit(solution)/shard_map/all_gather | solution.py:1464
  474.7 5.8 %collective-permute-start.78 = (bf16[200,256]{1,0:T(8,128)(2,1)S(1)}, bf16[200,256]{1,0:T(8,128)(2,1)S(1)}, u32[]{:S(2)}, u32[]{:S(2)}) collective-permute-start(bf16[200,256]{1,0:T(8,128)(2,1)S(1)} %get-tuple-element.215), channel_id=1, source_target_pairs={{0,2},{1,3},{2,0},{3,1},{4,6},{5,7},{6,4},{7,5},{8,10},{9,11},{10,... | collective-permute-start | bytes 307208 | tf_op jit(solution)/shard_map/ppermute | solution.py:33
  475.8 9.7 %collective-permute-start.79 = (bf16[200,256]{1,0:T(8,128)(2,1)S(1)}, bf16[200,256]{1,0:T(8,128)(2,1)S(1)}, u32[]{:S(2)}, u32[]{:S(2)}) collective-permute-start(bf16[200,256]{1,0:T(8,128)(2,1)S(1)} %get-tuple-element.217), channel_id=1, source_target_pairs={{0,4},{1,5},{2,6},{3,7},{4,0},{5,1},{6,2},{7,3},{8,12},{9,13},{10,... | collective-permute-start | bytes 307208 | tf_op jit(solution)/shard_map/ppermute | solution.py:33
  479.0 11.3 %collective-permute-start.80 = (bf16[200,256]{1,0:T(8,128)(2,1)S(1)}, bf16[200,256]{1,0:T(8,128)(2,1)S(1)}, u32[]{:S(2)}, u32[]{:S(2)}) collective-permute-start(bf16[200,256]{1,0:T(8,128)(2,1)S(1)} %get-tuple-element.216), channel_id=1, source_target_pairs={{0,6},{1,7},{2,4},{3,5},{4,2},{5,3},{6,0},{7,1},{8,14},{9,15},{10,... | collective-permute-start | bytes 307208 | tf_op jit(solution)/shard_map/ppermute | solution.py:33
  498.6 6.4 %collective-permute-start.81 = (bf16[200,256]{1,0:T(8,128)(2,1)S(1)}, bf16[200,256]{1,0:T(8,128)(2,1)S(1)}, u32[]{:S(2)}, u32[]{:S(2)}) collective-permute-start(bf16[200,256]{1,0:T(8,128)(2,1)S(1)} %add_convert_fusion.2), channel_id=1, source_target_pairs={{0,2},{1,3},{2,0},{3,1},{4,6},{5,7},{6,4},{7,5},{8,10},{9,11},{10,... | collective-permute-start | bytes 307208 | tf_op jit(solution)/shard_map/ppermute | solution.py:33
  498.9 10.1 %collective-permute-start.82 = (bf16[200,256]{1,0:T(8,128)(2,1)S(1)}, bf16[200,256]{1,0:T(8,128)(2,1)S(1)}, u32[]{:S(2)}, u32[]{:S(2)}) collective-permute-start(bf16[200,256]{1,0:T(8,128)(2,1)S(1)} %add_convert_fusion.2), channel_id=1, source_target_pairs={{0,4},{1,5},{2,6},{3,7},{4,0},{5,1},{6,2},{7,3},{8,12},{9,13},{10,... | collective-permute-start | bytes 307208 | tf_op jit(solution)/shard_map/ppermute | solution.py:33
  501.2 8.4 %collective-permute-start.83 = (bf16[200,256]{1,0:T(8,128)(2,1)S(1)}, bf16[200,256]{1,0:T(8,128)(2,1)S(1)}, u32[]{:S(2)}, u32[]{:S(2)}) collective-permute-start(bf16[200,256]{1,0:T(8,128)(2,1)S(1)} %add_convert_fusion.2), channel_id=1, source_target_pairs={{0,6},{1,7},{2,4},{3,5},{4,2},{5,3},{6,0},{7,1},{8,14},{9,15},{10,... | collective-permute-start | bytes 307208 | tf_op jit(solution)/shard_map/ppermute | solution.py:33
  510.3 14.3 %collective-permute-start.84 = (bf16[800,256]{1,0:T(8,128)(2,1)}, bf16[800,256]{1,0:T(8,128)(2,1)}, u32[]{:S(2)}, u32[]{:S(2)}) collective-permute-start(bf16[800,256]{1,0:T(8,128)(2,1)} %bitcast.30), channel_id=1, source_target_pairs={{0,8},{8,0},{16,24},{24,16},{1,9},{9,1},{17,25},{25,17},{2,10},{10... | collective-permute-start | bytes 1228808 | tf_op jit(solution)/shard_map/ppermute | solution.py:33
  513.7 12.1 %collective-permute-start.85 = (bf16[800,256]{1,0:T(8,128)(2,1)}, bf16[800,256]{1,0:T(8,128)(2,1)}, u32[]{:S(2)}, u32[]{:S(2)}) collective-permute-start(bf16[800,256]{1,0:T(8,128)(2,1)} %bitcast.30), channel_id=1, source_target_pairs={{0,16},{8,24},{16,0},{24,8},{1,17},{9,25},{17,1},{25,9},{2,18},{10... | collective-permute-start | bytes 1228808 | tf_op jit(solution)/shard_map/ppermute | solution.py:33
  522.3 18.8 %collective-permute-start.86 = (bf16[800,256]{1,0:T(8,128)(2,1)}, bf16[800,256]{1,0:T(8,128)(2,1)S(1)}, u32[]{:S(2)}, u32[]{:S(2)}) collective-permute-start(bf16[800,256]{1,0:T(8,128)(2,1)} %bitcast.30), channel_id=1, source_target_pairs={{0,24},{8,16},{16,8},{24,0},{1,25},{9,17},{17,9},{25,1},{2,26},{10... | collective-permute-start | bytes 1228808 | tf_op jit(solution)/shard_map/ppermute | solution.py:33
  545.0 6.0 %collective-permute-start.88 = (bf16[4096,256]{1,0:T(8,128)(2,1)}, bf16[4096,256]{1,0:T(8,128)(2,1)}, u32[]{:S(2)}, u32[]{:S(2)}) collective-permute-start(bf16[4096,256]{1,0:T(8,128)(2,1)} %all-gather.11.cloned.1.call-done.half), channel_id=1, source_target_pairs={{0,1},{1,0},{2,3},{3,2},{4,5},{5,4},{6,7},{7,6},{8,9},{9,8},{10,11... | collective-permute-start | bytes 6291464 | tf_op jit(solution)/shard_map/ppermute | solution.py:33
  545.1 14.0 %collective-permute-start.87 = (bf16[3200,256]{1,0:T(8,128)(2,1)S(1)}, bf16[3200,256]{1,0:T(8,128)(2,1)S(1)}, u32[]{:S(2)}, u32[]{:S(2)}) collective-permute-start(bf16[3200,256]{1,0:T(8,128)(2,1)S(1)} %bitcast.74), channel_id=1, source_target_pairs={{0,1},{1,0},{2,3},{3,2},{4,5},{5,4},{6,7},{7,6},{8,9},{9,8},{10,11... | collective-permute-start | bytes 4915208 | tf_op jit(solution)/shard_map/ppermute | solution.py:33
  (123 other events, 1671.9 us)
Sparse Core Ops, SparseCore 0:
  10.3 28.6 all-gather.4
  41.2 37.9 all-gather.6
  98.1 19.1 all-gather.8
  419.2 33.4 reduce-scatter.1
  455.0 43.5 all-reduce.1
  500.4 44.5 all-gather.10

commit v2 on v1

--- a/solution.py
+++ b/solution.py
@@ -63,18 +63,17 @@
     )
 
 
-def total(value):
-    for axis in ("chan", "clip"):
-        bits = lax.axis_size(axis).bit_length() - 1
-        levels = list(range(bits))
-        groups = [levels[:1]] if axis == "chan" else []
-        rest = levels[len(groups) :]
-        groups += [rest[index : index + 2] for index in range(0, len(rest), 2)]
-        for group in groups:
-            base = 1 << group[0]
-            parts = [flipped(value, axis, base * turn) for turn in range(1, 1 << len(group))]
-            value = value + sum(parts[1:], parts[0])
-    return value
+def total(value, beside=()):
+    steps = [("chan", group) for group in level_groups("chan")]
+    steps += [("clip", group) for group in level_groups("clip")]
+    for index, (axis, group) in enumerate(steps):
+        base = 1 << group[0]
+        parts = [flipped(value, axis, base * turn) for turn in range(1, 1 << len(group))]
+        if beside and index == len(steps) - 1:
+            tie = lax.optimization_barrier((parts, list(beside)))
+            parts, beside = tie
+        value = value + sum(parts[1:], parts[0])
+    return (value, *beside) if beside else value
 
 
 def level_groups(axis):
@@ -1379,7 +1378,7 @@
     )
     sums_two = total(sums_two)
     act_two, sums_three = last_conv(flags, pre_two, sums_two, gains_two, last_low)
-    sums_three, cot = tied(total(sums_three), cot)
+    sums_three, cot = total(sums_three, (cot,))
     residual_low, query, pair_own = embed_rows(
         flags, act_two, cells, last_low, sums_three, gains_three, embed_low
     )
@@ -1421,8 +1420,7 @@
     early = early_weight(
         place, flags, residual_low, projected_grad, attended, sums_four[4:5, :inner_width], attn_grad
     )
-    back_three = total(jnp.concatenate([back_three, norm_four[2:3]]))
-    early, back_three = tied(early, back_three)
+    back_three, *early = total(jnp.concatenate([back_three, norm_four[2:3]]), early)
     last_grad, two_grad, back_two = last_back(
         flags, pre_grad, act_two, last_low, sums_three, gains_three, back_three, pre_two, sums_two,
         gains_two,

time: 582 us -> 575 us (0.988)
  Pallas kernels: 101 us -> 124 us
  waiting for transfers between devices: 254 us -> 235 us
  starting transfers between devices: 118 us -> 107 us
    pallas_call x24, Pallas kernels: 101 us -> 124 us  [call(): pl.pallas_call(kernel, out_shape=shapes, in_specs=spaces, out_specs=out_s...]
    ppermute x85, waiting for transfers between devices: 243 us -> 231 us  [flipped(): return lax.ppermute(value, axis, pairs)]
    ppermute x85, starting transfers between devices: 110 us -> 99.6 us  [flipped(): return lax.ppermute(value, axis, pairs)]
    psum x1, waiting for transfers between devices: 7.32 us -> 0.02 us  [body(): early = lax.psum(early, 'chan', axis_index_groups=groups)]
  transfers between devices with their start and end apart: 95 -> 95, of which waited for: 52 -> 56; matrix products, arithmetic and copies ran while one was open for 6% -> 6% of each run, Pallas kernels for 13% -> 15%
where the time goes in v2:
time: 575 us; the launch traced here: 567 us
  waiting for transfers between devices  235 us (41%)
  Pallas kernels  124 us (22%)
  starting transfers between devices  107 us (19%)
  local copies, waits for them, and re-layouts  68.7 us (12%)
  between operations  21.3 us (4%)
  other arithmetic  11.2 us (2%)
    ppermute x85, waiting for transfers between devices, flipped(): return lax.ppermute(value, axis, pairs)  231 us
    pallas_call x24, Pallas kernels, call(): pl.pallas_call(kernel, out_shape=shapes, in_specs=spaces, out_specs=out_s...  124 us
    ppermute x85, starting transfers between devices, flipped(): return lax.ppermute(value, axis, pairs)  99.6 us
    unnamed x193, local copies, waits for them, and re-layouts  43.2 us
  transfers between devices with their start and end apart: 95, of which 56 were waited for; matrix products, arithmetic and copies ran while one was open for 6% of the time, Pallas kernels for 15%

profile of v2, /device:TPU:0, one launch (start us, length us, event | category | flops | bytes accessed | tf_op | source)
XLA Modules:
  0.0 567.2 jit_solution(9744685810713565954)
XLA Ops:
  12.2 5.0 collective-permute-start.4
  19.4 2.8 collective-permute-done.3
  22.2 2.5 collective-permute-start.7
  25.8 4.9 collective-permute-done.7
  30.7 2.5 collective-permute-done.6
  35.1 2.1 fusion.6
  37.2 3.2 collective-permute-start
  47.5 3.1 shard_map.421
  52.7 2.0 collective-permute-start.9
  57.7 2.2 collective-permute-start.11
  70.3 2.2 shard_map.422
  73.7 1.8 collective-permute-start.19
  91.5 2.3 collective-permute-start.25
  100.2 3.1 copy.71
  107.4 1.9 copy-done.27
  110.3 5.8 %shard_map.424 = (bf16[784,1024]{1,0:T(8,128)(2,1)S(1)}, bf16[784,512]{1,0:T(8,128)(2,1)}, bf16[784,1024]{1,0:T(8,128)(2,1)}) custom-call(f32[8]{0:T(128)S(1)} %stack.43.flags, bf16[784,256]{1,0:T(8,128)(2,1)S(1)} %copy-done.63, bf16[784,1024]{1,0:T(8,128)(2,1)S(1)} %reshape.185.cells, bf16[256,1024]{1,0:T(8,128)(2,1)S(1)} %bitcast.80, ...), custom_call_target="tpu_custom_call" | custom-call | flops 7000000000 | tf_op jit(solution)/shard_map/pallas_call | solution.py:207
  118.7 2.1 collective-permute-start.31
  120.8 47.5 %collective-permute-done.31.query = bf16[784,512]{1,0:T(8,128)(2,1)} collective-permute-done((bf16[784,512]{1,0:T(8,128)(2,1)}, bf16[784,512]{1,0:T(8,128)(2,1)}, u32[]{:S(2)}, u32[]{:S(2)}) %collective-permute-start.31) | collective-permute-done | bytes 802848 | tf_op jit(solution)/shard_map/ppermute | solution.py:33
  173.7 10.6 %shard_map.426 = (bf16[784,512]{1,0:T(8,128)(2,1)S(1)}, f32[8,896]{1,0:T(8,128)S(1)}) custom-call(s32[1]{0:T(128)} %bitcast.20.count, bf16[784,512]{1,0:T(8,128)(2,1)} %collective-permute-done.31.query, bf16[784,1024]{1,0:T(8,128)(2,1)} %get-tuple-element.130.one.refs_2_, bf16[784,1024]{1,0:T(8,128)(2,1)} %collective-permute-done.30.two.refs_3_, ...), custom_call_target="tpu_custom_call" | custom-call | flops 10000000000 | tf_op jit(solution)/shard_map/pallas_call | solution.py:207
  184.4 1.9 collective-permute-start.34
  187.4 10.6 %shard_map.425 = (bf16[784,512]{1,0:T(8,128)(2,1)S(1)}, f32[784,128]{1,0:T(8,128)S(1)}) custom-call(s32[1]{0:T(128)} %bitcast.5.count, bf16[784,512]{1,0:T(8,128)(2,1)} %get-tuple-element.129.query, bf16[784,1024]{1,0:T(8,128)(2,1)} %get-tuple-element.130.one.refs_2_, bf16[784,1024]{1,0:T(8,128)(2,1)} %collective-permute-done.30.two.refs_3_, ...), custom_call_target="tpu_custom_call" | custom-call | flops 10000000000 | tf_op jit(solution)/shard_map/pallas_call | solution.py:207
  198.0 25.7 %collective-permute-done.35.far_log = f32[8,896]{1,0:T(8,128)S(1)} collective-permute-done((f32[8,896]{1,0:T(8,128)S(1)}, f32[8,896]{1,0:T(8,128)S(1)}, u32[]{:S(2)}, u32[]{:S(2)}) %collective-permute-start.35) | collective-permute-done | bytes 28704 | tf_op jit(solution)/shard_map/ppermute | solution.py:33
  223.7 2.5 shard_map.427
  229.1 2.4 collective-permute-start.39
  231.5 2.0 collective-permute-start.38
  248.6 4.0 shard_map.428
  252.6 2.5 collective-permute-start.43
  255.6 19.5 %shard_map.429 = (f32[784,512]{1,0:T(8,128)S(1)}, bf16[784,1024]{1,0:T(8,128)(2,1)S(1)}, bf16[784,1024]{1,0:T(8,128)(2,1)S(1)}, bf16[784,1024]{1,0:T(8,128)(2,1)S(1)}, bf16[784,1024]{1,0:T(8,128)(2,1)S(1)}) custom-call(s32[1]{0:T(128)} %bitcast.5.count, bf16[784,512]{1,0:T(8,128)(2,1)} %get-tuple-element.129.query, ...), custom_call_target="tpu_custom_call" | custom-call | flops 16999999488 | tf_op jit(solution)/shard_map/pallas_call | solution.py:207
  278.5 10.2 %collective-permute-done.44.refs_0_ = f32[8,896]{1,0:T(8,128)S(1)} collective-permute-done((f32[8,896]{1,0:T(8,128)S(1)}, f32[8,896]{1,0:T(8,128)S(1)}, u32[]{:S(2)}, u32[]{:S(2)}) %collective-permute-start.44) | collective-permute-done | bytes 28704 | tf_op jit(solution)/shard_map/ppermute | solution.py:33
  288.8 11.6 %shard_map.430 = (f32[784,512]{1,0:T(8,128)S(1)}, bf16[784,1024]{1,0:T(8,128)(2,1)S(1)}, bf16[784,1024]{1,0:T(8,128)(2,1)S(1)}) custom-call(s32[1]{0:T(128)} %bitcast.20.count, bf16[784,512]{1,0:T(8,128)(2,1)} %collective-permute-done.31.query, bf16[784,512]{1,0:T(8,128)(2,1)S(1)} %collective-permute-done.43.grad, ...), custom_call_target="tpu_custom_call" | custom-call | flops 16999999488 | tf_op jit(solution)/shard_map/pallas_call | solution.py:207
  300.5 3.4 collective-permute-done.45
  303.9 2.0 add_convert_fusion
  306.4 12.4 %shard_map.431 = (bf16[784,512]{1,0:T(8,128)(2,1)S(1)}, bf16[784,1024]{1,0:T(8,128)(2,1)S(1)}, bf16[784,512]{1,0:T(8,128)(2,1)S(1)}, bf16[784,512]{1,0:T(8,128)(2,1)S(1)}) custom-call(s32[1]{0:T(128)} %bitcast.20.count, bf16[784,512]{1,0:T(8,128)(2,1)} %collective-permute-done.31.query, bf16[784,512]{1,0:T(8,128)(2,1)S(1)} %collective-permute-done.43.grad, ...), custom_call_target="tpu_custom_call" | custom-call | flops 16999999488 | tf_op jit(solution)/shard_map/pallas_call | solution.py:207
  318.8 2.2 collective-permute-start.46
  322.1 36.1 %collective-permute-done.46.query_far = bf16[784,512]{1,0:T(8,128)(2,1)S(1)} collective-permute-done((bf16[784,512]{1,0:T(8,128)(2,1)S(1)}, bf16[784,512]{1,0:T(8,128)(2,1)S(1)}, u32[]{:S(2)}, u32[]{:S(2)}) %collective-permute-start.46) | collective-permute-done | bytes 802848 | tf_op jit(solution)/shard_map/ppermute | solution.py:33
  358.2 2.2 collective-permute-done.49.far
  361.9 5.2 shard_map.432
  368.4 2.1 collective-permute-start.53
  370.5 2.3 collective-permute-start.52
  376.9 1.9 collective-permute-start.56
  378.8 5.7 shard_map.433
  385.2 2.2 shard_map.435
  394.2 2.0 collective-permute-done.60
  402.7 2.5 shard_map.436
  409.8 2.6 collective-permute-start.67
  414.7 2.0 collective-permute-start.69
  425.4 3.3 shard_map.438.middle
  429.2 3.9 shard_map.440
  435.3 3.3 collective-permute-start.74
  438.6 3.3 collective-permute-done.74.arrived
  451.2 9.7 %collective-permute-done.77 = bf16[800,256]{1,0:T(8,128)(2,1)} collective-permute-done((bf16[800,256]{1,0:T(8,128)(2,1)}, bf16[800,256]{1,0:T(8,128)(2,1)}, u32[]{:S(2)}, u32[]{:S(2)}) %collective-permute-start.77) | collective-permute-done | bytes 409632 | tf_op jit(solution)/shard_map/ppermute | solution.py:33
  460.9 7.8 %collective-permute-done.76 = bf16[800,256]{1,0:T(8,128)(2,1)} collective-permute-done((bf16[800,256]{1,0:T(8,128)(2,1)}, bf16[800,256]{1,0:T(8,128)(2,1)}, u32[]{:S(2)}, u32[]{:S(2)}) %collective-permute-start.76) | collective-permute-done | bytes 409632 | tf_op jit(solution)/shard_map/ppermute | solution.py:33
  473.7 2.0 collective-permute-start.78
  475.7 3.2 collective-permute-done.80
  478.9 12.1 %collective-permute-done.79 = bf16[200,256]{1,0:T(8,128)(2,1)S(1)} collective-permute-done((bf16[200,256]{1,0:T(8,128)(2,1)S(1)}, bf16[200,256]{1,0:T(8,128)(2,1)S(1)}, u32[]{:S(2)}, u32[]{:S(2)}) %collective-permute-start.79) | collective-permute-done | bytes 102432 | tf_op jit(solution)/shard_map/ppermute | solution.py:33
  493.4 3.1 collective-permute-start.83
  498.6 4.2 collective-permute-done.82
  506.3 2.4 copy.74
  513.9 2.4 copy.75
  520.6 14.3 %collective-permute-done.86 = bf16[800,256]{1,0:T(8,128)(2,1)S(1)} collective-permute-done((bf16[800,256]{1,0:T(8,128)(2,1)}, bf16[800,256]{1,0:T(8,128)(2,1)S(1)}, u32[]{:S(2)}, u32[]{:S(2)}) %collective-permute-start.86) | collective-permute-done | bytes 409632 | tf_op jit(solution)/shard_map/ppermute | solution.py:33
  534.9 2.8 all-gather.11.cloned.1.call-done.half
  539.0 4.7 collective-permute-done.88.other
  545.5 6.4 %shard_map.443 = (f32[3,1024,512]{2,1,0:T(8,128)}, f32[512,1024]{1,0:T(8,128)}, f32[3,128,512]{2,1,0:T(8,128)S(1)}, f32[64,1024]{1,0:T(8,128)S(1)}, f32[8,256]{1,0:T(8,128)S(1)}) custom-call(s32[3]{0:T(128)S(1)} %copy-done.23, f32[8]{0:T(128)S(1)} %copy-done.26, bf16[4096,256]{1,0:T(8,128)(2,1)S(1)} %copy-done.29, ...), custom_call_target="tpu_custom_call" | custom-call | flops 6000000000 | tf_op jit(solution)/shard_map/pallas_call | solution.py:207
  552.0 6.1 %shard_map.444 = (f32[3,1024,256]{2,1,0:T(8,128)}, f32[9,256,256]{2,1,0:T(8,128)}, f32[256,1024]{1,0:T(8,128)}, f32[2,128]{1,0:T(2,128)S(1)}, f32[3,128,256]{2,1...) custom-call(s32[3]{0:T(128)S(1)} %copy-done.23, ...), custom_call_target="tpu_custom_call" | custom-call | flops 8000000000 | tf_op jit(solution)/shard_map/pallas_call | solution.py:207
  (427 shorter events, 163.8 us)
Async XLA Ops:
  7.2 61.5 %all-gather.5.cloned.1.call-start = ((), (), s32[]{:S(2)}) async-start(), calls=%async_computation.1 | async-start | bytes 1916928 | tf_op jit(solution)/shard_map/all_gather | solution.py:1348
  10.0 96.4 %all-gather.7.cloned.1.call-start = ((), (), s32[]{:S(2)}) async-start(), calls=%async_computation.2 | async-start | bytes 3538944 | tf_op jit(solution)/shard_map/all_gather | solution.py:1356
  11.2 109.6 %all-gather.9.cloned.1.call-start = ((), (), s32[]{:S(2)}) async-start(), calls=%async_computation.3 | async-start | bytes 1179648 | tf_op jit(solution)/shard_map/all_gather | solution.py:1357
  12.2 7.3 %collective-permute-start.4 = (bf16[1,3,32,256]{3,2,1,0:T(8,128)(2,1)S(1)}, bf16[1,3,32,256]{3,2,1,0:T(8,128)(2,1)S(1)}, u32[]{:S(2)}, u32[]{:S(2)}) collective-permute-start(bf16[1,3,32,256]{3,2,1,0:T(8,128)(2,1)S(1)} %fusion), channel_id=1, source_target_pairs={{0,6},{1,7},{2,4},{3,5},{4,2},{5,3},{6,0},{7,1},{8,14},{9,15},{10,... | collective-permute-start | bytes 147464 | tf_op jit(solution)/shard_map/ppermute | solution.py:33
  17.2 5.0 collective-permute-start.3
  17.2 5.0 collective-permute-start.2
  22.2 8.5 %collective-permute-start.7 = (bf16[1,4,3,32,256]{4,3,2,1,0:T(8,128)(2,1)S(1)}, bf16[1,4,3,32,256]{4,3,2,1,0:T(8,128)(2,1)S(1)}, u32[]{:S(2)}, u32[]{:S(2)}) collective-permute-start(bf16[1,4,3,32,256]{4,3,2,1,0:T(8,128)(2,1)S(1)} %maximum_bitcast_fusion), channel_id=1, source_target_pairs={{0,24},{8,16},{16,8},{24,0},{1,25},{9,17},{17,9},{25,1},{2,26},{10... | collective-permute-start | bytes 589832 | tf_op jit(solution)/shard_map/ppermute | solution.py:33
  24.8 8.4 %collective-permute-start.6 = (bf16[1,4,3,32,256]{4,3,2,1,0:T(8,128)(2,1)S(1)}, bf16[1,4,3,32,256]{4,3,2,1,0:T(8,128)(2,1)S(1)}, u32[]{:S(2)}, u32[]{:S(2)}) collective-permute-start(bf16[1,4,3,32,256]{4,3,2,1,0:T(8,128)(2,1)S(1)} %maximum_bitcast_fusion), channel_id=1, source_target_pairs={{0,16},{8,24},{16,0},{24,8},{1,17},{9,25},{17,1},{25,9},{2,18},{10... | collective-permute-start | bytes 589832 | tf_op jit(solution)/shard_map/ppermute | solution.py:33
  25.3 8.0 %collective-permute-start.5 = (bf16[1,4,3,32,256]{4,3,2,1,0:T(8,128)(2,1)S(1)}, bf16[1,4,3,32,256]{4,3,2,1,0:T(8,128)(2,1)S(1)}, u32[]{:S(2)}, u32[]{:S(2)}) collective-permute-start(bf16[1,4,3,32,256]{4,3,2,1,0:T(8,128)(2,1)S(1)} %maximum_bitcast_fusion), channel_id=1, source_target_pairs={{0,8},{8,0},{16,24},{24,16},{1,9},{9,1},{17,25},{25,17},{2,10},{10... | collective-permute-start | bytes 589832 | tf_op jit(solution)/shard_map/ppermute | solution.py:33
  33.4 14.1 %collective-permute-start.8 = (bf16[4,4,3,32,256]{4,3,2,1,0:T(8,128)(2,1)S(1)}, bf16[4,4,3,32,256]{4,3,2,1,0:T(8,128)(2,1)S(1)}, u32[]{:S(2)}, u32[]{:S(2)}) collective-permute-start(bf16[4,4,3,32,256]{4,3,2,1,0:T(8,128)(2,1)S(1)} %pad_maximum_fusion.mine), channel_id=1, source_target_pairs={{0,1},{1,0},{2,3},{3,2},{4,5},{5,4},{6,7},{7,6},{8,9},{9,8},{10,11... | collective-permute-start | bytes 2359304 | tf_op jit(solution)/shard_map/ppermute | solution.py:33
  37.2 10.3 %collective-permute-start = (bf16[1,196,1024]{2,1,0:T(8,128)(2,1)}, bf16[1,196,1024]{2,1,0:T(8,128)(2,1)}, u32[]{:S(2)}, u32[]{:S(2)}) collective-permute-start(bf16[1,196,1024]{2,1,0:T(8,128)(2,1)} %get-tuple-element.222), channel_id=1, source_target_pairs={{0,1},{1,2},{2,3},{3,4},{4,5},{5,6},{6,7},{8,9},{9,10},{10,11},{11... | collective-permute-start | bytes 1204232 | tf_op jit(solution)/shard_map/ppermute | solution.py:61
  40.4 7.1 %collective-permute-start.1 = (bf16[1,196,1024]{2,1,0:T(8,128)(2,1)}, bf16[1,196,1024]{2,1,0:T(8,128)(2,1)}, u32[]{:S(2)}, u32[]{:S(2)}) collective-permute-start(bf16[1,196,1024]{2,1,0:T(8,128)(2,1)} %get-tuple-element.221), channel_id=1, source_target_pairs={{1,0},{2,1},{3,2},{4,3},{5,4},{6,5},{7,6},{9,8},{10,9},{11,10},{12... | collective-permute-start | bytes 1204232 | tf_op jit(solution)/shard_map/ppermute | solution.py:62
  55.5 5.4 collective-permute-start.12
  73.7 5.4 collective-permute-start.19
  89.4 5.5 collective-permute-start.26
  94.5 356.4 %reduce-scatter.2.cloned.1.call-start = ((), (), s32[]{:S(2)}) async-start(), calls=%async_computation.4 | async-start | bytes 2621440 | tf_op jit(solution)/shard_map/reduce_scatter | solution.py:1457
  96.1 8.8 %collective-permute-start.27 = (f32[2,1024]{1,0:T(2,128)S(1)}, f32[2,1024]{1,0:T(2,128)S(1)}, u32[]{:S(2)}, u32[]{:S(2)}) collective-permute-start(f32[2,1024]{1,0:T(2,128)S(1)} %add_add_fusion.5), channel_id=1, source_target_pairs={{0,8},{8,0},{16,24},{24,16},{1,9},{9,1},{17,25},{25,17},{2,10},{10... | collective-permute-start | bytes 24584 | tf_op jit(solution)/shard_map/ppermute | solution.py:33
  97.6 7.4 %collective-permute-start.28 = (f32[2,1024]{1,0:T(2,128)S(1)}, f32[2,1024]{1,0:T(2,128)}, u32[]{:S(2)}, u32[]{:S(2)}) collective-permute-start(f32[2,1024]{1,0:T(2,128)S(1)} %add_add_fusion.5), channel_id=1, source_target_pairs={{0,16},{8,24},{16,0},{24,8},{1,17},{9,25},{17,1},{25,9},{2,18},{10... | collective-permute-start | bytes 24584 | tf_op jit(solution)/shard_map/ppermute | solution.py:33
  98.2 7.4 %collective-permute-start.29 = (f32[2,1024]{1,0:T(2,128)S(1)}, f32[2,1024]{1,0:T(2,128)}, u32[]{:S(2)}, u32[]{:S(2)}) collective-permute-start(f32[2,1024]{1,0:T(2,128)S(1)} %add_add_fusion.5), channel_id=1, source_target_pairs={{0,24},{8,16},{16,8},{24,0},{1,25},{9,17},{17,9},{25,1},{2,26},{10... | collective-permute-start | bytes 24584 | tf_op jit(solution)/shard_map/ppermute | solution.py:33
  117.3 52.7 %collective-permute-start.32 = (bf16[784,1024]{1,0:T(8,128)(2,1)}, bf16[784,1024]{1,0:T(8,128)(2,1)}, u32[]{:S(2)}, u32[]{:S(2)}) collective-permute-start(bf16[784,1024]{1,0:T(8,128)(2,1)} %get-tuple-element.130.one.refs_2_), channel_id=1, source_target_pairs={{0,2},{1,3},{2,0},{3,1},{4,6},{5,7},{6,4},{7,5},{8,10},{9,11},{10,... | collective-permute-start | bytes 4816904 | tf_op jit(solution)/shard_map/ppermute | solution.py:33
  118.7 49.6 %collective-permute-start.31 = (bf16[784,512]{1,0:T(8,128)(2,1)}, bf16[784,512]{1,0:T(8,128)(2,1)}, u32[]{:S(2)}, u32[]{:S(2)}) collective-permute-start(bf16[784,512]{1,0:T(8,128)(2,1)} %get-tuple-element.129.query), channel_id=1, source_target_pairs={{0,4},{1,5},{2,6},{3,7},{4,0},{5,1},{6,2},{7,3},{8,12},{9,13},{10,... | collective-permute-start | bytes 2408456 | tf_op jit(solution)/shard_map/ppermute | solution.py:33
  120.8 51.1 %collective-permute-start.30 = (bf16[784,1024]{1,0:T(8,128)(2,1)}, bf16[784,1024]{1,0:T(8,128)(2,1)}, u32[]{:S(2)}, u32[]{:S(2)}) collective-permute-start(bf16[784,1024]{1,0:T(8,128)(2,1)} %get-tuple-element.130.one.refs_2_), channel_id=1, source_target_pairs={{0,1},{1,0},{2,3},{3,2},{4,5},{5,4},{6,7},{7,6},{8,9},{9,8},{10,11... | collective-permute-start | bytes 4816904 | tf_op jit(solution)/shard_map/ppermute | solution.py:33
  184.4 39.3 %collective-permute-start.34 = (bf16[784,512]{1,0:T(8,128)(2,1)S(1)}, bf16[784,512]{1,0:T(8,128)(2,1)S(1)}, u32[]{:S(2)}, u32[]{:S(2)}) collective-permute-start(bf16[784,512]{1,0:T(8,128)(2,1)S(1)} %get-tuple-element.135), channel_id=1, source_target_pairs={{0,4},{1,5},{2,6},{3,7},{4,0},{5,1},{6,2},{7,3},{8,12},{9,13},{10,... | collective-permute-start | bytes 2408456 | tf_op jit(solution)/shard_map/ppermute | solution.py:33
  186.2 37.5 %collective-permute-start.35 = (f32[8,896]{1,0:T(8,128)S(1)}, f32[8,896]{1,0:T(8,128)S(1)}, u32[]{:S(2)}, u32[]{:S(2)}) collective-permute-start(f32[8,896]{1,0:T(8,128)S(1)} %get-tuple-element.136), channel_id=1, source_target_pairs={{0,4},{1,5},{2,6},{3,7},{4,0},{5,1},{6,2},{7,3},{8,12},{9,13},{10,... | collective-permute-start | bytes 86024 | tf_op jit(solution)/shard_map/ppermute | solution.py:33
  229.1 5.7 %collective-permute-start.39 = (f32[5,1024]{1,0:T(8,128)S(1)}, f32[5,1024]{1,0:T(8,128)S(1)}, u32[]{:S(2)}, u32[]{:S(2)}) collective-permute-start(f32[5,1024]{1,0:T(8,128)S(1)} %add.289), channel_id=1, source_target_pairs={{0,6},{1,7},{2,4},{3,5},{4,2},{5,3},{6,0},{7,1},{8,14},{9,15},{10,... | collective-permute-start | bytes 61448 | tf_op jit(solution)/shard_map/ppermute | solution.py:33
  231.5 5.2 collective-permute-start.38
  236.6 4.9 collective-permute-start.42
  252.6 36.1 %collective-permute-start.43 = (bf16[784,512]{1,0:T(8,128)(2,1)S(1)}, bf16[784,512]{1,0:T(8,128)(2,1)S(1)}, u32[]{:S(2)}, u32[]{:S(2)}) collective-permute-start(bf16[784,512]{1,0:T(8,128)(2,1)S(1)} %get-tuple-element.143.grad), channel_id=1, source_target_pairs={{0,4},{1,5},{2,6},{3,7},{4,0},{5,1},{6,2},{7,3},{8,12},{9,13},{10,... | collective-permute-start | bytes 2408456 | tf_op jit(solution)/shard_map/ppermute | solution.py:33
  255.1 33.6 %collective-permute-start.44 = (f32[8,896]{1,0:T(8,128)S(1)}, f32[8,896]{1,0:T(8,128)S(1)}, u32[]{:S(2)}, u32[]{:S(2)}) collective-permute-start(f32[8,896]{1,0:T(8,128)S(1)} %get-tuple-element.146), channel_id=1, source_target_pairs={{0,4},{1,5},{2,6},{3,7},{4,0},{5,1},{6,2},{7,3},{8,12},{9,13},{10,... | collective-permute-start | bytes 86024 | tf_op jit(solution)/shard_map/ppermute | solution.py:33
  305.9 54.6 %collective-permute-start.49 = (bf16[784,1024]{1,0:T(8,128)(2,1)}, bf16[784,1024]{1,0:T(8,128)(2,1)S(1)}, u32[]{:S(2)}, u32[]{:S(2)}) collective-permute-start(bf16[784,1024]{1,0:T(8,128)(2,1)} %add_convert_fusion), channel_id=1, source_target_pairs={{0,2},{1,3},{2,0},{3,1},{4,6},{5,7},{6,4},{7,5},{8,10},{9,11},{10,... | collective-permute-start | bytes 4816904 | tf_op jit(solution)/shard_map/ppermute | solution.py:33
  318.8 39.4 %collective-permute-start.46 = (bf16[784,512]{1,0:T(8,128)(2,1)S(1)}, bf16[784,512]{1,0:T(8,128)(2,1)S(1)}, u32[]{:S(2)}, u32[]{:S(2)}) collective-permute-start(bf16[784,512]{1,0:T(8,128)(2,1)S(1)} %get-tuple-element.155), channel_id=1, source_target_pairs={{0,4},{1,5},{2,6},{3,7},{4,0},{5,1},{6,2},{7,3},{8,12},{9,13},{10,... | collective-permute-start | bytes 2408456 | tf_op jit(solution)/shard_map/ppermute | solution.py:33
  321.0 37.2 %collective-permute-start.47 = (bf16[784,512]{1,0:T(8,128)(2,1)S(1)}, bf16[784,512]{1,0:T(8,128)(2,1)S(1)}, u32[]{:S(2)}, u32[]{:S(2)}) collective-permute-start(bf16[784,512]{1,0:T(8,128)(2,1)S(1)} %get-tuple-element.157), channel_id=1, source_target_pairs={{0,1},{1,0},{2,3},{3,2},{4,5},{5,4},{6,7},{7,6},{8,9},{9,8},{10,11... | collective-permute-start | bytes 2408456 | tf_op jit(solution)/shard_map/ppermute | solution.py:33
  321.0 37.2 %collective-permute-start.48 = (bf16[784,512]{1,0:T(8,128)(2,1)S(1)}, bf16[784,512]{1,0:T(8,128)(2,1)S(1)}, u32[]{:S(2)}, u32[]{:S(2)}) collective-permute-start(bf16[784,512]{1,0:T(8,128)(2,1)S(1)} %get-tuple-element.158), channel_id=1, source_target_pairs={{0,1},{1,0},{2,3},{3,2},{4,5},{5,4},{6,7},{7,6},{8,9},{9,8},{10,11... | collective-permute-start | bytes 2408456 | tf_op jit(solution)/shard_map/ppermute | solution.py:33
  368.4 5.6 collective-permute-start.53
  370.5 4.6 collective-permute-start.52
  375.2 9.3 %collective-permute-start.54 = (f32[3,1024]{1,0:T(4,128)S(1)}, f32[3,1024]{1,0:T(4,128)S(1)}, u32[]{:S(2)}, u32[]{:S(2)}) collective-permute-start(f32[3,1024]{1,0:T(4,128)S(1)} %add_add_fusion.3), channel_id=1, source_target_pairs={{0,8},{8,0},{16,24},{24,16},{1,9},{9,1},{17,25},{25,17},{2,10},{10... | collective-permute-start | bytes 36872 | tf_op jit(solution)/shard_map/ppermute | solution.py:33
  375.2 9.2 %collective-permute-start.55 = (f32[3,1024]{1,0:T(4,128)S(1)}, f32[3,1024]{1,0:T(4,128)S(1)}, u32[]{:S(2)}, u32[]{:S(2)}) collective-permute-start(f32[3,1024]{1,0:T(4,128)S(1)} %add_add_fusion.3), channel_id=1, source_target_pairs={{0,16},{8,24},{16,0},{24,8},{1,17},{9,25},{17,1},{25,9},{2,18},{10... | collective-permute-start | bytes 36872 | tf_op jit(solution)/shard_map/ppermute | solution.py:33
  376.9 7.6 %collective-permute-start.56 = (f32[3,1024]{1,0:T(4,128)S(1)}, f32[3,1024]{1,0:T(4,128)S(1)}, u32[]{:S(2)}, u32[]{:S(2)}) collective-permute-start(f32[3,1024]{1,0:T(4,128)S(1)} %add_add_fusion.3), channel_id=1, source_target_pairs={{0,24},{8,16},{16,8},{24,0},{1,25},{9,17},{17,9},{25,1},{2,26},{10... | collective-permute-start | bytes 36872 | tf_op jit(solution)/shard_map/ppermute | solution.py:33
  384.5 27.9 %collective-permute-start.57 = (bf16[4096,256]{1,0:T(8,128)(2,1)S(1)}, bf16[4096,256]{1,0:T(8,128)(2,1)S(1)}, u32[]{:S(2)}, u32[]{:S(2)}) collective-permute-start(bf16[4096,256]{1,0:T(8,128)(2,1)S(1)} %get-tuple-element.167), channel_id=1, source_target_pairs={{0,1},{1,0},{2,3},{3,2},{4,5},{5,4},{6,7},{7,6},{8,9},{9,8},{10,11... | collective-permute-start | bytes 6291464 | tf_op jit(solution)/shard_map/ppermute | solution.py:33
  388.9 5.4 collective-permute-start.61
  408.0 6.3 %collective-permute-start.68 = (f32[2,256]{1,0:T(2,128)S(1)}, f32[2,256]{1,0:T(2,128)S(1)}, u32[]{:S(2)}, u32[]{:S(2)}) collective-permute-start(f32[2,256]{1,0:T(2,128)S(1)} %add.311), channel_id=1, source_target_pairs={{0,6},{1,7},{2,4},{3,5},{4,2},{5,3},{6,0},{7,1},{8,14},{9,15},{10,... | collective-permute-start | bytes 6152 | tf_op jit(solution)/shard_map/ppermute | solution.py:33
  409.5 4.7 collective-permute-start.66
  414.2 77.8 %all-reduce.2.cloned.1.call-start = ((), (), s32[]{:S(2)}) async-start(), calls=%async_computation.5 | async-start | bytes 1048576 | tf_op jit(solution)/shard_map/psum | solution.py:1458
  414.3 7.1 %collective-permute-start.71 = (f32[2,256]{1,0:T(2,128)S(1)}, f32[2,256]{1,0:T(2,128)S(1)}, u32[]{:S(2)}, u32[]{:S(2)}) collective-permute-start(f32[2,256]{1,0:T(2,128)S(1)} %add_add_fusion.7), channel_id=1, source_target_pairs={{0,24},{8,16},{16,8},{24,0},{1,25},{9,17},{17,9},{25,1},{2,26},{10... | collective-permute-start | bytes 6152 | tf_op jit(solution)/shard_map/ppermute | solution.py:33
  414.7 6.7 %collective-permute-start.69 = (f32[2,256]{1,0:T(2,128)S(1)}, f32[2,256]{1,0:T(2,128)S(1)}, u32[]{:S(2)}, u32[]{:S(2)}) collective-permute-start(f32[2,256]{1,0:T(2,128)S(1)} %add_add_fusion.7), channel_id=1, source_target_pairs={{0,8},{8,0},{16,24},{24,16},{1,9},{9,1},{17,25},{25,17},{2,10},{10... | collective-permute-start | bytes 6152 | tf_op jit(solution)/shard_map/ppermute | solution.py:33
  416.6 4.7 collective-permute-start.70
  422.8 5.9 %collective-permute-start.72 = (bf16[1,196,256]{2,1,0:T(8,128)(2,1)S(1)}, bf16[1,196,256]{2,1,0:T(8,128)(2,1)S(1)}, u32[]{:S(2)}, u32[]{:S(2)}) collective-permute-start(bf16[1,196,256]{2,1,0:T(8,128)(2,1)S(1)} %get-tuple-element.227), channel_id=1, source_target_pairs={{0,1},{1,2},{2,3},{3,4},{4,5},{5,6},{6,7},{8,9},{9,10},{10,11},{11... | collective-permute-start | bytes 301064 | tf_op jit(solution)/shard_map/ppermute | solution.py:61
  424.1 5.1 collective-permute-start.73
  435.3 6.6 %collective-permute-start.74 = (bf16[3200,256]{1,0:T(8,128)(2,1)}, bf16[3200,256]{1,0:T(8,128)(2,1)S(1)}, u32[]{:S(2)}, u32[]{:S(2)}) collective-permute-start(bf16[3200,256]{1,0:T(8,128)(2,1)} %get-tuple-element.179), channel_id=1, source_target_pairs={{0,1},{1,0},{2,3},{3,2},{4,5},{5,4},{6,7},{7,6},{8,9},{9,8},{10,11... | collective-permute-start | bytes 4915208 | tf_op jit(solution)/shard_map/ppermute | solution.py:33
  447.4 13.5 %collective-permute-start.77 = (bf16[800,256]{1,0:T(8,128)(2,1)}, bf16[800,256]{1,0:T(8,128)(2,1)}, u32[]{:S(2)}, u32[]{:S(2)}) collective-permute-start(bf16[800,256]{1,0:T(8,128)(2,1)} %get-tuple-element.219), channel_id=1, source_target_pairs={{0,24},{8,16},{16,8},{24,0},{1,25},{9,17},{17,9},{25,1},{2,26},{10... | collective-permute-start | bytes 1228808 | tf_op jit(solution)/shard_map/ppermute | solution.py:33
  448.3 20.5 %collective-permute-start.76 = (bf16[800,256]{1,0:T(8,128)(2,1)}, bf16[800,256]{1,0:T(8,128)(2,1)}, u32[]{:S(2)}, u32[]{:S(2)}) collective-permute-start(bf16[800,256]{1,0:T(8,128)(2,1)} %get-tuple-element.220), channel_id=1, source_target_pairs={{0,16},{8,24},{16,0},{24,8},{1,17},{9,25},{17,1},{25,9},{2,18},{10... | collective-permute-start | bytes 1228808 | tf_op jit(solution)/shard_map/ppermute | solution.py:33
  449.6 19.4 %collective-permute-start.75 = (bf16[800,256]{1,0:T(8,128)(2,1)}, bf16[800,256]{1,0:T(8,128)(2,1)}, u32[]{:S(2)}, u32[]{:S(2)}) collective-permute-start(bf16[800,256]{1,0:T(8,128)(2,1)} %get-tuple-element.218), channel_id=1, source_target_pairs={{0,8},{8,0},{16,24},{24,16},{1,9},{9,1},{17,25},{25,17},{2,10},{10... | collective-permute-start | bytes 1228808 | tf_op jit(solution)/shard_map/ppermute | solution.py:33
  450.9 86.8 %all-gather.11.cloned.1.call-start = ((), (), s32[]{:S(2)}) async-start(), calls=%async_computation.6 | async-start | bytes 2621440 | tf_op jit(solution)/shard_map/all_gather | solution.py:1462
  471.2 7.7 %collective-permute-start.80 = (bf16[200,256]{1,0:T(8,128)(2,1)S(1)}, bf16[200,256]{1,0:T(8,128)(2,1)S(1)}, u32[]{:S(2)}, u32[]{:S(2)}) collective-permute-start(bf16[200,256]{1,0:T(8,128)(2,1)S(1)} %get-tuple-element.224), channel_id=1, source_target_pairs={{0,6},{1,7},{2,4},{3,5},{4,2},{5,3},{6,0},{7,1},{8,14},{9,15},{10,... | collective-permute-start | bytes 307208 | tf_op jit(solution)/shard_map/ppermute | solution.py:33
  472.1 18.9 %collective-permute-start.79 = (bf16[200,256]{1,0:T(8,128)(2,1)S(1)}, bf16[200,256]{1,0:T(8,128)(2,1)S(1)}, u32[]{:S(2)}, u32[]{:S(2)}) collective-permute-start(bf16[200,256]{1,0:T(8,128)(2,1)S(1)} %get-tuple-element.225), channel_id=1, source_target_pairs={{0,4},{1,5},{2,6},{3,7},{4,0},{5,1},{6,2},{7,3},{8,12},{9,13},{10,... | collective-permute-start | bytes 307208 | tf_op jit(solution)/shard_map/ppermute | solution.py:33
  473.7 17.3 %collective-permute-start.78 = (bf16[200,256]{1,0:T(8,128)(2,1)S(1)}, bf16[200,256]{1,0:T(8,128)(2,1)S(1)}, u32[]{:S(2)}, u32[]{:S(2)}) collective-permute-start(bf16[200,256]{1,0:T(8,128)(2,1)S(1)} %get-tuple-element.223), channel_id=1, source_target_pairs={{0,2},{1,3},{2,0},{3,1},{4,6},{5,7},{6,4},{7,5},{8,10},{9,11},{10,... | collective-permute-start | bytes 307208 | tf_op jit(solution)/shard_map/ppermute | solution.py:33
  492.0 5.9 %collective-permute-start.81 = (bf16[200,256]{1,0:T(8,128)(2,1)S(1)}, bf16[200,256]{1,0:T(8,128)(2,1)S(1)}, u32[]{:S(2)}, u32[]{:S(2)}) collective-permute-start(bf16[200,256]{1,0:T(8,128)(2,1)S(1)} %add_convert_fusion.2), channel_id=1, source_target_pairs={{0,2},{1,3},{2,0},{3,1},{4,6},{5,7},{6,4},{7,5},{8,10},{9,11},{10,... | collective-permute-start | bytes 307208 | tf_op jit(solution)/shard_map/ppermute | solution.py:33
  492.1 10.7 %collective-permute-start.82 = (bf16[200,256]{1,0:T(8,128)(2,1)S(1)}, bf16[200,256]{1,0:T(8,128)(2,1)S(1)}, u32[]{:S(2)}, u32[]{:S(2)}) collective-permute-start(bf16[200,256]{1,0:T(8,128)(2,1)S(1)} %add_convert_fusion.2), channel_id=1, source_target_pairs={{0,4},{1,5},{2,6},{3,7},{4,0},{5,1},{6,2},{7,3},{8,12},{9,13},{10,... | collective-permute-start | bytes 307208 | tf_op jit(solution)/shard_map/ppermute | solution.py:33
  493.4 10.0 %collective-permute-start.83 = (bf16[200,256]{1,0:T(8,128)(2,1)S(1)}, bf16[200,256]{1,0:T(8,128)(2,1)S(1)}, u32[]{:S(2)}, u32[]{:S(2)}) collective-permute-start(bf16[200,256]{1,0:T(8,128)(2,1)S(1)} %add_convert_fusion.2), channel_id=1, source_target_pairs={{0,6},{1,7},{2,4},{3,5},{4,2},{5,3},{6,0},{7,1},{8,14},{9,15},{10,... | collective-permute-start | bytes 307208 | tf_op jit(solution)/shard_map/ppermute | solution.py:33
  504.1 14.4 %collective-permute-start.84 = (bf16[800,256]{1,0:T(8,128)(2,1)}, bf16[800,256]{1,0:T(8,128)(2,1)}, u32[]{:S(2)}, u32[]{:S(2)}) collective-permute-start(bf16[800,256]{1,0:T(8,128)(2,1)} %bitcast.30), channel_id=1, source_target_pairs={{0,8},{8,0},{16,24},{24,16},{1,9},{9,1},{17,25},{25,17},{2,10},{10... | collective-permute-start | bytes 1228808 | tf_op jit(solution)/shard_map/ppermute | solution.py:33
  508.6 10.9 %collective-permute-start.85 = (bf16[800,256]{1,0:T(8,128)(2,1)}, bf16[800,256]{1,0:T(8,128)(2,1)}, u32[]{:S(2)}, u32[]{:S(2)}) collective-permute-start(bf16[800,256]{1,0:T(8,128)(2,1)} %bitcast.30), channel_id=1, source_target_pairs={{0,16},{8,24},{16,0},{24,8},{1,17},{9,25},{17,1},{25,9},{2,18},{10... | collective-permute-start | bytes 1228808 | tf_op jit(solution)/shard_map/ppermute | solution.py:33
  516.3 18.6 %collective-permute-start.86 = (bf16[800,256]{1,0:T(8,128)(2,1)}, bf16[800,256]{1,0:T(8,128)(2,1)S(1)}, u32[]{:S(2)}, u32[]{:S(2)}) collective-permute-start(bf16[800,256]{1,0:T(8,128)(2,1)} %bitcast.30), channel_id=1, source_target_pairs={{0,24},{8,16},{16,8},{24,0},{1,25},{9,17},{17,9},{25,1},{2,26},{10... | collective-permute-start | bytes 1228808 | tf_op jit(solution)/shard_map/ppermute | solution.py:33
  537.7 6.0 %collective-permute-start.88 = (bf16[4096,256]{1,0:T(8,128)(2,1)}, bf16[4096,256]{1,0:T(8,128)(2,1)}, u32[]{:S(2)}, u32[]{:S(2)}) collective-permute-start(bf16[4096,256]{1,0:T(8,128)(2,1)} %all-gather.11.cloned.1.call-done.half), channel_id=1, source_target_pairs={{0,1},{1,0},{2,3},{3,2},{4,5},{5,4},{6,7},{7,6},{8,9},{9,8},{10,11... | collective-permute-start | bytes 6291464 | tf_op jit(solution)/shard_map/ppermute | solution.py:33
  537.8 14.0 %collective-permute-start.87 = (bf16[3200,256]{1,0:T(8,128)(2,1)S(1)}, bf16[3200,256]{1,0:T(8,128)(2,1)S(1)}, u32[]{:S(2)}, u32[]{:S(2)}) collective-permute-start(bf16[3200,256]{1,0:T(8,128)(2,1)S(1)} %bitcast.74), channel_id=1, source_target_pairs={{0,1},{1,0},{2,3},{3,2},{4,5},{5,4},{6,7},{7,6},{8,9},{9,8},{10,11... | collective-permute-start | bytes 4915208 | tf_op jit(solution)/shard_map/ppermute | solution.py:33
  (123 other events, 1630.1 us)
Sparse Core Ops, SparseCore 0:
  10.3 28.5 all-gather.4
  41.1 38.0 all-gather.6
  94.6 19.8 all-gather.8
  414.3 33.0 reduce-scatter.1
  451.0 40.2 all-reduce.1
  493.2 44.5 all-gather.10

commit v3 on v2

--- a/solution.py
+++ b/solution.py
@@ -37,11 +37,14 @@
     return lax.all_gather(shard.astype(jnp.bfloat16), "chan", axis=0, tiled=False)
 
 
-def quarters_of(shard):
+def quarter_of(shard):
     span = shard.shape[1] // 4
-    piece = lax.dynamic_slice_in_dim(
-        shard.astype(jnp.bfloat16), lax.axis_index("clip") * span, span, axis=1
-    )[None]
+    return lax.dynamic_slice_in_dim(
+        shard, lax.axis_index("clip") * span, span, axis=1
+    ).astype(jnp.bfloat16)[None]
+
+
+def quarters_of(piece):
     chips = jnp.concatenate(
         [piece] + [flipped(piece, "chan", 2 * turn) for turn in range(1, 4)]
     )[None]
@@ -1338,11 +1341,14 @@
         for index in range(0, 8, 2)
     ]
     shards = lax.axis_size("chan")
+    piece, middle_next, last_next, embed_next, back_next = tied(
+        quarter_of(weight_first), weight_middle, weight_last, weight_embed, weight_back
+    )
     tall = weight_middle.shape[0] * weight_middle.shape[1]
     packed = jnp.concatenate(
         [
-            weight_middle.reshape(tall, narrow),
-            jnp.moveaxis(weight_last.reshape(-1, model_width // 256, 256), 1, 0).reshape(-1, 256),
+            middle_next.reshape(tall, narrow),
+            jnp.moveaxis(last_next.reshape(-1, model_width // 256, 256), 1, 0).reshape(-1, 256),
         ]
     ).astype(LOW)
     packed = lax.all_gather(packed, "chan", axis=0, tiled=False)
@@ -1353,8 +1359,8 @@
     if weight_middle.shape[1] % 16:
         middle_low = jnp.moveaxis(middle_low, 0, 1).reshape(1, 9, narrow, narrow)
     embed_low, back_low = (
-        lax.all_gather(weight_embed.astype(LOW).reshape(-1, 3 * inner_width), "chan", axis=0, tiled=True),
-        lax.all_gather(weight_back.astype(LOW), "chan", axis=0, tiled=True),
+        lax.all_gather(embed_next.astype(LOW).reshape(-1, 3 * inner_width), "chan", axis=0, tiled=True),
+        lax.all_gather(back_next.astype(LOW), "chan", axis=0, tiled=True),
     )
     spots = np.arange(row_count)
     across, down = spots % WW, spots // WW % HH
@@ -1367,7 +1373,7 @@
     before, after = beside(features, spot_count)
     if shards == 8 and lax.axis_size("clip") == 4:
         pre_one, sums_one, first_low = first_conv_parts(
-            place, flags, cells, before, after, *quarters_of(weight_first)
+            place, flags, cells, before, after, *quarters_of(piece)
         )
     else:
         first_low = whole_of(weight_first)

time: 575 us -> 575 us (level)
    unnamed x193 -> x192, local copies, waits for them, and re-layouts: 43.2 us -> 42.8 us
where the time goes in v3:
time: 575 us; the launch traced here: 567 us
  waiting for transfers between devices  236 us (41%)
  Pallas kernels  124 us (22%)
  starting transfers between devices  107 us (19%)
  local copies, waits for them, and re-layouts  68.6 us (12%)
  between operations  21.3 us (4%)
  other arithmetic  11.2 us (2%)
    ppermute x85, waiting for transfers between devices, flipped(): return lax.ppermute(value, axis, pairs)  232 us
    pallas_call x24, Pallas kernels, call(): pl.pallas_call(kernel, out_shape=shapes, in_specs=spaces, out_specs=out_s...  124 us
    ppermute x85, starting transfers between devices, flipped(): return lax.ppermute(value, axis, pairs)  99 us
    unnamed x192, local copies, waits for them, and re-layouts  42.8 us
  transfers between devices with their start and end apart: 95, of which 56 were waited for; matrix products, arithmetic and copies ran while one was open for 6% of the time, Pallas kernels for 15%

profile of v3, /device:TPU:0, one launch (start us, length us, event | category | flops | bytes accessed | tf_op | source)
XLA Modules:
  0.0 567.4 jit_solution(7921342932439964209)
XLA Ops:
  12.2 5.1 collective-permute-start.4
  19.5 2.8 collective-permute-done.3
  22.3 2.5 collective-permute-start.7
  25.9 4.9 collective-permute-done.7
  30.8 2.5 collective-permute-done.6
  35.2 2.1 fusion.6
  37.2 3.2 collective-permute-start
  47.6 3.1 shard_map.421
  52.7 2.2 collective-permute-start.9
  57.7 2.4 collective-permute-start.11
  70.3 2.2 shard_map.422
  79.1 1.9 collective-permute-done.18
  91.4 2.4 collective-permute-start.25
  100.1 3.1 copy.71
  107.3 1.9 copy-done.27
  110.2 5.8 %shard_map.424 = (bf16[784,1024]{1,0:T(8,128)(2,1)S(1)}, bf16[784,512]{1,0:T(8,128)(2,1)}, bf16[784,1024]{1,0:T(8,128)(2,1)}) custom-call(f32[8]{0:T(128)S(1)} %stack.43.flags, bf16[784,256]{1,0:T(8,128)(2,1)S(1)} %copy-done.63, bf16[784,1024]{1,0:T(8,128)(2,1)S(1)} %reshape.185.cells, bf16[256,1024]{1,0:T(8,128)(2,1)S(1)} %bitcast.80, ...), custom_call_target="tpu_custom_call" | custom-call | flops 7000000000 | tf_op jit(solution)/shard_map/pallas_call | solution.py:210
  119.7 48.2 %collective-permute-done.31.query = bf16[784,512]{1,0:T(8,128)(2,1)} collective-permute-done((bf16[784,512]{1,0:T(8,128)(2,1)}, bf16[784,512]{1,0:T(8,128)(2,1)}, u32[]{:S(2)}, u32[]{:S(2)}) %collective-permute-start.31) | collective-permute-done | bytes 802848 | tf_op jit(solution)/shard_map/ppermute | solution.py:33
  173.5 10.6 %shard_map.426 = (bf16[784,512]{1,0:T(8,128)(2,1)S(1)}, f32[8,896]{1,0:T(8,128)S(1)}) custom-call(s32[1]{0:T(128)} %bitcast.20.count, bf16[784,512]{1,0:T(8,128)(2,1)} %collective-permute-done.31.query, bf16[784,1024]{1,0:T(8,128)(2,1)} %get-tuple-element.139.one.refs_2_, bf16[784,1024]{1,0:T(8,128)(2,1)} %collective-permute-done.30.two.refs_3_, ...), custom_call_target="tpu_custom_call" | custom-call | flops 10000000000 | tf_op jit(solution)/shard_map/pallas_call | solution.py:210
  187.1 10.6 %shard_map.425 = (bf16[784,512]{1,0:T(8,128)(2,1)S(1)}, f32[784,128]{1,0:T(8,128)S(1)}) custom-call(s32[1]{0:T(128)} %bitcast.5.count, bf16[784,512]{1,0:T(8,128)(2,1)} %get-tuple-element.138.query, bf16[784,1024]{1,0:T(8,128)(2,1)} %get-tuple-element.139.one.refs_2_, bf16[784,1024]{1,0:T(8,128)(2,1)} %collective-permute-done.30.two.refs_3_, ...), custom_call_target="tpu_custom_call" | custom-call | flops 10000000000 | tf_op jit(solution)/shard_map/pallas_call | solution.py:210
  197.7 25.7 %collective-permute-done.35.far_log = f32[8,896]{1,0:T(8,128)S(1)} collective-permute-done((f32[8,896]{1,0:T(8,128)S(1)}, f32[8,896]{1,0:T(8,128)S(1)}, u32[]{:S(2)}, u32[]{:S(2)}) %collective-permute-start.35) | collective-permute-done | bytes 28704 | tf_op jit(solution)/shard_map/ppermute | solution.py:33
  223.4 2.5 shard_map.427
  230.6 2.5 collective-permute-start.38
  235.9 2.8 collective-permute-start.40
  248.8 4.0 shard_map.428
  252.8 2.4 collective-permute-start.43
  255.8 19.5 %shard_map.429 = (f32[784,512]{1,0:T(8,128)S(1)}, bf16[784,1024]{1,0:T(8,128)(2,1)S(1)}, bf16[784,1024]{1,0:T(8,128)(2,1)S(1)}, bf16[784,1024]{1,0:T(8,128)(2,1)S(1)}, bf16[784,1024]{1,0:T(8,128)(2,1)S(1)}) custom-call(s32[1]{0:T(128)} %bitcast.5.count, bf16[784,512]{1,0:T(8,128)(2,1)} %get-tuple-element.138.query, ...), custom_call_target="tpu_custom_call" | custom-call | flops 16999999488 | tf_op jit(solution)/shard_map/pallas_call | solution.py:210
  278.7 10.2 %collective-permute-done.44.refs_0_ = f32[8,896]{1,0:T(8,128)S(1)} collective-permute-done((f32[8,896]{1,0:T(8,128)S(1)}, f32[8,896]{1,0:T(8,128)S(1)}, u32[]{:S(2)}, u32[]{:S(2)}) %collective-permute-start.44) | collective-permute-done | bytes 28704 | tf_op jit(solution)/shard_map/ppermute | solution.py:33
  289.0 11.6 %shard_map.430 = (f32[784,512]{1,0:T(8,128)S(1)}, bf16[784,1024]{1,0:T(8,128)(2,1)S(1)}, bf16[784,1024]{1,0:T(8,128)(2,1)S(1)}) custom-call(s32[1]{0:T(128)} %bitcast.20.count, bf16[784,512]{1,0:T(8,128)(2,1)} %collective-permute-done.31.query, bf16[784,512]{1,0:T(8,128)(2,1)S(1)} %collective-permute-done.43.grad, ...), custom_call_target="tpu_custom_call" | custom-call | flops 16999999488 | tf_op jit(solution)/shard_map/pallas_call | solution.py:210
  300.7 3.4 collective-permute-done.45
  304.1 2.0 add_convert_fusion
  306.6 12.4 %shard_map.431 = (bf16[784,512]{1,0:T(8,128)(2,1)S(1)}, bf16[784,1024]{1,0:T(8,128)(2,1)S(1)}, bf16[784,512]{1,0:T(8,128)(2,1)S(1)}, bf16[784,512]{1,0:T(8,128)(2,1)S(1)}) custom-call(s32[1]{0:T(128)} %bitcast.20.count, bf16[784,512]{1,0:T(8,128)(2,1)} %collective-permute-done.31.query, bf16[784,512]{1,0:T(8,128)(2,1)S(1)} %collective-permute-done.43.grad, ...), custom_call_target="tpu_custom_call" | custom-call | flops 16999999488 | tf_op jit(solution)/shard_map/pallas_call | solution.py:210
  319.0 2.2 collective-permute-start.46
  322.3 36.1 %collective-permute-done.46.query_far = bf16[784,512]{1,0:T(8,128)(2,1)S(1)} collective-permute-done((bf16[784,512]{1,0:T(8,128)(2,1)S(1)}, bf16[784,512]{1,0:T(8,128)(2,1)S(1)}, u32[]{:S(2)}, u32[]{:S(2)}) %collective-permute-start.46) | collective-permute-done | bytes 802848 | tf_op jit(solution)/shard_map/ppermute | solution.py:33
  358.5 2.2 collective-permute-done.49.far
  362.1 5.2 shard_map.432
  368.6 2.1 collective-permute-start.53
  370.7 2.3 collective-permute-start.52
  376.2 2.7 collective-permute-start.56
  379.0 5.7 shard_map.433
  385.4 2.2 shard_map.435
  394.5 2.0 collective-permute-done.60
  396.8 1.9 collective-permute-start.62
  402.3 2.5 shard_map.436
  407.6 1.9 collective-permute-start.68
  409.6 2.4 collective-permute-start.67
  424.8 3.3 shard_map.438.middle
  429.0 3.9 shard_map.440
  435.2 3.5 collective-permute-start.74
  438.7 3.3 collective-permute-done.74.arrived
  449.1 1.9 collective-permute-start.75
  451.3 9.7 %collective-permute-done.77 = bf16[800,256]{1,0:T(8,128)(2,1)} collective-permute-done((bf16[800,256]{1,0:T(8,128)(2,1)}, bf16[800,256]{1,0:T(8,128)(2,1)}, u32[]{:S(2)}, u32[]{:S(2)}) %collective-permute-start.77) | collective-permute-done | bytes 409632 | tf_op jit(solution)/shard_map/ppermute | solution.py:33
  461.1 8.2 %collective-permute-done.76 = bf16[800,256]{1,0:T(8,128)(2,1)} collective-permute-done((bf16[800,256]{1,0:T(8,128)(2,1)}, bf16[800,256]{1,0:T(8,128)(2,1)}, u32[]{:S(2)}, u32[]{:S(2)}) %collective-permute-start.76) | collective-permute-done | bytes 409632 | tf_op jit(solution)/shard_map/ppermute | solution.py:33
  474.0 1.9 collective-permute-start.78
  475.9 3.3 collective-permute-done.80
  479.2 12.3 %collective-permute-done.79 = bf16[200,256]{1,0:T(8,128)(2,1)S(1)} collective-permute-done((bf16[200,256]{1,0:T(8,128)(2,1)S(1)}, bf16[200,256]{1,0:T(8,128)(2,1)S(1)}, u32[]{:S(2)}, u32[]{:S(2)}) %collective-permute-start.79) | collective-permute-done | bytes 102432 | tf_op jit(solution)/shard_map/ppermute | solution.py:33
  494.2 2.8 collective-permute-start.83
  499.0 4.6 collective-permute-done.82
  505.7 2.4 copy.74
  514.4 2.4 copy.75
  521.4 13.7 %collective-permute-done.86 = bf16[800,256]{1,0:T(8,128)(2,1)S(1)} collective-permute-done((bf16[800,256]{1,0:T(8,128)(2,1)}, bf16[800,256]{1,0:T(8,128)(2,1)S(1)}, u32[]{:S(2)}, u32[]{:S(2)}) %collective-permute-start.86) | collective-permute-done | bytes 409632 | tf_op jit(solution)/shard_map/ppermute | solution.py:33
  535.2 2.8 all-gather.11.cloned.1.call-done.half
  539.2 4.7 collective-permute-done.88.other
  545.7 6.4 %shard_map.443 = (f32[3,1024,512]{2,1,0:T(8,128)}, f32[512,1024]{1,0:T(8,128)}, f32[3,128,512]{2,1,0:T(8,128)S(1)}, f32[64,1024]{1,0:T(8,128)S(1)}, f32[8,256]{1,0:T(8,128)S(1)}) custom-call(s32[3]{0:T(128)S(1)} %copy-done.23, f32[8]{0:T(128)S(1)} %copy-done.26, bf16[4096,256]{1,0:T(8,128)(2,1)S(1)} %copy-done.29, ...), custom_call_target="tpu_custom_call" | custom-call | flops 6000000000 | tf_op jit(solution)/shard_map/pallas_call | solution.py:210
  552.2 6.1 %shard_map.444 = (f32[3,1024,256]{2,1,0:T(8,128)}, f32[9,256,256]{2,1,0:T(8,128)}, f32[256,1024]{1,0:T(8,128)}, f32[2,128]{1,0:T(2,128)S(1)}, f32[3,128,256]{2,1...) custom-call(s32[3]{0:T(128)S(1)} %copy-done.23, ...), custom_call_target="tpu_custom_call" | custom-call | flops 8000000000 | tf_op jit(solution)/shard_map/pallas_call | solution.py:210
  (427 shorter events, 161.1 us)
Async XLA Ops:
  7.2 61.5 %all-gather.5.cloned.1.call-start = ((), (), s32[]{:S(2)}) async-start(), calls=%async_computation.1 | async-start | bytes 1916928 | tf_op jit(solution)/shard_map/all_gather | solution.py:1354
  10.9 95.4 %all-gather.7.cloned.1.call-start = ((), (), s32[]{:S(2)}) async-start(), calls=%async_computation.2 | async-start | bytes 3538944 | tf_op jit(solution)/shard_map/all_gather | solution.py:1362
  12.1 107.6 %all-gather.9.cloned.1.call-start = ((), (), s32[]{:S(2)}) async-start(), calls=%async_computation.3 | async-start | bytes 1179648 | tf_op jit(solution)/shard_map/all_gather | solution.py:1363
  12.2 7.3 %collective-permute-start.4 = (bf16[1,3,32,256]{3,2,1,0:T(8,128)(2,1)S(1)}, bf16[1,3,32,256]{3,2,1,0:T(8,128)(2,1)S(1)}, u32[]{:S(2)}, u32[]{:S(2)}) collective-permute-start(bf16[1,3,32,256]{3,2,1,0:T(8,128)(2,1)S(1)} %fusion), channel_id=1, source_target_pairs={{0,6},{1,7},{2,4},{3,5},{4,2},{5,3},{6,0},{7,1},{8,14},{9,15},{10,... | collective-permute-start | bytes 147464 | tf_op jit(solution)/shard_map/ppermute | solution.py:33
  17.3 5.0 collective-permute-start.3
  17.3 5.0 collective-permute-start.2
  22.3 8.5 %collective-permute-start.7 = (bf16[1,4,3,32,256]{4,3,2,1,0:T(8,128)(2,1)S(1)}, bf16[1,4,3,32,256]{4,3,2,1,0:T(8,128)(2,1)S(1)}, u32[]{:S(2)}, u32[]{:S(2)}) collective-permute-start(bf16[1,4,3,32,256]{4,3,2,1,0:T(8,128)(2,1)S(1)} %maximum_bitcast_fusion), channel_id=1, source_target_pairs={{0,24},{8,16},{16,8},{24,0},{1,25},{9,17},{17,9},{25,1},{2,26},{10... | collective-permute-start | bytes 589832 | tf_op jit(solution)/shard_map/ppermute | solution.py:33
  24.8 8.4 %collective-permute-start.6 = (bf16[1,4,3,32,256]{4,3,2,1,0:T(8,128)(2,1)S(1)}, bf16[1,4,3,32,256]{4,3,2,1,0:T(8,128)(2,1)S(1)}, u32[]{:S(2)}, u32[]{:S(2)}) collective-permute-start(bf16[1,4,3,32,256]{4,3,2,1,0:T(8,128)(2,1)S(1)} %maximum_bitcast_fusion), channel_id=1, source_target_pairs={{0,16},{8,24},{16,0},{24,8},{1,17},{9,25},{17,1},{25,9},{2,18},{10... | collective-permute-start | bytes 589832 | tf_op jit(solution)/shard_map/ppermute | solution.py:33
  25.3 8.0 %collective-permute-start.5 = (bf16[1,4,3,32,256]{4,3,2,1,0:T(8,128)(2,1)S(1)}, bf16[1,4,3,32,256]{4,3,2,1,0:T(8,128)(2,1)S(1)}, u32[]{:S(2)}, u32[]{:S(2)}) collective-permute-start(bf16[1,4,3,32,256]{4,3,2,1,0:T(8,128)(2,1)S(1)} %maximum_bitcast_fusion), channel_id=1, source_target_pairs={{0,8},{8,0},{16,24},{24,16},{1,9},{9,1},{17,25},{25,17},{2,10},{10... | collective-permute-start | bytes 589832 | tf_op jit(solution)/shard_map/ppermute | solution.py:33
  33.4 14.1 %collective-permute-start.8 = (bf16[4,4,3,32,256]{4,3,2,1,0:T(8,128)(2,1)S(1)}, bf16[4,4,3,32,256]{4,3,2,1,0:T(8,128)(2,1)S(1)}, u32[]{:S(2)}, u32[]{:S(2)}) collective-permute-start(bf16[4,4,3,32,256]{4,3,2,1,0:T(8,128)(2,1)S(1)} %pad_maximum_fusion.mine), channel_id=1, source_target_pairs={{0,1},{1,0},{2,3},{3,2},{4,5},{5,4},{6,7},{7,6},{8,9},{9,8},{10,11... | collective-permute-start | bytes 2359304 | tf_op jit(solution)/shard_map/ppermute | solution.py:33
  37.2 10.3 %collective-permute-start = (bf16[1,196,1024]{2,1,0:T(8,128)(2,1)}, bf16[1,196,1024]{2,1,0:T(8,128)(2,1)}, u32[]{:S(2)}, u32[]{:S(2)}) collective-permute-start(bf16[1,196,1024]{2,1,0:T(8,128)(2,1)} %get-tuple-element.232), channel_id=1, source_target_pairs={{0,1},{1,2},{2,3},{3,4},{4,5},{5,6},{6,7},{8,9},{9,10},{10,11},{11... | collective-permute-start | bytes 1204232 | tf_op jit(solution)/shard_map/ppermute | solution.py:64
  40.5 7.1 %collective-permute-start.1 = (bf16[1,196,1024]{2,1,0:T(8,128)(2,1)}, bf16[1,196,1024]{2,1,0:T(8,128)(2,1)}, u32[]{:S(2)}, u32[]{:S(2)}) collective-permute-start(bf16[1,196,1024]{2,1,0:T(8,128)(2,1)} %get-tuple-element.231), channel_id=1, source_target_pairs={{1,0},{2,1},{3,2},{4,3},{5,4},{6,5},{7,6},{9,8},{10,9},{11,10},{12... | collective-permute-start | bytes 1204232 | tf_op jit(solution)/shard_map/ppermute | solution.py:65
  55.7 5.5 collective-permute-start.12
  56.6 4.6 collective-permute-start.10
  73.7 5.4 collective-permute-start.19
  89.4 5.4 collective-permute-start.26
  94.5 356.5 %reduce-scatter.2.cloned.1.call-start = ((), (), s32[]{:S(2)}) async-start(), calls=%async_computation.4 | async-start | bytes 2621440 | tf_op jit(solution)/shard_map/reduce_scatter | solution.py:1463
  96.0 8.8 %collective-permute-start.27 = (f32[2,1024]{1,0:T(2,128)S(1)}, f32[2,1024]{1,0:T(2,128)S(1)}, u32[]{:S(2)}, u32[]{:S(2)}) collective-permute-start(f32[2,1024]{1,0:T(2,128)S(1)} %add_add_fusion.5), channel_id=1, source_target_pairs={{0,8},{8,0},{16,24},{24,16},{1,9},{9,1},{17,25},{25,17},{2,10},{10... | collective-permute-start | bytes 24584 | tf_op jit(solution)/shard_map/ppermute | solution.py:33
  97.5 7.3 %collective-permute-start.28 = (f32[2,1024]{1,0:T(2,128)S(1)}, f32[2,1024]{1,0:T(2,128)}, u32[]{:S(2)}, u32[]{:S(2)}) collective-permute-start(f32[2,1024]{1,0:T(2,128)S(1)} %add_add_fusion.5), channel_id=1, source_target_pairs={{0,16},{8,24},{16,0},{24,8},{1,17},{9,25},{17,1},{25,9},{2,18},{10... | collective-permute-start | bytes 24584 | tf_op jit(solution)/shard_map/ppermute | solution.py:33
  98.3 7.2 %collective-permute-start.29 = (f32[2,1024]{1,0:T(2,128)S(1)}, f32[2,1024]{1,0:T(2,128)}, u32[]{:S(2)}, u32[]{:S(2)}) collective-permute-start(f32[2,1024]{1,0:T(2,128)S(1)} %add_add_fusion.5), channel_id=1, source_target_pairs={{0,24},{8,16},{16,8},{24,0},{1,25},{9,17},{17,9},{25,1},{2,26},{10... | collective-permute-start | bytes 24584 | tf_op jit(solution)/shard_map/ppermute | solution.py:33
  117.2 52.5 %collective-permute-start.32 = (bf16[784,1024]{1,0:T(8,128)(2,1)}, bf16[784,1024]{1,0:T(8,128)(2,1)}, u32[]{:S(2)}, u32[]{:S(2)}) collective-permute-start(bf16[784,1024]{1,0:T(8,128)(2,1)} %get-tuple-element.139.one.refs_2_), channel_id=1, source_target_pairs={{0,2},{1,3},{2,0},{3,1},{4,6},{5,7},{6,4},{7,5},{8,10},{9,11},{10,... | collective-permute-start | bytes 4816904 | tf_op jit(solution)/shard_map/ppermute | solution.py:33
  118.3 49.6 %collective-permute-start.31 = (bf16[784,512]{1,0:T(8,128)(2,1)}, bf16[784,512]{1,0:T(8,128)(2,1)}, u32[]{:S(2)}, u32[]{:S(2)}) collective-permute-start(bf16[784,512]{1,0:T(8,128)(2,1)} %get-tuple-element.138.query), channel_id=1, source_target_pairs={{0,4},{1,5},{2,6},{3,7},{4,0},{5,1},{6,2},{7,3},{8,12},{9,13},{10,... | collective-permute-start | bytes 2408456 | tf_op jit(solution)/shard_map/ppermute | solution.py:33
  119.7 52.0 %collective-permute-start.30 = (bf16[784,1024]{1,0:T(8,128)(2,1)}, bf16[784,1024]{1,0:T(8,128)(2,1)}, u32[]{:S(2)}, u32[]{:S(2)}) collective-permute-start(bf16[784,1024]{1,0:T(8,128)(2,1)} %get-tuple-element.139.one.refs_2_), channel_id=1, source_target_pairs={{0,1},{1,0},{2,3},{3,2},{4,5},{5,4},{6,7},{7,6},{8,9},{9,8},{10,11... | collective-permute-start | bytes 4816904 | tf_op jit(solution)/shard_map/ppermute | solution.py:33
  184.1 39.3 %collective-permute-start.34 = (bf16[784,512]{1,0:T(8,128)(2,1)S(1)}, bf16[784,512]{1,0:T(8,128)(2,1)S(1)}, u32[]{:S(2)}, u32[]{:S(2)}) collective-permute-start(bf16[784,512]{1,0:T(8,128)(2,1)S(1)} %get-tuple-element.145), channel_id=1, source_target_pairs={{0,4},{1,5},{2,6},{3,7},{4,0},{5,1},{6,2},{7,3},{8,12},{9,13},{10,... | collective-permute-start | bytes 2408456 | tf_op jit(solution)/shard_map/ppermute | solution.py:33
  185.8 37.6 %collective-permute-start.35 = (f32[8,896]{1,0:T(8,128)S(1)}, f32[8,896]{1,0:T(8,128)S(1)}, u32[]{:S(2)}, u32[]{:S(2)}) collective-permute-start(f32[8,896]{1,0:T(8,128)S(1)} %get-tuple-element.146), channel_id=1, source_target_pairs={{0,4},{1,5},{2,6},{3,7},{4,0},{5,1},{6,2},{7,3},{8,12},{9,13},{10,... | collective-permute-start | bytes 86024 | tf_op jit(solution)/shard_map/ppermute | solution.py:33
  228.8 5.9 %collective-permute-start.39 = (f32[5,1024]{1,0:T(8,128)S(1)}, f32[5,1024]{1,0:T(8,128)S(1)}, u32[]{:S(2)}, u32[]{:S(2)}) collective-permute-start(f32[5,1024]{1,0:T(8,128)S(1)} %add.289), channel_id=1, source_target_pairs={{0,6},{1,7},{2,4},{3,5},{4,2},{5,3},{6,0},{7,1},{8,14},{9,15},{10,... | collective-permute-start | bytes 61448 | tf_op jit(solution)/shard_map/ppermute | solution.py:33
  230.6 5.2 collective-permute-start.38
  235.8 4.9 collective-permute-start.42
  235.9 5.0 collective-permute-start.40
  252.8 36.1 %collective-permute-start.43 = (bf16[784,512]{1,0:T(8,128)(2,1)S(1)}, bf16[784,512]{1,0:T(8,128)(2,1)S(1)}, u32[]{:S(2)}, u32[]{:S(2)}) collective-permute-start(bf16[784,512]{1,0:T(8,128)(2,1)S(1)} %get-tuple-element.153.grad), channel_id=1, source_target_pairs={{0,4},{1,5},{2,6},{3,7},{4,0},{5,1},{6,2},{7,3},{8,12},{9,13},{10,... | collective-permute-start | bytes 2408456 | tf_op jit(solution)/shard_map/ppermute | solution.py:33
  255.2 33.8 %collective-permute-start.44 = (f32[8,896]{1,0:T(8,128)S(1)}, f32[8,896]{1,0:T(8,128)S(1)}, u32[]{:S(2)}, u32[]{:S(2)}) collective-permute-start(f32[8,896]{1,0:T(8,128)S(1)} %get-tuple-element.156), channel_id=1, source_target_pairs={{0,4},{1,5},{2,6},{3,7},{4,0},{5,1},{6,2},{7,3},{8,12},{9,13},{10,... | collective-permute-start | bytes 86024 | tf_op jit(solution)/shard_map/ppermute | solution.py:33
  306.1 54.6 %collective-permute-start.49 = (bf16[784,1024]{1,0:T(8,128)(2,1)}, bf16[784,1024]{1,0:T(8,128)(2,1)S(1)}, u32[]{:S(2)}, u32[]{:S(2)}) collective-permute-start(bf16[784,1024]{1,0:T(8,128)(2,1)} %add_convert_fusion), channel_id=1, source_target_pairs={{0,2},{1,3},{2,0},{3,1},{4,6},{5,7},{6,4},{7,5},{8,10},{9,11},{10,... | collective-permute-start | bytes 4816904 | tf_op jit(solution)/shard_map/ppermute | solution.py:33
  319.0 39.4 %collective-permute-start.46 = (bf16[784,512]{1,0:T(8,128)(2,1)S(1)}, bf16[784,512]{1,0:T(8,128)(2,1)S(1)}, u32[]{:S(2)}, u32[]{:S(2)}) collective-permute-start(bf16[784,512]{1,0:T(8,128)(2,1)S(1)} %get-tuple-element.165), channel_id=1, source_target_pairs={{0,4},{1,5},{2,6},{3,7},{4,0},{5,1},{6,2},{7,3},{8,12},{9,13},{10,... | collective-permute-start | bytes 2408456 | tf_op jit(solution)/shard_map/ppermute | solution.py:33
  321.2 37.2 %collective-permute-start.47 = (bf16[784,512]{1,0:T(8,128)(2,1)S(1)}, bf16[784,512]{1,0:T(8,128)(2,1)S(1)}, u32[]{:S(2)}, u32[]{:S(2)}) collective-permute-start(bf16[784,512]{1,0:T(8,128)(2,1)S(1)} %get-tuple-element.167), channel_id=1, source_target_pairs={{0,1},{1,0},{2,3},{3,2},{4,5},{5,4},{6,7},{7,6},{8,9},{9,8},{10,11... | collective-permute-start | bytes 2408456 | tf_op jit(solution)/shard_map/ppermute | solution.py:33
  321.2 37.2 %collective-permute-start.48 = (bf16[784,512]{1,0:T(8,128)(2,1)S(1)}, bf16[784,512]{1,0:T(8,128)(2,1)S(1)}, u32[]{:S(2)}, u32[]{:S(2)}) collective-permute-start(bf16[784,512]{1,0:T(8,128)(2,1)S(1)} %get-tuple-element.168), channel_id=1, source_target_pairs={{0,1},{1,0},{2,3},{3,2},{4,5},{5,4},{6,7},{7,6},{8,9},{9,8},{10,11... | collective-permute-start | bytes 2408456 | tf_op jit(solution)/shard_map/ppermute | solution.py:33
  368.6 5.6 collective-permute-start.53
  370.7 4.6 collective-permute-start.52
  375.4 9.3 %collective-permute-start.54 = (f32[3,1024]{1,0:T(4,128)S(1)}, f32[3,1024]{1,0:T(4,128)S(1)}, u32[]{:S(2)}, u32[]{:S(2)}) collective-permute-start(f32[3,1024]{1,0:T(4,128)S(1)} %add_add_fusion.3), channel_id=1, source_target_pairs={{0,8},{8,0},{16,24},{24,16},{1,9},{9,1},{17,25},{25,17},{2,10},{10... | collective-permute-start | bytes 36872 | tf_op jit(solution)/shard_map/ppermute | solution.py:33
  375.9 8.7 %collective-permute-start.55 = (f32[3,1024]{1,0:T(4,128)S(1)}, f32[3,1024]{1,0:T(4,128)S(1)}, u32[]{:S(2)}, u32[]{:S(2)}) collective-permute-start(f32[3,1024]{1,0:T(4,128)S(1)} %add_add_fusion.3), channel_id=1, source_target_pairs={{0,16},{8,24},{16,0},{24,8},{1,17},{9,25},{17,1},{25,9},{2,18},{10... | collective-permute-start | bytes 36872 | tf_op jit(solution)/shard_map/ppermute | solution.py:33
  376.2 8.4 %collective-permute-start.56 = (f32[3,1024]{1,0:T(4,128)S(1)}, f32[3,1024]{1,0:T(4,128)S(1)}, u32[]{:S(2)}, u32[]{:S(2)}) collective-permute-start(f32[3,1024]{1,0:T(4,128)S(1)} %add_add_fusion.3), channel_id=1, source_target_pairs={{0,24},{8,16},{16,8},{24,0},{1,25},{9,17},{17,9},{25,1},{2,26},{10... | collective-permute-start | bytes 36872 | tf_op jit(solution)/shard_map/ppermute | solution.py:33
  384.7 27.3 %collective-permute-start.57 = (bf16[4096,256]{1,0:T(8,128)(2,1)S(1)}, bf16[4096,256]{1,0:T(8,128)(2,1)S(1)}, u32[]{:S(2)}, u32[]{:S(2)}) collective-permute-start(bf16[4096,256]{1,0:T(8,128)(2,1)S(1)} %get-tuple-element.177), channel_id=1, source_target_pairs={{0,1},{1,0},{2,3},{3,2},{4,5},{5,4},{6,7},{7,6},{8,9},{9,8},{10,11... | collective-permute-start | bytes 6291464 | tf_op jit(solution)/shard_map/ppermute | solution.py:33
  389.1 5.4 collective-permute-start.61
  407.6 6.3 %collective-permute-start.68 = (f32[2,256]{1,0:T(2,128)S(1)}, f32[2,256]{1,0:T(2,128)S(1)}, u32[]{:S(2)}, u32[]{:S(2)}) collective-permute-start(f32[2,256]{1,0:T(2,128)S(1)} %add.311), channel_id=1, source_target_pairs={{0,6},{1,7},{2,4},{3,5},{4,2},{5,3},{6,0},{7,1},{8,14},{9,15},{10,... | collective-permute-start | bytes 6152 | tf_op jit(solution)/shard_map/ppermute | solution.py:33
  413.8 78.6 %all-reduce.2.cloned.1.call-start = ((), (), s32[]{:S(2)}) async-start(), calls=%async_computation.5 | async-start | bytes 1048576 | tf_op jit(solution)/shard_map/psum | solution.py:1464
  414.1 6.7 %collective-permute-start.71 = (f32[2,256]{1,0:T(2,128)S(1)}, f32[2,256]{1,0:T(2,128)S(1)}, u32[]{:S(2)}, u32[]{:S(2)}) collective-permute-start(f32[2,256]{1,0:T(2,128)S(1)} %add_add_fusion.7), channel_id=1, source_target_pairs={{0,24},{8,16},{16,8},{24,0},{1,25},{9,17},{17,9},{25,1},{2,26},{10... | collective-permute-start | bytes 6152 | tf_op jit(solution)/shard_map/ppermute | solution.py:33
  415.3 5.5 collective-permute-start.69
  422.2 5.9 %collective-permute-start.72 = (bf16[1,196,256]{2,1,0:T(8,128)(2,1)S(1)}, bf16[1,196,256]{2,1,0:T(8,128)(2,1)S(1)}, u32[]{:S(2)}, u32[]{:S(2)}) collective-permute-start(bf16[1,196,256]{2,1,0:T(8,128)(2,1)S(1)} %get-tuple-element.237), channel_id=1, source_target_pairs={{0,1},{1,2},{2,3},{3,4},{4,5},{5,6},{6,7},{8,9},{9,10},{10,11},{11... | collective-permute-start | bytes 301064 | tf_op jit(solution)/shard_map/ppermute | solution.py:64
  423.5 5.5 collective-permute-start.73
  435.2 6.8 %collective-permute-start.74 = (bf16[3200,256]{1,0:T(8,128)(2,1)}, bf16[3200,256]{1,0:T(8,128)(2,1)S(1)}, u32[]{:S(2)}, u32[]{:S(2)}) collective-permute-start(bf16[3200,256]{1,0:T(8,128)(2,1)} %get-tuple-element.189), channel_id=1, source_target_pairs={{0,1},{1,0},{2,3},{3,2},{4,5},{5,4},{6,7},{7,6},{8,9},{9,8},{10,11... | collective-permute-start | bytes 4915208 | tf_op jit(solution)/shard_map/ppermute | solution.py:33
  447.5 13.6 %collective-permute-start.77 = (bf16[800,256]{1,0:T(8,128)(2,1)}, bf16[800,256]{1,0:T(8,128)(2,1)}, u32[]{:S(2)}, u32[]{:S(2)}) collective-permute-start(bf16[800,256]{1,0:T(8,128)(2,1)} %get-tuple-element.229), channel_id=1, source_target_pairs={{0,24},{8,16},{16,8},{24,0},{1,25},{9,17},{17,9},{25,1},{2,26},{10... | collective-permute-start | bytes 1228808 | tf_op jit(solution)/shard_map/ppermute | solution.py:33
  448.8 20.4 %collective-permute-start.76 = (bf16[800,256]{1,0:T(8,128)(2,1)}, bf16[800,256]{1,0:T(8,128)(2,1)}, u32[]{:S(2)}, u32[]{:S(2)}) collective-permute-start(bf16[800,256]{1,0:T(8,128)(2,1)} %get-tuple-element.230), channel_id=1, source_target_pairs={{0,16},{8,24},{16,0},{24,8},{1,17},{9,25},{17,1},{25,9},{2,18},{10... | collective-permute-start | bytes 1228808 | tf_op jit(solution)/shard_map/ppermute | solution.py:33
  449.1 20.2 %collective-permute-start.75 = (bf16[800,256]{1,0:T(8,128)(2,1)}, bf16[800,256]{1,0:T(8,128)(2,1)}, u32[]{:S(2)}, u32[]{:S(2)}) collective-permute-start(bf16[800,256]{1,0:T(8,128)(2,1)} %get-tuple-element.228), channel_id=1, source_target_pairs={{0,8},{8,0},{16,24},{24,16},{1,9},{9,1},{17,25},{25,17},{2,10},{10... | collective-permute-start | bytes 1228808 | tf_op jit(solution)/shard_map/ppermute | solution.py:33
  451.0 86.9 %all-gather.11.cloned.1.call-start = ((), (), s32[]{:S(2)}) async-start(), calls=%async_computation.6 | async-start | bytes 2621440 | tf_op jit(solution)/shard_map/all_gather | solution.py:1468
  471.5 7.7 %collective-permute-start.80 = (bf16[200,256]{1,0:T(8,128)(2,1)S(1)}, bf16[200,256]{1,0:T(8,128)(2,1)S(1)}, u32[]{:S(2)}, u32[]{:S(2)}) collective-permute-start(bf16[200,256]{1,0:T(8,128)(2,1)S(1)} %get-tuple-element.234), channel_id=1, source_target_pairs={{0,6},{1,7},{2,4},{3,5},{4,2},{5,3},{6,0},{7,1},{8,14},{9,15},{10,... | collective-permute-start | bytes 307208 | tf_op jit(solution)/shard_map/ppermute | solution.py:33
  472.3 19.1 %collective-permute-start.79 = (bf16[200,256]{1,0:T(8,128)(2,1)S(1)}, bf16[200,256]{1,0:T(8,128)(2,1)S(1)}, u32[]{:S(2)}, u32[]{:S(2)}) collective-permute-start(bf16[200,256]{1,0:T(8,128)(2,1)S(1)} %get-tuple-element.235), channel_id=1, source_target_pairs={{0,4},{1,5},{2,6},{3,7},{4,0},{5,1},{6,2},{7,3},{8,12},{9,13},{10,... | collective-permute-start | bytes 307208 | tf_op jit(solution)/shard_map/ppermute | solution.py:33
  474.0 17.4 %collective-permute-start.78 = (bf16[200,256]{1,0:T(8,128)(2,1)S(1)}, bf16[200,256]{1,0:T(8,128)(2,1)S(1)}, u32[]{:S(2)}, u32[]{:S(2)}) collective-permute-start(bf16[200,256]{1,0:T(8,128)(2,1)S(1)} %get-tuple-element.233), channel_id=1, source_target_pairs={{0,2},{1,3},{2,0},{3,1},{4,6},{5,7},{6,4},{7,5},{8,10},{9,11},{10,... | collective-permute-start | bytes 307208 | tf_op jit(solution)/shard_map/ppermute | solution.py:33
  492.5 5.9 %collective-permute-start.81 = (bf16[200,256]{1,0:T(8,128)(2,1)S(1)}, bf16[200,256]{1,0:T(8,128)(2,1)S(1)}, u32[]{:S(2)}, u32[]{:S(2)}) collective-permute-start(bf16[200,256]{1,0:T(8,128)(2,1)S(1)} %add_convert_fusion.2), channel_id=1, source_target_pairs={{0,2},{1,3},{2,0},{3,1},{4,6},{5,7},{6,4},{7,5},{8,10},{9,11},{10,... | collective-permute-start | bytes 307208 | tf_op jit(solution)/shard_map/ppermute | solution.py:33
  493.4 10.3 %collective-permute-start.82 = (bf16[200,256]{1,0:T(8,128)(2,1)S(1)}, bf16[200,256]{1,0:T(8,128)(2,1)S(1)}, u32[]{:S(2)}, u32[]{:S(2)}) collective-permute-start(bf16[200,256]{1,0:T(8,128)(2,1)S(1)} %add_convert_fusion.2), channel_id=1, source_target_pairs={{0,4},{1,5},{2,6},{3,7},{4,0},{5,1},{6,2},{7,3},{8,12},{9,13},{10,... | collective-permute-start | bytes 307208 | tf_op jit(solution)/shard_map/ppermute | solution.py:33
  494.2 10.2 %collective-permute-start.83 = (bf16[200,256]{1,0:T(8,128)(2,1)S(1)}, bf16[200,256]{1,0:T(8,128)(2,1)S(1)}, u32[]{:S(2)}, u32[]{:S(2)}) collective-permute-start(bf16[200,256]{1,0:T(8,128)(2,1)S(1)} %add_convert_fusion.2), channel_id=1, source_target_pairs={{0,6},{1,7},{2,4},{3,5},{4,2},{5,3},{6,0},{7,1},{8,14},{9,15},{10,... | collective-permute-start | bytes 307208 | tf_op jit(solution)/shard_map/ppermute | solution.py:33
  505.0 14.3 %collective-permute-start.84 = (bf16[800,256]{1,0:T(8,128)(2,1)}, bf16[800,256]{1,0:T(8,128)(2,1)}, u32[]{:S(2)}, u32[]{:S(2)}) collective-permute-start(bf16[800,256]{1,0:T(8,128)(2,1)} %bitcast.30), channel_id=1, source_target_pairs={{0,8},{8,0},{16,24},{24,16},{1,9},{9,1},{17,25},{25,17},{2,10},{10... | collective-permute-start | bytes 1228808 | tf_op jit(solution)/shard_map/ppermute | solution.py:33
  508.1 12.3 %collective-permute-start.85 = (bf16[800,256]{1,0:T(8,128)(2,1)}, bf16[800,256]{1,0:T(8,128)(2,1)}, u32[]{:S(2)}, u32[]{:S(2)}) collective-permute-start(bf16[800,256]{1,0:T(8,128)(2,1)} %bitcast.30), channel_id=1, source_target_pairs={{0,16},{8,24},{16,0},{24,8},{1,17},{9,25},{17,1},{25,9},{2,18},{10... | collective-permute-start | bytes 1228808 | tf_op jit(solution)/shard_map/ppermute | solution.py:33
  516.8 18.3 %collective-permute-start.86 = (bf16[800,256]{1,0:T(8,128)(2,1)}, bf16[800,256]{1,0:T(8,128)(2,1)S(1)}, u32[]{:S(2)}, u32[]{:S(2)}) collective-permute-start(bf16[800,256]{1,0:T(8,128)(2,1)} %bitcast.30), channel_id=1, source_target_pairs={{0,24},{8,16},{16,8},{24,0},{1,25},{9,17},{17,9},{25,1},{2,26},{10... | collective-permute-start | bytes 1228808 | tf_op jit(solution)/shard_map/ppermute | solution.py:33
  537.9 6.0 %collective-permute-start.88 = (bf16[4096,256]{1,0:T(8,128)(2,1)}, bf16[4096,256]{1,0:T(8,128)(2,1)}, u32[]{:S(2)}, u32[]{:S(2)}) collective-permute-start(bf16[4096,256]{1,0:T(8,128)(2,1)} %all-gather.11.cloned.1.call-done.half), channel_id=1, source_target_pairs={{0,1},{1,0},{2,3},{3,2},{4,5},{5,4},{6,7},{7,6},{8,9},{9,8},{10,11... | collective-permute-start | bytes 6291464 | tf_op jit(solution)/shard_map/ppermute | solution.py:33
  538.0 14.0 %collective-permute-start.87 = (bf16[3200,256]{1,0:T(8,128)(2,1)S(1)}, bf16[3200,256]{1,0:T(8,128)(2,1)S(1)}, u32[]{:S(2)}, u32[]{:S(2)}) collective-permute-start(bf16[3200,256]{1,0:T(8,128)(2,1)S(1)} %bitcast.74), channel_id=1, source_target_pairs={{0,1},{1,0},{2,3},{3,2},{4,5},{5,4},{6,7},{7,6},{8,9},{9,8},{10,11... | collective-permute-start | bytes 4915208 | tf_op jit(solution)/shard_map/ppermute | solution.py:33
  (123 other events, 1628.8 us)
Sparse Core Ops, SparseCore 0:
  11.0 28.5 all-gather.4
  41.8 38.2 all-gather.6
  94.6 19.9 all-gather.8
  413.9 33.6 reduce-scatter.1
  451.2 41.0 all-reduce.1
  494.1 43.8 all-gather.10
